TPU v7x, 32 devices: a whole 2x2x4 slice. The times are simulated.
32 devices in a mesh: dp: 16 (over z, y, x), tower: 2 (over core).
Axes of the slice: x: 2, y: 2, z: 4, core: 2. Of those that a mesh axis runs over, the one named last changes fastest.
Arguments:
- query_tokens: bfloat16 [32, 64, 768], P('dp'), may hold values from -8 to 8
- passage_tokens: bfloat16 [32, 512, 768], P('dp'), may hold values from -8 to 8
- lengths: int32 [2, 32], P('tower', 'dp'), may hold values from 1 to 512, as said below
- positives: int32 [32], replicated, may hold values from 0 to 31, each once
- query_weight: bfloat16 [768, 768], P('dp'), may hold values from -0.21875 to 0.21875
- key_weight: bfloat16 [768, 768], P('dp'), may hold values from -0.21875 to 0.21875
- value_weight: bfloat16 [768, 768], P('dp'), may hold values from -0.21875 to 0.21875
- output_weight: bfloat16 [768, 768], P('dp'), may hold values from -0.4375 to 0.4375
- inner_weight: bfloat16 [768, 3072], P('dp'), may hold values from -0.21875 to 0.21875
- outer_weight: bfloat16 [3072, 768], P('dp'), may hold values from -0.109375 to 0.109375
- query_bias: bfloat16 [768], P('dp'), may hold values from -1.75 to 1.75
- value_bias: bfloat16 [768], P('dp'), may hold values from -1.75 to 1.75
- output_bias: bfloat16 [768], P('dp'), may hold values from -0.625 to 0.625
- inner_bias: bfloat16 [3072], P('dp'), may hold values from -1.75 to 1.75
- outer_bias: bfloat16 [768], P('dp'), may hold values from -0.625 to 0.625
- first_gain: bfloat16 [768], P('dp'), may hold values from 0.5 to 1.5
- first_shift: bfloat16 [768], P('dp'), may hold values from -0.625 to 0.625
- second_gain: bfloat16 [768], P('dp'), may hold values from 0.5 to 1.5
- second_shift: bfloat16 [768], P('dp'), may hold values from -0.625 to 0.625
Outputs:
- loss_value: float32 [], replicated
- query_grads: float32 [32, 64, 768], P('dp')
- passage_grads: float32 [32, 512, 768], P('dp')
- grad_query: float32 [768, 768], P('dp')
- grad_key: float32 [768, 768], P('dp')
- grad_value: float32 [768, 768], P('dp')
- grad_output: float32 [768, 768], P('dp')
- grad_inner: float32 [768, 3072], P('dp')
- grad_outer: float32 [3072, 768], P('dp')
- grad_qbias: float32 [768], P('dp')
- grad_vbias: float32 [768], P('dp')
- grad_obias: float32 [768], P('dp')
- grad_inbias: float32 [3072], P('dp')
- grad_outbias: float32 [768], P('dp')
- grad_gainone: float32 [768], P('dp')
- grad_shiftone: float32 [768], P('dp')
- grad_gaintwo: float32 [768], P('dp')
- grad_shifttwo: float32 [768], P('dp')
Inputs may be any that keep to these rules, and one draw needn't show every extreme that they name: Query lengths (row 0) are at most 64, and some query has exactly 64; some passage has exactly 512. `positives`: each passage is the positive of exactly one query.
All inputs are finite; a program needn't handle non-finite values.
Results may differ from a plain program's by a relative error of at most 0.014.
Values may be sent and summed in bfloat16 or wider, within the bound.
A program may use at most 256 MiB of HBM per device.

v0:
```python
import jax
import jax.numpy as jnp
from jax import lax
from jax.sharding import PartitionSpec as P

HEADS = 12
HDIM = 64
MB = 2


contrast_scale_divisor = 0.01
highest = lax.Precision.HIGHEST


def swapped(shard, axis, apart):
    return lax.ppermute(shard, axis, [(i, i ^ 1 << apart) for i in range(lax.axis_size(axis))])


def linear_product(left, right):
    return jnp.dot(left, right, preferred_element_type=jnp.float32)


def left_t(left, right):
    return lax.dot_general(
        left, right, (((0,), (0,)), ((), ())), preferred_element_type=jnp.float32
    )


def right_t(left, right):
    return lax.dot_general(
        left, right, (((1,), (1,)), ((), ())), preferred_element_type=jnp.float32
    )


def layer_norm(hidden, gain, shift):
    center = hidden - jnp.mean(hidden, axis=-1, keepdims=True)
    spread = jnp.mean(center * center, axis=-1, keepdims=True)
    return center * lax.rsqrt(spread + 1e-12) * gain + shift


def exact_gelu(values):
    return jax.nn.gelu(values, approximate=False)


def normalize(pooled):
    return pooled / jnp.sqrt(jnp.sum(pooled * pooled, axis=-1, keepdims=True) + 1e-06)


def contrast(query_rows, passage_rows, targets):
    pair_score_table = (
        jnp.dot(query_rows, passage_rows.T, precision=highest, preferred_element_type=jnp.float32)
        / contrast_scale_divisor
    )
    onehot = targets[:, None] == jnp.arange(passage_rows.shape[0], dtype=jnp.int32)[None, :]
    picked = jnp.sum(jnp.where(onehot, pair_score_table, 0.0), axis=-1)
    return jnp.sum(jax.nn.logsumexp(pair_score_table, axis=-1) - picked)


def forward(token_row, length, gathered):
    (
        query_w,
        key_w,
        value_w,
        output_w,
        inner_w,
        outer_w,
        query_b,
        value_b,
        output_b,
        inner_b,
        outer_b,
        gain_one,
        shift_one,
        second_norm_gain,
        shift_two,
    ) = gathered
    seq_len = token_row.shape[0]
    head_scale = HDIM ** (-0.5)
    queries = (linear_product(token_row, query_w) + query_b.astype(jnp.float32)).astype(
        jnp.bfloat16
    )
    lookup_sequence_states = linear_product(token_row, key_w).astype(jnp.bfloat16)
    values_seq = (linear_product(token_row, value_w) + value_b.astype(jnp.float32)).astype(
        jnp.bfloat16
    )
    query_heads = queries.reshape(seq_len, HEADS, HDIM)
    key_heads = lookup_sequence_states.reshape(seq_len, HEADS, HDIM)
    value_heads = values_seq.reshape(seq_len, HEADS, HDIM)
    scores = (
        jnp.einsum("qhd,khd->hqk", query_heads, key_heads, preferred_element_type=jnp.float32)
        * head_scale
    )
    key_valid = jnp.arange(seq_len) < length
    scores = jnp.where(key_valid[None, None, :], scores, -1000000000.0)
    probs_all = jax.nn.softmax(scores, axis=-1)
    probs_low = probs_all.astype(jnp.bfloat16)
    context = jnp.einsum("hqk,khd->qhd", probs_low, value_heads, preferred_element_type=jnp.float32)
    context = context.astype(jnp.bfloat16).reshape(seq_len, HEADS * HDIM)
    first_in = token_row.astype(jnp.float32) + (
        linear_product(context, output_w) + output_b.astype(jnp.float32)
    )
    normed = layer_norm(first_in, gain_one.astype(jnp.float32), shift_one.astype(jnp.float32))
    normed_low = normed.astype(jnp.bfloat16)
    inner_pre = linear_product(normed_low, inner_w) + inner_b.astype(jnp.float32)
    activation = exact_gelu(inner_pre).astype(jnp.bfloat16)
    second_in = normed + (linear_product(activation, outer_w) + outer_b.astype(jnp.float32))
    output_rows = layer_norm(
        second_in, second_norm_gain.astype(jnp.float32), shift_two.astype(jnp.float32)
    )
    row_mask = key_valid.astype(jnp.float32)
    pooled = jnp.sum(output_rows * row_mask[:, None], axis=0) / length.astype(jnp.float32)
    return {
        "query_heads": query_heads,
        "key_heads": key_heads,
        "value_heads": value_heads,
        "probs_all": probs_all,
        "probs_low": probs_low,
        "context": context,
        "first_in": first_in,
        "normed_low": normed_low,
        "inner_pre": inner_pre,
        "activation": activation,
        "second_in": second_in,
        "row_mask": row_mask,
        "pooled": pooled,
    }


def backward(token_row, length, pooled_grad, gathered):
    (
        query_w,
        key_w,
        value_w,
        output_w,
        inner_w,
        outer_w,
        query_b,
        value_b,
        output_b,
        inner_b,
        outer_b,
        gain_one,
        shift_one,
        second_norm_gain,
        shift_two,
    ) = gathered
    kept = forward(token_row, length, gathered)
    seq_len = token_row.shape[0]
    head_scale = HDIM ** (-0.5)
    d_rows = kept["row_mask"][:, None] * (pooled_grad / length.astype(jnp.float32))[None, :]
    _, second_back = jax.vjp(
        layer_norm,
        kept["second_in"],
        second_norm_gain.astype(jnp.float32),
        shift_two.astype(jnp.float32),
    )
    d_second, d_gain_two, d_shift_two = second_back(d_rows)
    d_outer = d_second.astype(jnp.bfloat16)
    g_outer_w = left_t(kept["activation"], d_outer)
    g_outer_b = jnp.sum(d_outer.astype(jnp.float32), axis=0)
    d_activation = right_t(d_outer, outer_w)
    _, gelu_back = jax.vjp(exact_gelu, kept["inner_pre"])
    d_inner = gelu_back(d_activation)[0].astype(jnp.bfloat16)
    g_inner_w = left_t(kept["normed_low"], d_inner)
    g_inner_b = jnp.sum(d_inner.astype(jnp.float32), axis=0)
    d_normed = d_second + right_t(d_inner, inner_w)
    _, first_back = jax.vjp(
        layer_norm, kept["first_in"], gain_one.astype(jnp.float32), shift_one.astype(jnp.float32)
    )
    d_first, d_gain_one, d_shift_one = first_back(d_normed)
    d_attended = d_first.astype(jnp.bfloat16)
    g_output_w = left_t(kept["context"], d_attended)
    g_output_b = jnp.sum(d_attended.astype(jnp.float32), axis=0)
    d_context = right_t(d_attended, output_w).astype(jnp.bfloat16).reshape(seq_len, HEADS, HDIM)
    d_values = jnp.einsum(
        "hqk,qhd->khd", kept["probs_low"], d_context, preferred_element_type=jnp.float32
    )
    d_values = d_values.astype(jnp.bfloat16).reshape(seq_len, HEADS * HDIM)
    d_probs = jnp.einsum(
        "qhd,khd->hqk", d_context, kept["value_heads"], preferred_element_type=jnp.float32
    )
    probs_all = kept["probs_all"]
    d_scores = probs_all * (d_probs - jnp.sum(probs_all * d_probs, axis=-1, keepdims=True))
    d_scores = d_scores.astype(jnp.bfloat16)
    d_queries = (
        jnp.einsum("hqk,khd->qhd", d_scores, kept["key_heads"], preferred_element_type=jnp.float32)
        * head_scale
    )
    d_queries = d_queries.astype(jnp.bfloat16).reshape(seq_len, HEADS * HDIM)
    d_keys = (
        jnp.einsum(
            "hqk,qhd->khd", d_scores, kept["query_heads"], preferred_element_type=jnp.float32
        )
        * head_scale
    )
    d_keys = d_keys.astype(jnp.bfloat16).reshape(seq_len, HEADS * HDIM)
    g_query_w = left_t(token_row, d_queries)
    g_key_w = left_t(token_row, d_keys)
    g_value_w = left_t(token_row, d_values)
    g_query_b = jnp.sum(d_queries.astype(jnp.float32), axis=0)
    g_value_b = jnp.sum(d_values.astype(jnp.float32), axis=0)
    d_token = (
        d_first + right_t(d_queries, query_w) + right_t(d_keys, key_w) + right_t(d_values, value_w)
    )
    return (
        d_token,
        (
            g_query_w,
            g_key_w,
            g_value_w,
            g_output_w,
            g_inner_w,
            g_outer_w,
            g_query_b,
            g_value_b,
            g_output_b,
            g_inner_b,
            g_outer_b,
            d_gain_one,
            d_shift_one,
            d_gain_two,
            d_shift_two,
        ),
    )


def fetch(shards):
    return (
        lax.all_gather(shards[0], "dp", axis=0, tiled=True),
        lax.all_gather(shards[1], "dp", axis=0, tiled=True),
        lax.all_gather(shards[2], "dp", axis=0, tiled=True),
        lax.all_gather(shards[3], "dp", axis=0, tiled=True),
        lax.all_gather(shards[4], "dp", axis=0, tiled=True),
        lax.all_gather(shards[5], "dp", axis=0, tiled=True),
        lax.all_gather(shards[6], "dp", axis=0, tiled=True),
        lax.all_gather(shards[7], "dp", axis=0, tiled=True),
        lax.all_gather(shards[8], "dp", axis=0, tiled=True),
        lax.all_gather(shards[9], "dp", axis=0, tiled=True),
        lax.all_gather(shards[10], "dp", axis=0, tiled=True),
        lax.all_gather(shards[11], "dp", axis=0, tiled=True),
        lax.all_gather(shards[12], "dp", axis=0, tiled=True),
        lax.all_gather(shards[13], "dp", axis=0, tiled=True),
        lax.all_gather(shards[14], "dp", axis=0, tiled=True),
    )


def reduce_grads(grads):
    pieces = (
        lax.psum_scatter(grads[0], "dp", scatter_dimension=0, tiled=True),
        lax.psum_scatter(grads[1], "dp", scatter_dimension=0, tiled=True),
        lax.psum_scatter(grads[2], "dp", scatter_dimension=0, tiled=True),
        lax.psum_scatter(grads[3], "dp", scatter_dimension=0, tiled=True),
        lax.psum_scatter(grads[4], "dp", scatter_dimension=0, tiled=True),
        lax.psum_scatter(grads[5], "dp", scatter_dimension=0, tiled=True),
        lax.psum_scatter(grads[6], "dp", scatter_dimension=0, tiled=True),
        lax.psum_scatter(grads[7], "dp", scatter_dimension=0, tiled=True),
        lax.psum_scatter(grads[8], "dp", scatter_dimension=0, tiled=True),
        lax.psum_scatter(grads[9], "dp", scatter_dimension=0, tiled=True),
        lax.psum_scatter(grads[10], "dp", scatter_dimension=0, tiled=True),
        lax.psum_scatter(grads[11], "dp", scatter_dimension=0, tiled=True),
        lax.psum_scatter(grads[12], "dp", scatter_dimension=0, tiled=True),
        lax.psum_scatter(grads[13], "dp", scatter_dimension=0, tiled=True),
        lax.psum_scatter(grads[14], "dp", scatter_dimension=0, tiled=True),
    )
    return (
        lax.psum(pieces[0].astype(jnp.bfloat16), "tower").astype(jnp.float32),
        lax.psum(pieces[1].astype(jnp.bfloat16), "tower").astype(jnp.float32),
        lax.psum(pieces[2].astype(jnp.bfloat16), "tower").astype(jnp.float32),
        lax.psum(pieces[3].astype(jnp.bfloat16), "tower").astype(jnp.float32),
        lax.psum(pieces[4].astype(jnp.bfloat16), "tower").astype(jnp.float32),
        lax.psum(pieces[5].astype(jnp.bfloat16), "tower").astype(jnp.float32),
        lax.psum(pieces[6].astype(jnp.bfloat16), "tower").astype(jnp.float32),
        lax.psum(pieces[7].astype(jnp.bfloat16), "tower").astype(jnp.float32),
        lax.psum(pieces[8].astype(jnp.bfloat16), "tower").astype(jnp.float32),
        lax.psum(pieces[9].astype(jnp.bfloat16), "tower").astype(jnp.float32),
        lax.psum(pieces[10].astype(jnp.bfloat16), "tower").astype(jnp.float32),
        lax.psum(pieces[11].astype(jnp.bfloat16), "tower").astype(jnp.float32),
        lax.psum(pieces[12].astype(jnp.bfloat16), "tower").astype(jnp.float32),
        lax.psum(pieces[13].astype(jnp.bfloat16), "tower").astype(jnp.float32),
        lax.psum(pieces[14].astype(jnp.bfloat16), "tower").astype(jnp.float32),
    )


def pooled_block(token_rows, row_lengths, gathered):

    def pooled_one_row(record):
        return forward(record[0], record[1], gathered)["pooled"]

    return lax.map(pooled_one_row, (token_rows, row_lengths))


def backward_block(token_rows, row_lengths, pooled_grads, gathered):
    zeros_init = jax.tree.map(lambda tensor: jnp.zeros(tensor.shape, jnp.float32), gathered)

    def backward_one_row(carry, record):
        d_token, param_grads = backward(record[0], record[1], record[2], gathered)
        return (jax.tree.map(jnp.add, carry, param_grads), d_token)

    return lax.scan(backward_one_row, zeros_init, (token_rows, row_lengths, pooled_grads))


def per_device(
    query_tokens,
    passage_tokens,
    lengths,
    positives,
    query_weight,
    key_weight,
    value_weight,
    output_weight,
    inner_weight,
    outer_weight,
    query_bias,
    value_bias,
    output_bias,
    inner_bias,
    outer_bias,
    first_gain,
    first_shift,
    second_gain,
    second_shift,
):
    shards = (
        query_weight,
        key_weight,
        value_weight,
        output_weight,
        inner_weight,
        outer_weight,
        query_bias,
        value_bias,
        output_bias,
        inner_bias,
        outer_bias,
        first_gain,
        first_shift,
        second_gain,
        second_shift,
    )
    tower_id = lax.axis_index("tower")
    dp_id = lax.axis_index("dp")
    row_lengths = lengths[0]
    seq_count = passage_tokens.shape[0]
    per_micro = seq_count // MB
    seq_len = passage_tokens.shape[1]
    is_query = tower_id == 0
    pooled_parts = []
    for micro_idx in range(MB):
        gathered = fetch(shards)
        lower = micro_idx * per_micro
        micro_lengths = row_lengths[lower : lower + per_micro]
        query_micro = query_tokens[lower : lower + per_micro]
        passage_micro = passage_tokens[lower : lower + per_micro]
        pooled_parts.append(
            lax.cond(
                is_query,
                lambda: pooled_block(query_micro, micro_lengths, gathered),
                lambda: pooled_block(passage_micro, micro_lengths, gathered),
            )
        )
    pooled = jnp.concatenate(pooled_parts, axis=0)
    unit, unit_back = jax.vjp(normalize, pooled)
    partner_rows = swapped(unit, "tower", 0)
    query_side = jnp.where(is_query, unit, partner_rows)
    passage_side = jnp.where(is_query, partner_rows, unit)
    embedded = lax.all_gather(jnp.stack([query_side, passage_side]), "dp", axis=1, tiled=True)
    all_queries = embedded[0]
    all_passages = embedded[1]
    pair_count = all_queries.shape[0]
    row_start = dp_id * seq_count
    incoming_adjoint = jnp.float32(seq_len)
    query_block = lax.dynamic_slice_in_dim(all_queries, row_start, seq_count, 0)
    target_block = lax.dynamic_slice_in_dim(positives, row_start, seq_count, 0)

    def block_loss(query_rows, passage_rows):
        return contrast(query_rows, passage_rows, target_block)

    partial_loss, loss_back = jax.vjp(block_loss, query_block, all_passages)
    loss_value = lax.psum(partial_loss, "dp") / pair_count
    d_query_block, d_passage_all = loss_back(incoming_adjoint)
    d_passage_mine = lax.psum_scatter(d_passage_all, "dp", scatter_dimension=0, tiled=True)
    d_unit = jnp.where(is_query, d_query_block, d_passage_mine)
    pooled_gradient = unit_back(d_unit)[0]
    query_parts = []
    passage_parts = []
    reduced = None
    for micro_idx in range(MB):
        gathered = fetch(shards)
        lower = micro_idx * per_micro
        micro_lengths = row_lengths[lower : lower + per_micro]
        micro_pooled = pooled_gradient[lower : lower + per_micro]
        query_micro = query_tokens[lower : lower + per_micro]
        passage_micro = passage_tokens[lower : lower + per_micro]

        def query_pass():
            grads_here, d_rows_here = backward_block(
                query_micro, micro_lengths, micro_pooled, gathered
            )
            return (grads_here, d_rows_here, jnp.zeros(passage_micro.shape, jnp.float32))

        def passage_pass():
            grads_here, d_rows_here = backward_block(
                passage_micro, micro_lengths, micro_pooled, gathered
            )
            return (grads_here, jnp.zeros(query_micro.shape, jnp.float32), d_rows_here)

        micro_grads, d_query_rows, d_passage_rows = lax.cond(is_query, query_pass, passage_pass)
        query_parts.append(d_query_rows)
        passage_parts.append(d_passage_rows)
        shared = reduce_grads(micro_grads)
        reduced = shared if reduced is None else jax.tree.map(jnp.add, reduced, shared)
    query_grads, passage_grads = (
        lax.psum(jnp.concatenate(query_parts, axis=0).astype(jnp.bfloat16), "tower").astype(
            jnp.float32
        ),
        lax.psum(jnp.concatenate(passage_parts, axis=0).astype(jnp.bfloat16), "tower").astype(
            jnp.float32
        ),
    )
    return (loss_value, query_grads, passage_grads) + tuple(reduced)


def solution(mesh):
    placed = (
        P("dp", None, None),
        P("dp", None, None),
        P("tower", "dp"),
        P(),
        P("dp", None),
        P("dp", None),
        P("dp", None),
        P("dp", None),
        P("dp", None),
        P("dp", None),
        P("dp"),
        P("dp"),
        P("dp"),
        P("dp"),
        P("dp"),
        P("dp"),
        P("dp"),
        P("dp"),
        P("dp"),
    )
    return jax.shard_map(
        per_device,
        mesh=mesh,
        in_specs=placed,
        out_specs=(
            P(),
            P("dp", None, None),
            P("dp", None, None),
            P("dp", None),
            P("dp", None),
            P("dp", None),
            P("dp", None),
            P("dp", None),
            P("dp", None),
            P("dp"),
            P("dp"),
            P("dp"),
            P("dp"),
            P("dp"),
            P("dp"),
            P("dp"),
            P("dp"),
            P("dp"),
        ),
        check_vma=False,
    )
```

profile of v0, /device:TPU:0, one launch (start us, length us, event | category | flops | bytes accessed | tf_op | source)
XLA Modules:
  0.0 2684.5 jit_solution(12807423982081417881)
XLA Ops:
  21.4 79.0 %all-reduce.29 = (bf16[768]{0:T(1024)(128)(2,1)S(1)}, bf16[768]{0:T(1024)(128)(2,1)S(1)}, bf16[768]{0:T(1024)(128)(2,1)}, bf16[768]{0:T(1024)(128)(2,1)}, bf16[7...) all-reduce(bf16[768]{0:T(1024)(128)(2,1)S(1)} %dynamic-update-slice, ...), channel_id=1, replica_groups=mesh['dp'=16,'tower'=2] {'dp'}, use_global_device_ids=true, to_apply=%add | all-reduce | flops 9216 | bytes 36864
  105.1 22.6 all-gather.11.cloned.1.call-done
  127.7 57.8 %all-gather.7.cloned.1.call-done = bf16[768,768]{1,0:T(8,128)(2,1)} async-done(((bf16[48,768]{1,0:T(8,128)(2,1)}), bf16[768,768]{1,0:T(8,128)(2,1)}) %all-gather.7.cloned.1.call-update) | async-done | bytes 1179664 | tf_op jit(solution)/shard_map/all_gather | solution.py:231
  185.6 57.7 %all-gather.13.cloned.1.call-done = bf16[768,768]{1,0:T(8,128)(2,1)} async-done(((bf16[48,768]{1,0:T(8,128)(2,1)}), bf16[768,768]{1,0:T(8,128)(2,1)}) %all-gather.13.cloned.1.call-update) | async-done | bytes 1179664 | tf_op jit(solution)/shard_map/all_gather | solution.py:232
  243.3 82.0 %all-gather.15.cloned.1.call-done = bf16[768,3072]{1,0:T(8,128)(2,1)} async-done(((bf16[48,3072]{1,0:T(8,128)(2,1)}), bf16[768,3072]{1,0:T(8,128)(2,1)}) %all-gather.15.cloned.1.call-update) | async-done | bytes 4718608 | tf_op jit(solution)/shard_map/all_gather | solution.py:233
  325.3 81.8 %all-gather.17.cloned.1.call-done = bf16[3072,768]{1,0:T(8,128)(2,1)} async-done(((bf16[192,768]{1,0:T(8,128)(2,1)}), bf16[3072,768]{1,0:T(8,128)(2,1)}) %all-gather.17.cloned.1.call-update) | async-done | bytes 4718608 | tf_op jit(solution)/shard_map/all_gather | solution.py:234
  407.1 31.1 %conditional.5 = (f32[1,768]{1,0:T(1,128)S(1)}) conditional(s32[]{:T(128)} %convert_element_type.1098, (bf16[1,512,768]{2,1,0:T(8,128)(2,1)}, bf16[768,768]{1,0:T(8,128)(2,1)}, bf16[768]{0:T(1024)(128)(2,1)S(1)}, s32[1]{0:T(128)}, bf16[768,768]{1,0:T(8,128)(2,1)}, /*index=5*/bf16[768]{0:T(1024)(128)(2,1)S(1)}, bf16[768,768]{1,0:T(8,128)(2,1)}, ...), branch_computations={%region_16.24_spmd, %region_24.32_spmd} | conditional | flops 8189128704 | bytes 86706344 | solution.py:355
  430.8 7.0 fusion.589
  438.8 23.1 conditional.4
  454.5 7.0 fusion.575
  463.5 67.5 %collective-permute-start = (f32[2,768]{1,0:T(2,128)S(1)}, f32[2,768]{1,0:T(2,128)S(1)}, u32[]{:S(2)}, u32[]{:S(2)}) collective-permute-start(f32[2,768]{1,0:T(2,128)S(1)} %broadcast_divide_fusion.16), channel_id=1, source_target_pairs={{0,1},{1,0},{2,3},{3,2},{4,5},{5,4},{6,7},{7,6},{8,9},{9,8},{10,11... | collective-permute-start | bytes 18440 | tf_op jit(solution)/shard_map/ppermute | solution.py:16
  532.6 40.2 %all_gather.47 = f32[2,32,768]{2,0,1:T(2,128)S(1)} all-gather(f32[2,2,768]{2,0,1:T(2,128)S(1)} %copy.237), channel_id=1, replica_groups=mesh['dp'=16,'tower'=2] {'dp'}, dimensions={1}, use_global_device_ids=true | all-gather | bytes 208896 | tf_op jit(solution)/shard_map/all_gather | solution.py:366
  575.9 98.5 %all-reduce.35.cloned.1.call-done = f32[32,768]{1,0:T(8,128)} async-done(((f32[32,768]{1,0:T(8,128)}), f32[32,768]{1,0:T(8,128)}) %all-reduce.35.cloned.1.call-update) | async-done | bytes 98320
  676.9 75.2 %conditional.7 = (f32[768,768]{0,1:T(8,128)}, f32[768,768]{0,1:T(8,128)}, f32[768,768]{0,1:T(8,128)}, f32[768,768]{1,0:T(8,128)}, f32[768,3072]{1,0:T(8,128)}, /...) conditional(s32[]{:T(128)} %convert_element_type.1098, ...), branch_computations={%region_82.103_spmd, %region_103.124_spmd} | conditional | flops 24372316160 | bytes 456674720 | solution.py:407
  698.3 5.3 multiply_convert_fusion.10
  716.0 2.7 convert_reduce_fusion.16
  740.8 5.1 fusion.529
  745.8 5.1 fusion.630
  752.1 3.1 copy.239
  755.3 3.1 copy.241
  758.5 3.2 copy.243
  761.8 92.6 %conditional.6 = (f32[768,768]{0,1:T(8,128)}, f32[768,768]{0,1:T(8,128)}, f32[768,768]{0,1:T(8,128)}, f32[768,768]{1,0:T(8,128)}, f32[768,3072]{1,0:T(8,128)}, /...) conditional(s32[]{:T(128)} %convert_element_type.1098, ...), branch_computations={%region_40.61_spmd, %region_61.82_spmd} | conditional | flops 24372316160 | bytes 455222944 | solution.py:407
  791.0 2.6 fusion.595
  798.0 5.6 multiply_convert_fusion.4
  814.3 2.7 multiply_reduce_fusion.18
  817.0 2.8 convert_reduce_fusion.6
  821.1 2.5 convert_reduce_fusion.7
  843.2 5.0 fusion.428
  848.3 4.9 fusion.624
  854.6 3.1 copy.238
  857.7 3.1 copy.240
  860.9 3.1 copy.242
  868.2 2.7 pad_maximum_fusion
  870.9 75.2 %reduce-scatter.27.cloned.1.call-done = f32[48,768]{1,0:T(8,128)} async-done(((f32[768,768]{1,0:T(8,128)}), f32[48,768]{1,0:T(8,128)}) %reduce-scatter.27.cloned.1.call-update) | async-done | bytes 147472 | tf_op jit(solution)/shard_map/reduce_scatter | solution.py:252
  947.7 131.8 %reduce-scatter.15.cloned.1.call-done = f32[48,768]{1,0:T(8,128)} async-done(((f32[768,768]{1,0:T(8,128)}), f32[48,768]{1,0:T(8,128)}) %reduce-scatter.15.cloned.1.call-update) | async-done | bytes 147472 | tf_op jit(solution)/shard_map/reduce_scatter | solution.py:249
  1081.0 130.9 %reduce-scatter.19.cloned.1.call-done = f32[48,768]{1,0:T(8,128)} async-done(((f32[768,768]{1,0:T(8,128)}), f32[48,768]{1,0:T(8,128)}) %reduce-scatter.19.cloned.1.call-update) | async-done | bytes 147472 | tf_op jit(solution)/shard_map/reduce_scatter | solution.py:250
  1213.4 131.7 %reduce-scatter.23.cloned.1.call-done = f32[48,768]{1,0:T(8,128)} async-done(((f32[768,768]{1,0:T(8,128)}), f32[48,768]{1,0:T(8,128)}) %reduce-scatter.23.cloned.1.call-update) | async-done | bytes 147472 | tf_op jit(solution)/shard_map/reduce_scatter | solution.py:251
  1346.6 130.7 %reduce-scatter.25.cloned.1.call-done = f32[48,768]{1,0:T(8,128)} async-done(((f32[768,768]{1,0:T(8,128)}), f32[48,768]{1,0:T(8,128)}) %reduce-scatter.25.cloned.1.call-update) | async-done | bytes 147472 | tf_op jit(solution)/shard_map/reduce_scatter | solution.py:252
  1478.9 131.6 %reduce-scatter.13.cloned.1.call-done = f32[48,768]{1,0:T(8,128)} async-done(((f32[768,768]{1,0:T(8,128)}), f32[48,768]{1,0:T(8,128)}) %reduce-scatter.13.cloned.1.call-update) | async-done | bytes 147472 | tf_op jit(solution)/shard_map/reduce_scatter | solution.py:249
  1612.1 130.6 %reduce-scatter.17.cloned.1.call-done = f32[48,768]{1,0:T(8,128)} async-done(((f32[768,768]{1,0:T(8,128)}), f32[48,768]{1,0:T(8,128)}) %reduce-scatter.17.cloned.1.call-update) | async-done | bytes 147472 | tf_op jit(solution)/shard_map/reduce_scatter | solution.py:250
  1744.2 131.5 %reduce-scatter.21.cloned.1.call-done = f32[48,768]{1,0:T(8,128)} async-done(((f32[768,768]{1,0:T(8,128)}), f32[48,768]{1,0:T(8,128)}) %reduce-scatter.21.cloned.1.call-update) | async-done | bytes 147472 | tf_op jit(solution)/shard_map/reduce_scatter | solution.py:251
  1877.3 174.1 %reduce-scatter.31.cloned.1.call-done = f32[48,3072]{1,0:T(8,128)} async-done(((f32[768,3072]{1,0:T(8,128)}), f32[48,3072]{1,0:T(8,128)}) %reduce-scatter.31.cloned.1.call-update) | async-done | bytes 589840 | tf_op jit(solution)/shard_map/reduce_scatter | solution.py:253
  2053.3 174.7 %reduce-scatter.35.cloned.1.call-done = f32[192,768]{1,0:T(8,128)} async-done(((f32[3072,768]{1,0:T(8,128)}), f32[192,768]{1,0:T(8,128)}) %reduce-scatter.35.cloned.1.call-update) | async-done | bytes 589840 | tf_op jit(solution)/shard_map/reduce_scatter | solution.py:254
  2229.8 174.0 %reduce-scatter.29.cloned.1.call-done = f32[48,3072]{1,0:T(8,128)} async-done(((f32[768,3072]{1,0:T(8,128)}), f32[48,3072]{1,0:T(8,128)}) %reduce-scatter.29.cloned.1.call-update) | async-done | bytes 589840 | tf_op jit(solution)/shard_map/reduce_scatter | solution.py:253
  2405.6 174.9 %reduce-scatter.33.cloned.1.call-done = f32[192,768]{1,0:T(8,128)} async-done(((f32[3072,768]{1,0:T(8,128)}), f32[192,768]{1,0:T(8,128)}) %reduce-scatter.33.cloned.1.call-update) | async-done | bytes 589840 | tf_op jit(solution)/shard_map/reduce_scatter | solution.py:254
  2584.6 75.9 %all-reduce.28 = (f32[]{:T(128)}, bf16[768]{0:T(1024)(128)(2,1)S(1)}, bf16[768]{0:T(1024)(128)(2,1)S(1)}, bf16[768]{0:T(1024)(128)(2,1)S(1)}, bf16[768]{0:T(1024...) all-reduce(f32[]{:T(128)} %get-tuple-element.1415, ...), channel_id=1, replica_groups=mesh['dp'=16,'tower'=2] {'dp'}, use_global_device_ids=true, to_apply=%region_37.38 | all-reduce | flops 18433 | bytes 110600 | tf_op jit(solution)/shard_map/psum | solution.py:379
  2662.5 2.6 all-reduce.30
  2669.5 3.4 convert_element_type.1100
  (529 shorter events, 190.8 us)
Async XLA Ops:
  7.2 97.9 %all-gather.9.cloned.1.call-start = ((), (), s32[]{:S(2)}) async-start(), calls=%async_computation.13 | async-start | bytes 1253376 | tf_op jit(solution)/shard_map/all_gather | solution.py:229
  7.9 119.8 %all-gather.11.cloned.1.call-start = ((), (), s32[]{:S(2)}) async-start(), calls=%async_computation.14 | async-start | bytes 1253376 | tf_op jit(solution)/shard_map/all_gather | solution.py:230
  8.7 176.9 %all-gather.7.cloned.1.call-start = ((), (), s32[]{:S(2)}) async-start(), calls=%async_computation.12 | async-start | bytes 1253376 | tf_op jit(solution)/shard_map/all_gather | solution.py:231
  9.4 233.9 %all-gather.13.cloned.1.call-start = ((), (), s32[]{:S(2)}) async-start(), calls=%async_computation.15 | async-start | bytes 1253376 | tf_op jit(solution)/shard_map/all_gather | solution.py:232
  10.0 315.3 %all-gather.15.cloned.1.call-start = ((), (), s32[]{:S(2)}) async-start(), calls=%async_computation.16 | async-start | bytes 5013504 | tf_op jit(solution)/shard_map/all_gather | solution.py:233
  10.6 396.5 %all-gather.17.cloned.1.call-start = ((), (), s32[]{:S(2)}) async-start(), calls=%async_computation.17 | async-start | bytes 5013504 | tf_op jit(solution)/shard_map/all_gather | solution.py:234
  11.1 663.3 %all-reduce.35.cloned.1.call-start = ((), (), s32[]{:S(2)}) async-start(), calls=%async_computation.30 | async-start | bytes 196608
  100.4 576.5 %copy-start.92 = (bf16[3072]{0:T(1024)(128)(2,1)}, bf16[3072]{0:T(1024)(128)(2,1)S(1)}, u32[]{:S(2)}) copy-start(bf16[3072]{0:T(1024)(128)(2,1)S(1)} %get-tuple-element.1224) | copy-start | bytes 18436
  102.7 335.5 %copy-start.29 = (bf16[1,64,768]{2,1,0:T(8,128)(2,1)}, bf16[1,64,768]{2,1,0:T(8,128)(2,1)S(1)}, u32[]{:S(2)}) copy-start(bf16[1,64,768]{2,1,0:T(8,128)(2,1)S(1)} %get-tuple-element.1404) | copy-start | bytes 294916
  105.1 333.1 %copy-start.33 = (bf16[1,512,768]{2,1,0:T(8,128)(2,1)}, bf16[1,512,768]{2,1,0:T(8,128)(2,1)S(1)}, u32[]{:S(2)}) copy-start(bf16[1,512,768]{2,1,0:T(8,128)(2,1)S(1)} %get-tuple-element.1400) | copy-start | bytes 2359300
  411.6 14.0 copy-start.7
  463.5 68.4 %collective-permute-start = (f32[2,768]{1,0:T(2,128)S(1)}, f32[2,768]{1,0:T(2,128)S(1)}, u32[]{:S(2)}, u32[]{:S(2)}) collective-permute-start(f32[2,768]{1,0:T(2,128)S(1)} %broadcast_divide_fusion.16), channel_id=1, source_target_pairs={{0,1},{1,0},{2,3},{3,2},{4,5},{5,4},{6,7},{7,6},{8,9},{9,8},{10,11... | collective-permute-start | bytes 18440 | tf_op jit(solution)/shard_map/ppermute | solution.py:16
  575.2 370.9 %reduce-scatter.27.cloned.1.call-start = ((), (), s32[]{:S(2)}) async-start(), calls=%async_computation.25 | async-start | bytes 2506752 | tf_op jit(solution)/shard_map/reduce_scatter | solution.py:252
  695.3 20.7 copy-start.79
  697.5 11.2 slice-start.10
  698.0 13.0 copy-start.36
  698.0 13.0 copy-start.116
  698.2 12.8 copy-start.133
  698.2 10.5 slice-start.11
  716.0 12.7 copy-start.16
  721.3 10.7 copy-start.2
  752.1 327.4 %reduce-scatter.15.cloned.1.call-start = ((), (), s32[]{:S(2)}) async-start(), calls=%async_computation.19 | async-start | bytes 2506752 | tf_op jit(solution)/shard_map/reduce_scatter | solution.py:249
  755.2 456.7 %reduce-scatter.19.cloned.1.call-start = ((), (), s32[]{:S(2)}) async-start(), calls=%async_computation.21 | async-start | bytes 2506752 | tf_op jit(solution)/shard_map/reduce_scatter | solution.py:250
  758.4 586.7 %reduce-scatter.23.cloned.1.call-start = ((), (), s32[]{:S(2)}) async-start(), calls=%async_computation.23 | async-start | bytes 2506752 | tf_op jit(solution)/shard_map/reduce_scatter | solution.py:251
  761.8 715.6 %reduce-scatter.25.cloned.1.call-start = ((), (), s32[]{:S(2)}) async-start(), calls=%async_computation.24 | async-start | bytes 2506752 | tf_op jit(solution)/shard_map/reduce_scatter | solution.py:252
  780.0 10.9 copy-start.157
  783.8 12.0 copy-start.128
  795.8 12.4 slice-start.14
  797.7 12.7 copy-start.38
  797.7 12.7 copy-start.118
  797.9 12.5 copy-start.135
  854.5 756.0 %reduce-scatter.13.cloned.1.call-start = ((), (), s32[]{:S(2)}) async-start(), calls=%async_computation.18 | async-start | bytes 2506752 | tf_op jit(solution)/shard_map/reduce_scatter | solution.py:249
  857.7 885.0 %reduce-scatter.17.cloned.1.call-start = ((), (), s32[]{:S(2)}) async-start(), calls=%async_computation.20 | async-start | bytes 2506752 | tf_op jit(solution)/shard_map/reduce_scatter | solution.py:250
  860.8 1015.0 %reduce-scatter.21.cloned.1.call-start = ((), (), s32[]{:S(2)}) async-start(), calls=%async_computation.22 | async-start | bytes 2506752 | tf_op jit(solution)/shard_map/reduce_scatter | solution.py:251
  864.0 1187.4 %reduce-scatter.31.cloned.1.call-start = ((), (), s32[]{:S(2)}) async-start(), calls=%async_computation.27 | async-start | bytes 10027008 | tf_op jit(solution)/shard_map/reduce_scatter | solution.py:253
  864.6 1363.4 %reduce-scatter.35.cloned.1.call-start = ((), (), s32[]{:S(2)}) async-start(), calls=%async_computation.29 | async-start | bytes 10027008 | tf_op jit(solution)/shard_map/reduce_scatter | solution.py:254
  865.2 1538.6 %reduce-scatter.29.cloned.1.call-start = ((), (), s32[]{:S(2)}) async-start(), calls=%async_computation.26 | async-start | bytes 10027008 | tf_op jit(solution)/shard_map/reduce_scatter | solution.py:253
  865.8 1714.7 %reduce-scatter.33.cloned.1.call-start = ((), (), s32[]{:S(2)}) async-start(), calls=%async_computation.28 | async-start | bytes 10027008 | tf_op jit(solution)/shard_map/reduce_scatter | solution.py:254
  866.5 1801.2 %all-reduce.37.cloned.1.call-start = ((), (), s32[]{:S(2)}) async-start(), calls=%async_computation.31 | async-start | bytes 7077888 | tf_op jit(solution)/shard_map/psum | solution.py:413
  2053.2 530.3 %copy-start.115 = (f32[12,64]{1,0:T(8,128)S(1)}, f32[12,64]{1,0:T(8,128)}, u32[]{:S(2)}) copy-start(f32[12,64]{1,0:T(8,128)} %get-tuple-element.1153) | copy-start | bytes 9220
  2053.2 530.4 %copy-start.141 = (f32[12,64]{1,0:T(8,128)S(1)}, f32[12,64]{1,0:T(8,128)}, u32[]{:S(2)}) copy-start(f32[12,64]{1,0:T(8,128)} %get-tuple-element.1155) | copy-start | bytes 9220
  2053.2 531.3 %copy-start.121 = (f32[768]{0:T(1024)S(1)}, f32[768]{0:T(1024)}, u32[]{:S(2)}) copy-start(f32[768]{0:T(1024)} %get-tuple-element.1167) | copy-start | bytes 9220
  2053.2 531.3 %copy-start.122 = (f32[768]{0:T(1024)S(1)}, f32[768]{0:T(1024)}, u32[]{:S(2)}) copy-start(f32[768]{0:T(1024)} %get-tuple-element.1169) | copy-start | bytes 9220
  2053.2 531.3 %copy-start.125 = (f32[768]{0:T(1024)S(1)}, f32[768]{0:T(1024)}, u32[]{:S(2)}) copy-start(f32[768]{0:T(1024)} %get-tuple-element.1161) | copy-start | bytes 9220
  2053.3 531.3 %copy-start.126 = (f32[768]{0:T(1024)S(1)}, f32[768]{0:T(1024)}, u32[]{:S(2)}) copy-start(f32[768]{0:T(1024)} %get-tuple-element.1157) | copy-start | bytes 9220
  2053.3 531.3 %copy-start.139 = (f32[3072]{0:T(1024)S(1)}, f32[3072]{0:T(1024)}, u32[]{:S(2)}) copy-start(f32[3072]{0:T(1024)} %get-tuple-element.1159) | copy-start | bytes 36868
  2053.3 531.3 %copy-start.143 = (f32[768]{0:T(1024)S(1)}, f32[768]{0:T(1024)}, u32[]{:S(2)}) copy-start(f32[768]{0:T(1024)} %get-tuple-element.1163) | copy-start | bytes 9220
  2053.3 531.3 %copy-start.144 = (f32[768]{0:T(1024)S(1)}, f32[768]{0:T(1024)}, u32[]{:S(2)}) copy-start(f32[768]{0:T(1024)} %get-tuple-element.1165) | copy-start | bytes 9220
  (87 other events, 384.1 us)
Sparse Core Ops, SparseCore 0:
  10.8 59.1 all-gather.8
  72.9 54.8 all-gather.10
  130.5 54.9 all-gather.6
  188.2 54.9 all-gather.12
  245.9 79.3 all-gather.14
  327.9 79.0 all-gather.16
  575.4 99.0 all-reduce.34
  752.2 193.8 reduce-scatter.26
  951.8 127.6 reduce-scatter.14
  1084.2 127.5 reduce-scatter.18
  1217.6 127.4 reduce-scatter.22
  1349.9 127.4 reduce-scatter.24
  1483.0 127.4 reduce-scatter.12
  1615.9 126.7 reduce-scatter.16
  1748.2 127.5 reduce-scatter.20
  1881.3 170.0 reduce-scatter.30
  2057.9 170.0 reduce-scatter.34
  2233.5 170.1 reduce-scatter.28
  2410.4 169.9 reduce-scatter.32
  2584.9 24.6 all-reduce.36
where the time goes:
time: 2690 us; the launch traced here: 2680 us
  waiting for transfers between devices  2100 us (78%)
  blocking collectives  198 us (7%)
  matrix products  130 us (5%)
  other arithmetic  74 us (3%)
  starting transfers between devices  68.3 us (3%)
  local copies, waits for them, and re-layouts  62.8 us (2%)
  loops' own time  33.2 us (1%)
    reduce_scatter x2, waiting for transfers between devices, reduce_grads(): lax.psum_scatter(grads[5], 'dp', scatter_dimension=0, tiled=True)  350 us
    reduce_scatter x2, waiting for transfers between devices, reduce_grads(): lax.psum_scatter(grads[4], 'dp', scatter_dimension=0, tiled=True)  348 us
    reduce_scatter x2, waiting for transfers between devices, reduce_grads(): lax.psum_scatter(grads[0], 'dp', scatter_dimension=0, tiled=True)  263 us
    reduce_scatter x2, waiting for transfers between devices, reduce_grads(): lax.psum_scatter(grads[2], 'dp', scatter_dimension=0, tiled=True)  263 us
    reduce_scatter x2, waiting for transfers between devices, reduce_grads(): lax.psum_scatter(grads[1], 'dp', scatter_dimension=0, tiled=True)  261 us
    reduce_scatter x2, waiting for transfers between devices, reduce_grads(): lax.psum_scatter(grads[3], 'dp', scatter_dimension=0, tiled=True)  206 us
    unnamed x21, waiting for transfers between devices  105 us
    all_gather x1, waiting for transfers between devices, fetch(): lax.all_gather(shards[4], 'dp', axis=0, tiled=True)  82 us
  transfers between devices with their start and end apart: 21, of which 19 were waited for; matrix products, arithmetic and copies ran while one was open for 5% of the time, Pallas kernels for 0%

commit v1 on v0

v1 whole, which is shorter than its diff:
```python
import functools

import jax
import jax.numpy as jnp
from jax import lax
from jax.experimental import pallas as pl
from jax.experimental.pallas import tpu as pltpu
from jax.sharding import PartitionSpec as P

MESH = pl.DeviceIdType.MESH
ANY = pl.BlockSpec(memory_space=pl.ANY)
VM = pl.BlockSpec(memory_space=pltpu.VMEM)


class Place:
    def __init__(self, inner):
        dp = lax.axis_index("dp")
        self.c = lax.axis_index("tower")
        self.inner = inner
        self.low = lax.rem(dp, inner)
        self.me = dp // inner
        self.z = self.me // 4
        self.quad = lax.rem(self.me, 4)
        s1 = 1 + self.c
        s2 = 2 - self.c
        b1 = lax.rem(self.quad // s1, 2)
        b2 = lax.rem(self.quad // s2, 2)
        self.q1 = self.quad + s1 * (1 - 2 * b1)
        self.q2 = self.quad + s2 * (1 - 2 * b2)
        self.q12 = 3 - self.quad
        self.quads = (self.quad, self.q1, self.q2, self.q12)

    def ring(self, k):
        return lax.rem(self.z + k, 4)

    def dev(self, group):
        return {"dp": group * self.inner + self.low, "tower": self.c}

    def n1(self):
        return self.dev(self.z * 4 + self.q1)

    def n2(self):
        return self.dev(self.z * 4 + self.q2)

    def up(self, k):
        return self.dev(self.ring(k) * 4 + self.quad)

    def sib(self):
        return {"dp": self.me * self.inner + self.low, "tower": 1 - self.c}

    def barrier(self):
        sem = pltpu.get_barrier_semaphore()
        for target in (self.up(1), self.up(2), self.up(3), self.n1(), self.n2(), self.sib()):
            pl.semaphore_signal(sem, inc=1, device_id=target, device_id_type=MESH)
        pl.semaphore_wait(sem, 6)


def remote(src, dst, send_sem, recv_sem, target):
    return pltpu.make_async_remote_copy(
        src_ref=src, dst_ref=dst, send_sem=send_sem, recv_sem=recv_sem, device_id=target, device_id_type=MESH
    )


class Cut:
    def __init__(self, per):
        self.per = per
        self.each = 4 // per
        self.count = 3 * self.each

    def kind(self, g):
        return g // self.each, g % self.each

    def shape(self, kind):
        per = self.per
        return ((per, 48, 384), (48, 384 * per), (48 * per, 384))[kind]

    def whole(self, refs, g, s, which):
        per = self.per
        kind, n = self.kind(g)
        ref = refs[kind]
        if kind == 0:
            return ref.at[pl.ds(n * per, per), pl.ds(pl.multiple_of(s * 48, 16), 48), pl.ds(pl.multiple_of(which * 384, 128), 384)]
        if kind == 1:
            return ref.at[pl.ds(pl.multiple_of(s * 48, 16), 48), pl.ds(pl.multiple_of((2 * n + which) * 384 * per, 128), 384 * per)]
        return ref.at[pl.ds(pl.multiple_of(s * 192 + n * 48 * per, 16), 48 * per), pl.ds(pl.multiple_of(which * 384, 128), 384)]

    def shard(self, refs, g, which):
        per = self.per
        kind, n = self.kind(g)
        ref = refs[kind]
        if kind == 0:
            return ref.at[pl.ds(n * per, per), :, pl.ds(pl.multiple_of(which * 384, 128), 384)]
        if kind == 1:
            return ref.at[:, pl.ds(pl.multiple_of((2 * n + which) * 384 * per, 128), 384 * per)]
        return ref.at[pl.ds(n * 48 * per, 48 * per), pl.ds(pl.multiple_of(which * 384, 128), 384)]


def gather_kernel(inner, cut, v_in, a_in, i_in, o_in, len_in, v_out, a_out, i_out, o_out, len_out, ssem, rsem, lsem, xsem):
    p = Place(inner)
    c = p.c
    groups = cut.count + 1
    ins = (a_in, i_in, o_in)
    outs = (a_out, i_out, o_out)
    local = [pltpu.make_async_copy(len_in, len_out.at[c], lsem.at[0]), pltpu.make_async_copy(v_in, v_out.at[p.me], lsem.at[1])]
    rows = pl.ds(pl.multiple_of(p.me * 48, 16), 48)
    local.append(pltpu.make_async_copy(a_in, a_out.at[:, rows], lsem.at[2]))
    local.append(pltpu.make_async_copy(i_in, i_out.at[rows], lsem.at[3]))
    local.append(pltpu.make_async_copy(o_in, o_out.at[pl.ds(pl.multiple_of(p.me * 192, 16), 192)], lsem.at[4]))
    for copy in local:
        copy.start()
    p.barrier()

    def slot(t, s, which):
        if t == 0:
            return v_out.at[s, :, pl.ds(pl.multiple_of(which * 128, 128), 128)]
        return cut.whole(outs, t - 1, s, which)

    def own(t):
        if t == 0:
            return v_in.at[:, pl.ds(pl.multiple_of(c * 128, 128), 128)]
        return cut.shard(ins, t - 1, c)

    lens = remote(len_in, len_out.at[c], xsem.at[0], xsem.at[1], p.sib())
    lens.start()

    def push(t, src, s, k, target):
        remote(src, slot(t, s, c), ssem.at[t, k], rsem.at[t, k], target).start()

    def arrived(t, s, k, which):
        view = slot(t, s, which)
        remote(view, view, ssem.at[t, k], rsem.at[t, k], p.sib()).wait_recv()

    def shard(k, q):
        return p.ring(4 - k) * 4 + p.quads[q]

    def stage_own(t):
        for k in range(1, 4):
            push(t, own(t), p.me, k, p.up(k))
        push(t, own(t), p.me, 4, p.n1())
        push(t, own(t), p.me, 8, p.n2())

    def stage_z(t):
        for k in range(1, 4):
            s = shard(k, 0)
            arrived(t, s, k, c)
            view = slot(t, s, c)
            push(t, view, s, 4 + k, p.n1())
            push(t, view, s, 8 + k, p.n2())
            push(t, view, s, 16 + k, p.sib())

    def stage_one(t):
        for k in range(4):
            s = shard(k, 1)
            arrived(t, s, 4 + k, c)
            view = slot(t, s, c)
            push(t, view, s, 12 + k, p.n2())
            push(t, view, s, 20 + k, p.sib())

    def stage_two(t):
        for q in (2, 3):
            for k in range(4):
                s = shard(k, q)
                arrived(t, s, q * 4 + k, c)
                view = slot(t, s, c)
                push(t, view, s, 16 + q * 4 + k, p.sib())

    ahead = AHEAD
    for t in range(ahead):
        stage_own(t)
    for step in range(groups + 2):
        if step < groups:
            stage_z(step)
        if step + ahead < groups:
            stage_own(step + ahead)
        if 0 <= step - 1 < groups:
            stage_one(step - 1)
        if 0 <= step - 2 < groups:
            stage_two(step - 2)

    for t in range(groups):
        for q in range(4):
            sq = (0, 2, 1, 3)[q]
            for k in range(4):
                if q == 0 and k == 0:
                    continue
                s = shard(k, sq)
                arrived(t, s, 16 + q * 4 + k, 1 - c)
    for t in range(groups):
        for k in range(1, 32):
            if k == 16:
                continue
            view = slot(t, p.me, c)
            remote(view, view, ssem.at[t, k], rsem.at[t, k], p.sib()).wait_send()
    for copy in local:
        copy.wait()
    lens.wait_send()
    remote(len_in, len_out.at[1 - c], xsem.at[0], xsem.at[1], p.sib()).wait_recv()

AHEAD = 1

def gather_all(inner, cut, vec, wa, wi, wo, lens, cid=0):
    bf = jnp.bfloat16
    groups = cut.count + 1
    return pl.pallas_call(
        functools.partial(gather_kernel, inner, cut),
        out_shape=(
            jax.ShapeDtypeStruct((16,) + vec.shape, bf),
            jax.ShapeDtypeStruct((4, 768, 768), bf),
            jax.ShapeDtypeStruct((768, 3072), bf),
            jax.ShapeDtypeStruct((3072, 768), bf),
            jax.ShapeDtypeStruct((2,) + lens.shape, jnp.int32),
        ),
        in_specs=[ANY] * 5,
        out_specs=[ANY] * 5,
        scratch_shapes=[
            pltpu.SemaphoreType.DMA((groups, 32)),
            pltpu.SemaphoreType.DMA((groups, 32)),
            pltpu.SemaphoreType.DMA((5,)),
            pltpu.SemaphoreType.DMA((2,)),
        ],
        compiler_params=pltpu.CompilerParams(collective_id=cid, has_side_effects=True),
        name="gather_weights",
    )(vec, wa, wi, wo, lens)


def scatter_kernel(inner, cut, v_in, a_in, i_in, o_in, x_in, v_out, a_out, i_out, o_out, q_out, p_out, *scr):
    p = Place(inner)
    c = p.c
    groups = cut.count + 1
    bufs = [scr[4 * i : 4 * i + 4] for i in range(5)]
    ssem, rsem, lsem, xsem = scr[20:24]
    ins = (a_in, i_in, o_in)
    outs = (a_out, i_out, o_out)

    def buf(level, t):
        if t == 0:
            return bufs[level][0]
        kind, n = cut.kind(t - 1)
        return bufs[level][1 + kind].at[n]

    def part(t, s, which):
        if t == 0:
            return v_in.at[s, :, pl.ds(pl.multiple_of(which * 128, 128), 128)]
        return cut.whole(ins, t - 1, s, which)

    def result(t, which):
        if t == 0:
            return v_out.at[:, pl.ds(pl.multiple_of(which * 128, 128), 128)]
        return cut.shard(outs, t - 1, which)

    order = tuple(range(groups - 1, -1, -1))
    for t in order:
        @pl.loop(0, 16)
        def _(s):
            pltpu.make_async_copy(part(t, s, c), buf(0, t).at[s], lsem.at[t]).start()

    p_rows = x_in.at[pl.ds(0, p_out.shape[1])]
    q_rows = x_in.at[pl.ds(p_out.shape[1], q_out.shape[1])]
    mine = [pltpu.make_async_copy(p_rows, p_out.at[c], xsem.at[0]), pltpu.make_async_copy(q_rows, q_out.at[c], xsem.at[1])]
    for copy in mine:
        copy.start()
    p.barrier()
    theirs = [remote(p_rows, p_out.at[c], xsem.at[2], xsem.at[3], p.sib()), remote(q_rows, q_out.at[c], xsem.at[4], xsem.at[5], p.sib())]

    def share(t):
        for sq in (p.q12, p.q1, p.q2, p.quad):
            @pl.loop(0, 4)
            def _(z):
                s = z * 4 + sq
                remote(part(t, s, 1 - c), buf(1, t).at[s], ssem.at[t, s], rsem.at[t, s], p.sib()).start()

    def add(t, s, other):
        acc = buf(0, t)
        acc[s] = (acc[s].astype(jnp.float32) + other.astype(jnp.float32)).astype(acc.dtype)

    def recv(t, k, ref):
        remote(ref, ref, ssem.at[t, k], rsem.at[t, k], p.sib()).wait_recv()

    def stage0(t):
        acc, r0, r1 = buf(0, t), buf(1, t), buf(2, t)
        pltpu.make_async_copy(acc, acc, lsem.at[t]).wait()
        for j, q in enumerate((p.q2, p.q12)):
            @pl.loop(0, 4)
            def _(z):
                s = z * 4 + q
                recv(t, s, r0.at[s])
                add(t, s, r0[s])
                k = 16 + z * 2 + j
                remote(acc.at[s], r1.at[z * 2 + j], ssem.at[t, k], rsem.at[t, k], p.n2()).start()
        for q in (p.q1, p.quad):
            @pl.loop(0, 4)
            def _(z):
                s = z * 4 + q
                recv(t, s, r0.at[s])
                add(t, s, r0[s])

    def stage1(t):
        acc, r1, r2 = buf(0, t), buf(2, t), buf(3, t)
        @pl.loop(0, 4)
        def _(z):
            s = z * 4 + p.q1
            recv(t, 17 + z * 2, r1.at[z * 2 + 1])
            add(t, s, r1[z * 2 + 1])
            remote(acc.at[s], r2.at[z], ssem.at[t, 24 + z], rsem.at[t, 24 + z], p.n1()).start()
        @pl.loop(0, 4)
        def _(z):
            s = z * 4 + p.quad
            recv(t, 16 + z * 2, r1.at[z * 2])
            add(t, s, r1[z * 2])

    def stage2(t):
        acc, r2, r3 = buf(0, t), buf(3, t), buf(4, t)
        for k in range(1, 4):
            z = p.ring(k)
            s = z * 4 + p.quad
            recv(t, 24 + z, r2.at[z])
            add(t, s, r2[z])
            remote(acc.at[s], r3.at[k], ssem.at[t, 28 + k], rsem.at[t, 28 + k], p.up(k)).start()
        recv(t, 24 + p.z, r2.at[p.z])

    def stage3(t):
        acc, r2, r3 = buf(0, t), buf(3, t), buf(4, t)
        total = acc[p.me].astype(jnp.float32) + r2[p.z].astype(jnp.float32)
        for k in range(1, 4):
            recv(t, 28 + k, r3.at[k])
            total = total + r3[k].astype(jnp.float32)
        view = result(t, c)
        view[...] = total
        remote(view, view, ssem.at[t, 28], rsem.at[t, 28], p.sib()).start()

    ahead = AHEAD
    for t in order[:ahead]:
        share(t)
    for step in range(groups + 3):
        if step + ahead < groups:
            share(order[step + ahead])
        for lag, stage in enumerate((stage0, stage1, stage2, stage3)):
            if 0 <= step - lag < groups:
                stage(order[step - lag])
    for copy in theirs:
        copy.start()
    for copy in theirs:
        copy.wait_send()
    remote(p_rows, p_out.at[1 - c], xsem.at[2], xsem.at[3], p.sib()).wait_recv()
    remote(q_rows, q_out.at[1 - c], xsem.at[4], xsem.at[5], p.sib()).wait_recv()
    for copy in mine:
        copy.wait()
    for t in order:
        recv(t, 28, result(t, 1 - c))
        acc = buf(0, t)
        @pl.loop(0, 28)
        def _(k):
            remote(acc.at[0], acc.at[0], ssem.at[t, k], rsem.at[t, k], p.sib()).wait_send()
        for k in range(1, 4):
            remote(acc.at[0], acc.at[0], ssem.at[t, 28 + k], rsem.at[t, 28 + k], p.sib()).wait_send()
        remote(result(t, c), result(t, c), ssem.at[t, 28], rsem.at[t, 28], p.sib()).wait_send()


def scatter_all(inner, cut, vec, ga, gi, go, dx, cid=1):
    f32, bf = jnp.float32, jnp.bfloat16
    groups = cut.count + 1
    scratch = []
    for count in (16, 16, 8, 4, 4):
        scratch.append(pltpu.VMEM((count, 16, 128), f32))
        scratch += [pltpu.VMEM((cut.each, count) + cut.shape(kind), bf) for kind in range(3)]
    return pl.pallas_call(
        functools.partial(scatter_kernel, inner, cut),
        out_shape=(
            jax.ShapeDtypeStruct((16, 256), f32),
            jax.ShapeDtypeStruct((4, 48, 768), f32),
            jax.ShapeDtypeStruct((48, 3072), f32),
            jax.ShapeDtypeStruct((192, 768), f32),
            jax.ShapeDtypeStruct((2, Q, 768), f32),
            jax.ShapeDtypeStruct((2, S, 768), f32),
        ),
        in_specs=[ANY] * 5,
        out_specs=[VM] * 4 + [ANY] * 2,
        scratch_shapes=scratch + [
            pltpu.SemaphoreType.DMA((groups, 32)),
            pltpu.SemaphoreType.DMA((groups, 32)),
            pltpu.SemaphoreType.DMA((groups,)),
            pltpu.SemaphoreType.DMA((6,)),
        ],
        compiler_params=pltpu.CompilerParams(collective_id=cid, has_side_effects=True, vmem_limit_bytes=56 << 20),
        name="scatter_grads",
    )(vec, ga, gi, go, dx)


S, Q = 512, 64
T = S + Q


def dot(left, right):
    return jnp.dot(left, right, preferred_element_type=jnp.float32)


def dot_nt(left, right):
    return lax.dot_general(left, right, (((1,), (1,)), ((), ())), preferred_element_type=jnp.float32)


def block(index, size):
    return pl.ds(pl.multiple_of(index * size, size), size)


def low(x):
    return x.astype(jnp.bfloat16)


def wide(x):
    return x.astype(jnp.float32)


def head_mask(h):
    lane = lax.broadcasted_iota(jnp.int32, (1, 128), 1)
    return low(jnp.where(lane // 64 == h, 1.0, 0.0))


SPANS = ((0, S, 256), (S, Q, Q))


def forward_kernel(lens, x, vec, a_hbm, i_hbm, o_hbm,
                   q, k, v, prob, prob_q, x_t, q_t, ctx_t, norm_t, act_t, slope, y1, r1, y2, r2, pooled,
                   wa, wi, wo, ctx, normed, act, sem):
    loads = [pltpu.make_async_copy(a_hbm, wa, sem.at[0]), pltpu.make_async_copy(i_hbm, wi, sem.at[1]), pltpu.make_async_copy(o_hbm, wo, sem.at[2])]
    for load in loads:
        load.start()
    x_t[...] = x[...].T
    loads[0].wait()
    for m, (out, row) in enumerate(((q, 0), (k, None), (v, 1))):
        @pl.loop(0, 3)
        def _(n):
            cols = block(n, 256)
            acc = dot(x[...], wa[m, :, cols])
            if row is not None:
                acc = acc + vec[row : row + 1, cols]
            out[:, cols] = low(acc)
    q_t[...] = q[...].T

    @pl.loop(0, 6)
    def _(j):
        cols = block(j, 128)
        for (start, size, rb), probs, length in zip(SPANS, (prob, prob_q), (lens[0], lens[1])):
            rows = slice(start, start + size)
            kp, vp = k[rows, cols], v[rows, cols]
            valid = lax.broadcasted_iota(jnp.int32, (1, size), 1) < length
            for r in range(0, size, rb):
                qp = q[start + r : start + r + rb, cols]
                total = None
                for h in range(2):
                    mask = head_mask(h)
                    scores = dot_nt(qp * (mask * 0.125), kp)
                    scores = jnp.where(valid, scores, -1e9)
                    e = jnp.exp(scores - jnp.max(scores, axis=1, keepdims=True))
                    p = low(e * (1.0 / jnp.sum(e, axis=1, keepdims=True)))
                    probs[2 * j + h, r : r + rb] = p
                    part = dot(p, vp * mask)
                    total = part if total is None else total + part
                ctx[start + r : start + r + rb, cols] = low(total)
    ctx_t[...] = ctx[...].T

    @pl.loop(0, 3)
    def _(n):
        rows = block(n, 192)
        first = wide(x[rows]) + (dot(ctx[rows], wa[3]) + vec[2:3, :768])
        center = first - jnp.mean(first, axis=1, keepdims=True)
        scale = lax.rsqrt(jnp.mean(center * center, axis=1, keepdims=True) + 1e-12)
        y = center * scale
        y1[rows] = y
        r1[rows] = scale
        normed[rows] = low(y * vec[4:5, :768] + vec[5:6, :768])
    norm_t[...] = normed[...].T
    loads[1].wait()

    @pl.loop(0, 12)
    def _(n):
        cols = block(n, 256)
        u = dot(normed[...], wi[:, cols]) + vec[8:9, cols]
        cdf = 0.5 * (1.0 + lax.erf(u * 0.7071067811865476))
        a = low(u * cdf)
        act[:, cols] = a
        act_t[cols] = a.T
        slope[:, cols] = low(cdf + u * (0.3989422804014327 * jnp.exp(-0.5 * u * u)))
    loads[2].wait()
    pooled[...] = jnp.zeros_like(pooled)

    @pl.loop(0, 3)
    def _(n):
        rows = block(n, 192)
        second = y1[rows] * vec[4:5, :768] + vec[5:6, :768] + (dot(act[rows], wo[...]) + vec[3:4, :768])
        center = second - jnp.mean(second, axis=1, keepdims=True)
        scale = lax.rsqrt(jnp.mean(center * center, axis=1, keepdims=True) + 1e-12)
        y = center * scale
        y2[rows] = y
        r2[rows] = scale
        out = y * vec[6:7, :768] + vec[7:8, :768]
        at = lax.broadcasted_iota(jnp.int32, (192, 1), 0) + n * 192
        for row, keep in ((0, (at >= S) & (at - S < lens[1])), (1, (at < S) & (at < lens[0]))):
            pooled[row : row + 1] += jnp.sum(jnp.where(keep, out, 0.0), axis=0, keepdims=True)
    pooled[0:1] = pooled[0:1] / wide(jnp.full((1, 1), lens[1], jnp.int32))
    pooled[1:2] = pooled[1:2] / wide(jnp.full((1, 1), lens[0], jnp.int32))


def forward_call(lens, x, vec, wa, wi, wo):
    bf, f32 = jnp.bfloat16, jnp.float32
    sds = jax.ShapeDtypeStruct
    outs = [sds((T, 768), bf)] * 3 + [sds((12, S, S), bf), sds((12, Q, Q), bf)] + [sds((768, T), bf)] * 4 + [
        sds((3072, T), bf), sds((T, 3072), bf), sds((T, 768), f32), sds((T, 1), f32), sds((T, 768), f32), sds((T, 1), f32), sds((2, 768), f32)]
    return pl.pallas_call(
        forward_kernel,
        out_shape=outs,
        in_specs=[pl.BlockSpec(memory_space=pltpu.SMEM), VM, VM, ANY, ANY, ANY],
        out_specs=[VM] * len(outs),
        scratch_shapes=[
            pltpu.VMEM((4, 768, 768), bf), pltpu.VMEM((768, 3072), bf), pltpu.VMEM((3072, 768), bf),
            pltpu.VMEM((T, 768), bf), pltpu.VMEM((T, 768), bf), pltpu.VMEM((T, 3072), bf), pltpu.SemaphoreType.DMA((3,))],
        compiler_params=pltpu.CompilerParams(vmem_limit_bytes=60 << 20),
        name="layer_forward",
    )(lens, x, vec, wa, wi, wo)


def backward_kernel(lens, d_pool, vec, a_hbm, i_hbm, o_hbm, q, k, v, prob_hbm, prob_q, x_t, q_t, ctx_t, norm_t, act_t, slope, y1, r1, y2, r2,
                    d_x, d_vec, ga, gi, go,
                    wa, wi, wo, prob, stage, d_second, d_low, d_inner, d_ctx, d_ctx_t, dq, dk, dv, t_k, t_v, ds_buf, sem, gsem):
    loads = [pltpu.make_async_copy(o_hbm, wo, sem.at[0]), pltpu.make_async_copy(i_hbm, wi, sem.at[1]),
             pltpu.make_async_copy(a_hbm, wa, sem.at[2]), pltpu.make_async_copy(prob_hbm, prob, sem.at[3])]
    for load in loads:
        load.start()
    d_vec[...] = jnp.zeros_like(d_vec)

    def gain(row):
        return vec[row : row + 1, :768]

    def tally(row, value):
        d_vec[row : row + 1, :768] += jnp.sum(value, axis=0, keepdims=True)

    written = []

    def emit(value, target):
        i = len(written)
        if i >= 2:
            written[i - 2].wait()
        stage[i % 2] = low(value)
        copy = pltpu.make_async_copy(stage.at[i % 2], target, gsem.at[i % 2])
        copy.start()
        written.append(copy)

    len_p, len_q = lens[0], lens[1]
    pool_q = d_pool[0:1] / wide(jnp.full((1, 1), len_q, jnp.int32))
    pool_p = d_pool[1:2] / wide(jnp.full((1, 1), len_p, jnp.int32))

    @pl.loop(0, 3)
    def _(n):
        rows = block(n, 192)
        at = lax.broadcasted_iota(jnp.int32, (192, 1), 0) + n * 192
        d_rows = jnp.where(at < S, jnp.where(at < len_p, pool_p, 0.0), jnp.where(at - S < len_q, pool_q, 0.0))
        y = y2[rows]
        tally(6, d_rows * y)
        tally(7, d_rows)
        g = d_rows * gain(6)
        d = (g - jnp.mean(g, axis=1, keepdims=True) - y * jnp.mean(g * y, axis=1, keepdims=True)) * r2[rows]
        d_second[rows] = d
        d_low[rows] = low(d)
        tally(3, wide(low(d)))

    for n in range(4):
        emit(dot(act_t[n * 768 : (n + 1) * 768], d_low[...]), go.at[pl.ds(n * 768, 768)])
    loads[0].wait()

    @pl.loop(0, 12)
    def _(n):
        cols = block(n, 256)
        d = low(dot_nt(d_low[...], wo[cols]) * wide(slope[:, cols]))
        d_inner[:, cols] = d
        d_vec[8:9, cols] = jnp.sum(wide(d), axis=0, keepdims=True)

    for n in range(4):
        cols = slice(n * 768, (n + 1) * 768)
        emit(dot(norm_t[...], d_inner[:, cols]), gi.at[:, pl.ds(n * 768, 768)])
    loads[1].wait()

    @pl.loop(0, 3)
    def _(n):
        rows = block(n, 192)
        d_normed = d_second[rows] + dot_nt(d_inner[rows], wi[...])
        y = y1[rows]
        tally(4, d_normed * y)
        tally(5, d_normed)
        g = d_normed * gain(4)
        d = (g - jnp.mean(g, axis=1, keepdims=True) - y * jnp.mean(g * y, axis=1, keepdims=True)) * r1[rows]
        d_second[rows] = d
        d_low[rows] = low(d)
        tally(2, wide(low(d)))

    emit(dot(ctx_t[...], d_low[...]), ga.at[3])
    loads[2].wait()

    @pl.loop(0, 3)
    def _(n):
        rows = block(n, 192)
        d_ctx[rows] = low(dot_nt(d_low[rows], wa[3]))
    d_ctx_t[...] = d_ctx[...].T
    loads[3].wait()

    @pl.loop(0, 6)
    def _(j):
        cols = block(j, 128)
        for (start, size, rb), probs in zip(SPANS, (prob, prob_q)):
            rows = slice(start, start + size)
            kp, vp = k[rows, cols], v[rows, cols]
            dq_parts = [None] * (size // rb)
            for h in range(2):
                mask = head_mask(h)
                for r in range(0, size, rb):
                    d_p = dot_nt(d_ctx[start + r : start + r + rb, cols] * mask, vp)
                    p = wide(probs[2 * j + h, r : r + rb])
                    ds = low(p * (d_p - jnp.sum(p * d_p, axis=1, keepdims=True)))
                    ds_buf[h, r : r + rb, :size] = ds
                    part = dot(ds, kp * mask)
                    i = r // rb
                    dq_parts[i] = part if dq_parts[i] is None else dq_parts[i] + part
                head = block(2 * j + h, 64)
                t_v[head, rows] = low(dot(d_ctx_t[head, rows], probs[2 * j + h]))
                t_k[head, rows] = low(dot(q_t[head, rows], ds_buf[h, :size, :size]) * 0.125)
            for i, part in enumerate(dq_parts):
                dq[start + i * rb : start + (i + 1) * rb, cols] = low(part * 0.125)
    dk[...] = t_k[...].T
    dv[...] = t_v[...].T
    for n, d in enumerate((dq, dk, dv)):
        emit(dot(x_t[...], d[...]), ga.at[n])
    tally(0, wide(dq[...]))
    tally(1, wide(dv[...]))

    @pl.loop(0, 3)
    def _(n):
        rows = block(n, 192)
        d_x[rows] = d_second[rows] + dot_nt(dq[rows], wa[0]) + dot_nt(dk[rows], wa[1]) + dot_nt(dv[rows], wa[2])
    for copy in written[-2:]:
        copy.wait()


def backward_call(lens, d_pool, vec, wa, wi, wo, saved):
    bf, f32 = jnp.bfloat16, jnp.float32
    sds = jax.ShapeDtypeStruct
    outs = [sds((T, 768), f32), sds((16, 3072), f32), sds((4, 768, 768), bf), sds((768, 3072), bf), sds((3072, 768), bf)]
    specs = [VM] * 15
    specs[3] = ANY
    return pl.pallas_call(
        backward_kernel,
        out_shape=outs,
        in_specs=[pl.BlockSpec(memory_space=pltpu.SMEM), VM, VM, ANY, ANY, ANY] + specs,
        out_specs=[VM, VM, ANY, ANY, ANY],
        scratch_shapes=[
            pltpu.VMEM((4, 768, 768), bf), pltpu.VMEM((768, 3072), bf), pltpu.VMEM((3072, 768), bf),
            pltpu.VMEM((12, S, S), bf), pltpu.VMEM((2, 768, 768), bf), pltpu.VMEM((T, 768), f32), pltpu.VMEM((T, 768), bf),
            pltpu.VMEM((T, 3072), bf), pltpu.VMEM((T, 768), bf), pltpu.VMEM((768, T), bf)]
            + [pltpu.VMEM((T, 768), bf)] * 3 + [pltpu.VMEM((768, T), bf)] * 2 + [pltpu.VMEM((2, S, S), bf),
            pltpu.SemaphoreType.DMA((4,)), pltpu.SemaphoreType.DMA((2,))],
        compiler_params=pltpu.CompilerParams(vmem_limit_bytes=62 << 20),
        name="layer_backward",
    )(lens, d_pool, vec, wa, wi, wo, *saved)


def loss_kernel(pooled, targets, seq, d_pool, loss, rows, ssem, rsem):
    pairs = targets.shape[0]
    me = lax.axis_index("dp") * 2 + lax.axis_index("tower")

    def device(at):
        return {"dp": at // 2, "tower": lax.rem(at, 2)}

    sem = pltpu.get_barrier_semaphore()

    @pl.loop(1, pairs)
    def _(k):
        pl.semaphore_signal(sem, inc=1, device_id=device(lax.rem(me + k, pairs)), device_id_type=MESH)
    mine = pooled[...]
    root = jnp.sqrt(jnp.sum(mine * mine, axis=1, keepdims=True) + 1e-6)
    unit = mine / root
    rows[me] = unit
    pl.semaphore_wait(sem, pairs - 1)

    @pl.loop(1, pairs)
    def _(k):
        remote(rows.at[me], rows.at[me], ssem, rsem, device(lax.rem(me + k, pairs))).start()
    rest = rows.at[pl.ds(0, pairs - 1)]
    remote(rest, rest, ssem, rsem, device(me)).wait_recv()
    remote(rest, rest, ssem, rsem, device(me)).wait_send()
    exact = lax.Precision.HIGHEST
    qs, ps = rows[:, 0, :], rows[:, 1, :]
    logits = lax.dot_general(qs, ps, (((1,), (1,)), ((), ())), precision=exact, preferred_element_type=jnp.float32) / 0.01
    hit = targets[...] == lax.broadcasted_iota(jnp.int32, (pairs, pairs), 1)
    top = jnp.max(logits, axis=1, keepdims=True)
    lse = jnp.log(jnp.sum(jnp.exp(logits - top), axis=1, keepdims=True)) + top
    picked = jnp.sum(jnp.where(hit, logits, 0.0), axis=1, keepdims=True)
    loss[...] = jnp.broadcast_to(jnp.sum(lse - picked, axis=0, keepdims=True) / pairs, loss.shape)
    d_logits = seq * (jnp.exp(logits - lse) - jnp.where(hit, 1.0, 0.0))
    d_q = jnp.dot(d_logits, ps, precision=exact, preferred_element_type=jnp.float32) / 0.01
    d_p = lax.dot_general(d_logits, qs, (((0,), (0,)), ((), ())), precision=exact, preferred_element_type=jnp.float32) / 0.01
    own = lax.broadcasted_iota(jnp.int32, (pairs, 1), 0) == me
    for row, d in enumerate((d_q, d_p)):
        d_unit = jnp.sum(jnp.where(own, d, 0.0), axis=0, keepdims=True)
        u = unit[row : row + 1]
        d_pool[row : row + 1] = (d_unit - u * jnp.sum(u * d_unit, axis=1, keepdims=True)) / root[row : row + 1]


def loss_call(pooled, targets, seq, cid=2):
    pairs = targets.shape[0]
    return pl.pallas_call(
        lambda *refs: loss_kernel(refs[0], refs[1], float(seq), *refs[2:]),
        out_shape=(jax.ShapeDtypeStruct((2, 768), jnp.float32), jax.ShapeDtypeStruct((8, 128), jnp.float32)),
        in_specs=[VM] * 2,
        out_specs=[VM] * 2,
        scratch_shapes=[pltpu.VMEM((pairs, 2, 768), jnp.float32), pltpu.SemaphoreType.DMA, pltpu.SemaphoreType.DMA],
        compiler_params=pltpu.CompilerParams(collective_id=cid, has_side_effects=True),
        name="pair_loss",
    )(pooled, targets)


CUT = Cut(1)


def group_rows(x, groups):
    if groups is None:
        return x
    return lax.all_gather(x, "dp", axis=0, tiled=True, axis_index_groups=groups)


def per_device(
    query_tokens, passage_tokens, lengths, positives,
    query_weight, key_weight, value_weight, output_weight, inner_weight, outer_weight,
    query_bias, value_bias, output_bias, inner_bias, outer_bias,
    first_gain, first_shift, second_gain, second_shift,
):
    inner = lax.axis_size("dp") // 16
    groups = None if inner == 1 else [[h * inner + i for i in range(inner)] for h in range(16)]
    tower = lax.axis_index("tower")
    seq = passage_tokens.shape[1]

    def fetch(w):
        return group_rows(w, groups)

    wa = jnp.stack([fetch(w) for w in (query_weight, key_weight, value_weight, output_weight)])
    narrow = [fetch(w) for w in (query_bias, value_bias, output_bias, outer_bias, first_gain, first_shift, second_gain, second_shift)]
    vec = jnp.stack([jnp.pad(w, (0, 256 - w.shape[0])) for w in narrow + [fetch(inner_bias)]])
    vec = jnp.pad(vec, ((0, 7), (0, 0)))
    lens = jnp.pad(lengths, ((0, 7), (0, 126)))
    gv, ga, gi, go, gl = gather_all(inner, CUT, vec, wa, fetch(inner_weight), fetch(outer_weight), lens)
    full = jnp.pad(jnp.swapaxes(gv[:, :8, :48], 0, 1).reshape(8, 768), ((0, 0), (0, 2304)))
    full = jnp.pad(jnp.concatenate([full, gv[:, 8, :192].reshape(1, 3072)]), ((0, 7), (0, 0))).astype(jnp.float32)
    pair = lax.dynamic_index_in_dim(gl[:, 0, :2], tower, 1, keepdims=False)
    own = jnp.stack([pair[1], pair[0]])
    x = jnp.concatenate([
        lax.dynamic_index_in_dim(passage_tokens, tower, 0, keepdims=False),
        lax.dynamic_index_in_dim(query_tokens, tower, 0, keepdims=False),
    ])
    *saved, pooled = forward_call(own, x, full, ga, gi, go)
    d_pool, loss = loss_call(pooled, positives[:, None], seq)
    d_x, d_vec, da, di, do = backward_call(own, d_pool, full, ga, gi, go, saved)
    pv = jnp.swapaxes(d_vec[:8, :768].reshape(8, 16, 48), 0, 1)
    pv = jnp.pad(pv, ((0, 0), (0, 0), (0, 208)))
    pi = jnp.pad(d_vec[8].reshape(16, 1, 192), ((0, 0), (0, 7), (0, 64)))
    rv, ra, ri, ro, query_grads, passage_grads = scatter_all(inner, CUT, jnp.concatenate([pv, pi], axis=1), da, di, do, d_x)

    def finish(x):
        if groups is None:
            return x
        return lax.psum_scatter(x, "dp", scatter_dimension=0, tiled=True, axis_index_groups=groups)

    grads = [finish(ra[i]) for i in range(4)] + [finish(ri), finish(ro)]
    flat = [finish(rv[i, :48]) for i in range(8)] + [finish(rv[8, :192])]
    grads += [flat[0], flat[1], flat[2], flat[8], flat[3], flat[4], flat[5], flat[6], flat[7]]
    return (loss[0, 0], query_grads, passage_grads) + tuple(grads)


def solution(mesh):
    rows3, rows2, rows1 = P("dp", None, None), P("dp", None), P("dp")
    return jax.shard_map(
        per_device,
        mesh=mesh,
        in_specs=(rows3, rows3, P("tower", "dp"), P()) + (rows2,) * 6 + (rows1,) * 9,
        out_specs=(P(), rows3, rows3) + (rows2,) * 6 + (rows1,) * 9,
        check_vma=False,
    )
```

time: 2690 us -> 314 us (0.12)
  waiting for transfers between devices: 2100 us -> 0 us
  Pallas kernels: 0 us -> 279 us
  blocking collectives: 198 us -> 0 us
  matrix products: 130 us -> 0 us
  starting transfers between devices: 68.3 us -> 0 us
  other arithmetic: 74 us -> 6.03 us
  local copies, waits for them, and re-layouts: 62.8 us -> 28 us
  loops' own time: 33.2 us -> 0 us
    reduce_scatter x12 -> x0, waiting for transfers between devices: 1690 us -> none  [the longest x2 350 us: reduce_grads(): lax.psum_scatter(grads[5], 'dp', scatter_dimension=0, tiled=True)]
    all_gather x6 -> x0, waiting for transfers between devices: 302 us -> none  [the longest x1 82 us: fetch(): lax.all_gather(shards[4], 'dp', axis=0, tiled=True)]
    pallas_call x0 -> x5, Pallas kernels: none -> 279 us  [the longest x1 88.9 us: scatter_all(): pl.pallas_call(functools.partial(scatter_kernel, inner, cut), out_shape=(...]
    dot_general x63 -> x0, matrix products: 125 us -> none  [the longest x22 47.1 us: linear_product(): return jnp.dot(left, right, preferred_element_type=jnp.float32)]
    unnamed x21 -> x0, waiting for transfers between devices: 105 us -> none
    unnamed x1 -> x0, blocking collectives: 79 us -> none
    psum x2 -> x0, blocking collectives: 78.4 us -> none  [the longest x1 75.9 us: per_device(): loss_value = lax.psum(partial_loss, 'dp') / pair_count]
    ppermute x1 -> x0, starting transfers between devices: 67.5 us -> none  [swapped(): lax.ppermute(shard, axis, [(i, i ^ 1 << apart) for i in range(lax.axis_si...]
  transfers between devices with their start and end apart: 21 -> 0, of which waited for: 19 -> 0; matrix products, arithmetic and copies ran while one was open for 5% -> 0% of each run, Pallas kernels for 0% -> 0%
where the time goes in v1:
time: 314 us
  Pallas kernels  279 us (89%)
  local copies, waits for them, and re-layouts  28 us (9%)
  other arithmetic  6.03 us (2%)
    pallas_call x1, Pallas kernels, scatter_all(): pl.pallas_call(functools.partial(scatter_kernel, inner, cut), out_shape=(...  88.9 us
    pallas_call x1, Pallas kernels, gather_all(): pl.pallas_call(functools.partial(gather_kernel, inner, cut), out_shape=(j...  86.1 us
    pallas_call x1, Pallas kernels, backward_call(): pl.pallas_call(backward_kernel, out_shape=outs, in_specs=[pl.BlockSpec(me...  53.2 us
    pallas_call x1, Pallas kernels, forward_call(): pl.pallas_call(forward_kernel, out_shape=outs, in_specs=[pl.BlockSpec(mem...  40.1 us
    pallas_call x1, Pallas kernels, loss_call(): pl.pallas_call(lambda *refs: loss_kernel(refs[0], refs[1], float(seq), *r...  10.5 us
    unnamed x14, local copies, waits for them, and re-layouts  7.39 us

profile of v1, /device:TPU:0, one launch (start us, length us, event | category | flops | bytes accessed | tf_op | source)
XLA Modules:
  0.0 313.5 jit_solution(3378553016530787402)
XLA Ops:
  0.7 0.0 copy-start
  0.7 0.8 pad.53
  1.5 0.7 pad.54
  2.1 0.7 pad.55
  2.8 0.7 pad.56
  3.5 0.7 pad.57
  4.1 0.7 pad.58
  4.8 0.7 pad.59
  5.5 0.7 pad.60
  6.1 0.7 pad.61
  6.8 0.6 pad.62.v_in
  7.4 1.7 pad_maximum_fusion.1.a_in
  9.2 1.3 pad.63.len_in
  10.4 86.1 %gather_weights.1 = (bf16[16,16,256]{2,1,0:T(8,128)(2,1)}, bf16[4,768,768]{2,1,0:T(8,128)(2,1)}, bf16[768,3072]{1,0:T(8,128)(2,1)}, bf16[3072,768]{1,0:T(8,128)(2,1)}, s32[2,8,128]{2,1,0:T(8,128)}) custom-call(bf16[16,256]{1,0:T(8,128)(2,1)} %pad.62.v_in, bf16[4,48,768]{2,1,0:T(8,128)(2,1)} %pad_maximum_fusion.1.a_in, bf16[48,3072]{1,0:T(8,128)(2,1)} %i_in.1, ...), custom_call_target="tpu_custom_call" | custom-call | tf_op jit(solution)/shard_map/gather_weights/pallas_call | solution.py:204
  96.6 0.7 slice.69
  97.3 0.6 constant_dynamic-slice_fusion
  97.9 1.9 pad_add_fusion.lens
  99.7 0.9 dynamic-slice_bitcast_fusion.1
  100.6 0.0 copy-done
  100.6 0.1 dynamic-slice_bitcast_fusion
  100.7 1.0 pad_maximum_fusion.x
  101.7 0.8 slice_bitcast_fusion.4
  102.5 0.1 reshape.46
  102.6 0.9 slice_reduce_fusion
  103.5 0.1 reshape_squeeze.6
  103.6 0.7 pad_convert_fusion.vec
  104.3 40.1 %layer_forward.1 = (bf16[576,768]{1,0:T(8,128)(2,1)}, bf16[576,768]{1,0:T(8,128)(2,1)}, bf16[576,768]{1,0:T(8,128)(2,1)}, bf16[12,512,512]{2,1,0:T(8,128)(2,1)},...) custom-call(s32[2]{0:T(128)} %pad_add_fusion.lens, ...), custom_call_target="tpu_custom_call" | custom-call | tf_op jit(solution)/shard_map/layer_forward/pallas_call | solution.py:508
  144.4 0.0 copy-done.4
  144.4 0.7 copy.40.refs_1_
  145.1 10.5 %pair_loss.1 = (f32[2,768]{1,0:T(2,128)}, f32[8,128]{1,0:T(8,128)}) custom-call(f32[2,768]{1,0:T(2,128)} %get-tuple-element.57.refs_0_, s32[32,1]{1,0:T(8,128)} %copy.40.refs_1_), custom_call_target="tpu_custom_call" | custom-call | tf_op jit(solution)/shard_map/pair_loss/pallas_call | solution.py:707
  155.6 1.2 slice.76
  156.8 53.2 %layer_backward.1 = (f32[576,768]{1,0:T(8,128)}, f32[16,3072]{1,0:T(8,128)}, bf16[4,768,768]{2,1,0:T(8,128)(2,1)}, bf16[768,3072]{1,0:T(8,128)(2,1)}, bf16[3072,768]{1,0:T(8,128)(2,1)}) custom-call(s32[2]{0:T(128)} %pad_add_fusion.lens, f32[2,768]{1,0:T(2,128)} %get-tuple-element.59.d_pool, f32[16,3072]{1,0:T(8,128)} %pad_convert_fusion.vec, ...), custom_call_target="tpu_custom_call" | custom-call | tf_op jit(solution)/shard_map/layer_backward/pallas_call | solution.py:647
  209.9 0.9 slice_reduce_fusion.1
  210.9 0.1 reshape_squeeze.7
  211.0 0.7 slice.77
  211.7 0.1 reshape.47
  211.8 0.7 select_maximum_fusion.v_in
  212.6 88.9 %scatter_grads.1 = (f32[16,256]{1,0:T(8,128)}, f32[4,48,768]{2,1,0:T(8,128)}, f32[48,3072]{1,0:T(8,128)}, f32[192,768]{1,0:T(8,128)}, f32[2,64,768]{2,1,0:T(8,128)}, /*index=5*/f32[2,512,768]{2,1,0:T(8,128)}) custom-call(f32[16,16,256]{2,1,0:T(8,128)} %select_maximum_fusion.v_in, bf16[4,768,768]{2,1,0:T(8,128)(2,1)} %get-tuple-element.76.a_in, ...), custom_call_target="tpu_custom_call" | custom-call | tf_op jit(solution)/shard_map/scatter_grads/pallas_call | solution.py:366
  301.4 1.9 slice_bitcast_fusion
  303.4 1.5 slice_bitcast_fusion.5
  304.9 1.3 slice.86
  306.2 1.9 copy.48
  308.1 3.9 %copy.49 = f32[2,512,768]{2,1,0:T(8,128)} copy(f32[2,512,768]{2,1,0:T(8,128)} %get-tuple-element.120) | data formatting | bytes 6291456
  311.9 0.0 copy-done.3
  311.9 0.8 copy.50
  312.7 0.0 copy-done.2
  312.7 0.8 copy.51
  313.5 0.0 copy-done.1
  (17 shorter events, 0.2 us)
Async XLA Ops:
  0.7 100.0 %copy-start = (bf16[2,512,768]{2,1,0:T(8,128)(2,1)S(1)}, bf16[2,512,768]{2,1,0:T(8,128)(2,1)}, u32[]{:S(2)}) copy-start(bf16[2,512,768]{2,1,0:T(8,128)(2,1)} %param.20) | copy-start | bytes 4718596
  104.3 40.1 %copy-start.4 = (s32[32]{0:T(128)S(1)}, s32[32]{0:T(128)}, u32[]{:S(2)}) copy-start(s32[32]{0:T(128)} %param.22) | copy-start | bytes 388
  306.2 7.4 %copy-start.1 = (bf16[2,512,768]{2,1,0:T(8,128)(2,1)S(1)}, bf16[2,512,768]{2,1,0:T(8,128)(2,1)}, u32[]{:S(2)}) copy-start(bf16[2,512,768]{2,1,0:T(8,128)(2,1)} %param.20) | copy-start | bytes 4718596
  308.1 3.9 %copy-start.3 = (f32[48,3072]{1,0:T(8,128)S(1)}, f32[48,3072]{1,0:T(8,128)}, u32[]{:S(2)}) copy-start(f32[48,3072]{1,0:T(8,128)} %get-tuple-element.125) | copy-start | bytes 1769476
  308.1 4.7 %copy-start.2 = (f32[192,768]{1,0:T(8,128)S(1)}, f32[192,768]{1,0:T(8,128)}, u32[]{:S(2)}) copy-start(f32[192,768]{1,0:T(8,128)} %get-tuple-element.126) | copy-start | bytes 1769476

commit v2 on v1

--- a/solution.py
+++ b/solution.py
@@ -223,169 +223,6 @@
     )(vec, wa, wi, wo, lens)
 
 
-def scatter_kernel(inner, cut, v_in, a_in, i_in, o_in, x_in, v_out, a_out, i_out, o_out, q_out, p_out, *scr):
-    p = Place(inner)
-    c = p.c
-    groups = cut.count + 1
-    bufs = [scr[4 * i : 4 * i + 4] for i in range(5)]
-    ssem, rsem, lsem, xsem = scr[20:24]
-    ins = (a_in, i_in, o_in)
-    outs = (a_out, i_out, o_out)
-
-    def buf(level, t):
-        if t == 0:
-            return bufs[level][0]
-        kind, n = cut.kind(t - 1)
-        return bufs[level][1 + kind].at[n]
-
-    def part(t, s, which):
-        if t == 0:
-            return v_in.at[s, :, pl.ds(pl.multiple_of(which * 128, 128), 128)]
-        return cut.whole(ins, t - 1, s, which)
-
-    def result(t, which):
-        if t == 0:
-            return v_out.at[:, pl.ds(pl.multiple_of(which * 128, 128), 128)]
-        return cut.shard(outs, t - 1, which)
-
-    order = tuple(range(groups - 1, -1, -1))
-    for t in order:
-        @pl.loop(0, 16)
-        def _(s):
-            pltpu.make_async_copy(part(t, s, c), buf(0, t).at[s], lsem.at[t]).start()
-
-    p_rows = x_in.at[pl.ds(0, p_out.shape[1])]
-    q_rows = x_in.at[pl.ds(p_out.shape[1], q_out.shape[1])]
-    mine = [pltpu.make_async_copy(p_rows, p_out.at[c], xsem.at[0]), pltpu.make_async_copy(q_rows, q_out.at[c], xsem.at[1])]
-    for copy in mine:
-        copy.start()
-    p.barrier()
-    theirs = [remote(p_rows, p_out.at[c], xsem.at[2], xsem.at[3], p.sib()), remote(q_rows, q_out.at[c], xsem.at[4], xsem.at[5], p.sib())]
-
-    def share(t):
-        for sq in (p.q12, p.q1, p.q2, p.quad):
-            @pl.loop(0, 4)
-            def _(z):
-                s = z * 4 + sq
-                remote(part(t, s, 1 - c), buf(1, t).at[s], ssem.at[t, s], rsem.at[t, s], p.sib()).start()
-
-    def add(t, s, other):
-        acc = buf(0, t)
-        acc[s] = (acc[s].astype(jnp.float32) + other.astype(jnp.float32)).astype(acc.dtype)
-
-    def recv(t, k, ref):
-        remote(ref, ref, ssem.at[t, k], rsem.at[t, k], p.sib()).wait_recv()
-
-    def stage0(t):
-        acc, r0, r1 = buf(0, t), buf(1, t), buf(2, t)
-        pltpu.make_async_copy(acc, acc, lsem.at[t]).wait()
-        for j, q in enumerate((p.q2, p.q12)):
-            @pl.loop(0, 4)
-            def _(z):
-                s = z * 4 + q
-                recv(t, s, r0.at[s])
-                add(t, s, r0[s])
-                k = 16 + z * 2 + j
-                remote(acc.at[s], r1.at[z * 2 + j], ssem.at[t, k], rsem.at[t, k], p.n2()).start()
-        for q in (p.q1, p.quad):
-            @pl.loop(0, 4)
-            def _(z):
-                s = z * 4 + q
-                recv(t, s, r0.at[s])
-                add(t, s, r0[s])
-
-    def stage1(t):
-        acc, r1, r2 = buf(0, t), buf(2, t), buf(3, t)
-        @pl.loop(0, 4)
-        def _(z):
-            s = z * 4 + p.q1
-            recv(t, 17 + z * 2, r1.at[z * 2 + 1])
-            add(t, s, r1[z * 2 + 1])
-            remote(acc.at[s], r2.at[z], ssem.at[t, 24 + z], rsem.at[t, 24 + z], p.n1()).start()
-        @pl.loop(0, 4)
-        def _(z):
-            s = z * 4 + p.quad
-            recv(t, 16 + z * 2, r1.at[z * 2])
-            add(t, s, r1[z * 2])
-
-    def stage2(t):
-        acc, r2, r3 = buf(0, t), buf(3, t), buf(4, t)
-        for k in range(1, 4):
-            z = p.ring(k)
-            s = z * 4 + p.quad
-            recv(t, 24 + z, r2.at[z])
-            add(t, s, r2[z])
-            remote(acc.at[s], r3.at[k], ssem.at[t, 28 + k], rsem.at[t, 28 + k], p.up(k)).start()
-        recv(t, 24 + p.z, r2.at[p.z])
-
-    def stage3(t):
-        acc, r2, r3 = buf(0, t), buf(3, t), buf(4, t)
-        total = acc[p.me].astype(jnp.float32) + r2[p.z].astype(jnp.float32)
-        for k in range(1, 4):
-            recv(t, 28 + k, r3.at[k])
-            total = total + r3[k].astype(jnp.float32)
-        view = result(t, c)
-        view[...] = total
-        remote(view, view, ssem.at[t, 28], rsem.at[t, 28], p.sib()).start()
-
-    ahead = AHEAD
-    for t in order[:ahead]:
-        share(t)
-    for step in range(groups + 3):
-        if step + ahead < groups:
-            share(order[step + ahead])
-        for lag, stage in enumerate((stage0, stage1, stage2, stage3)):
-            if 0 <= step - lag < groups:
-                stage(order[step - lag])
-    for copy in theirs:
-        copy.start()
-    for copy in theirs:
-        copy.wait_send()
-    remote(p_rows, p_out.at[1 - c], xsem.at[2], xsem.at[3], p.sib()).wait_recv()
-    remote(q_rows, q_out.at[1 - c], xsem.at[4], xsem.at[5], p.sib()).wait_recv()
-    for copy in mine:
-        copy.wait()
-    for t in order:
-        recv(t, 28, result(t, 1 - c))
-        acc = buf(0, t)
-        @pl.loop(0, 28)
-        def _(k):
-            remote(acc.at[0], acc.at[0], ssem.at[t, k], rsem.at[t, k], p.sib()).wait_send()
-        for k in range(1, 4):
-            remote(acc.at[0], acc.at[0], ssem.at[t, 28 + k], rsem.at[t, 28 + k], p.sib()).wait_send()
-        remote(result(t, c), result(t, c), ssem.at[t, 28], rsem.at[t, 28], p.sib()).wait_send()
-
-
-def scatter_all(inner, cut, vec, ga, gi, go, dx, cid=1):
-    f32, bf = jnp.float32, jnp.bfloat16
-    groups = cut.count + 1
-    scratch = []
-    for count in (16, 16, 8, 4, 4):
-        scratch.append(pltpu.VMEM((count, 16, 128), f32))
-        scratch += [pltpu.VMEM((cut.each, count) + cut.shape(kind), bf) for kind in range(3)]
-    return pl.pallas_call(
-        functools.partial(scatter_kernel, inner, cut),
-        out_shape=(
-            jax.ShapeDtypeStruct((16, 256), f32),
-            jax.ShapeDtypeStruct((4, 48, 768), f32),
-            jax.ShapeDtypeStruct((48, 3072), f32),
-            jax.ShapeDtypeStruct((192, 768), f32),
-            jax.ShapeDtypeStruct((2, Q, 768), f32),
-            jax.ShapeDtypeStruct((2, S, 768), f32),
-        ),
-        in_specs=[ANY] * 5,
-        out_specs=[VM] * 4 + [ANY] * 2,
-        scratch_shapes=scratch + [
-            pltpu.SemaphoreType.DMA((groups, 32)),
-            pltpu.SemaphoreType.DMA((groups, 32)),
-            pltpu.SemaphoreType.DMA((groups,)),
-            pltpu.SemaphoreType.DMA((6,)),
-        ],
-        compiler_params=pltpu.CompilerParams(collective_id=cid, has_side_effects=True, vmem_limit_bytes=56 << 20),
-        name="scatter_grads",
-    )(vec, ga, gi, go, dx)
-
-
 S, Q = 512, 64
 T = S + Q
 
@@ -478,8 +315,13 @@
         cdf = 0.5 * (1.0 + lax.erf(u * 0.7071067811865476))
         a = low(u * cdf)
         act[:, cols] = a
-        act_t[cols] = a.T
         slope[:, cols] = low(cdf + u * (0.3989422804014327 * jnp.exp(-0.5 * u * u)))
+    for b in range(4):
+        turned = act[:, b * 768 : (b + 1) * 768].T
+        for s in range(4):
+            for n in range(4):
+                row = n * 768 + (b * 4 + s) * 48
+                act_t[row : row + 48] = turned[s * 192 + n * 48 : s * 192 + n * 48 + 48]
     loads[2].wait()
     pooled[...] = jnp.zeros_like(pooled)
 
@@ -518,144 +360,396 @@
     )(lens, x, vec, wa, wi, wo)
 
 
-def backward_kernel(lens, d_pool, vec, a_hbm, i_hbm, o_hbm, q, k, v, prob_hbm, prob_q, x_t, q_t, ctx_t, norm_t, act_t, slope, y1, r1, y2, r2,
-                    d_x, d_vec, ga, gi, go,
-                    wa, wi, wo, prob, stage, d_second, d_low, d_inner, d_ctx, d_ctx_t, dq, dk, dv, t_k, t_v, ds_buf, sem, gsem):
-    loads = [pltpu.make_async_copy(o_hbm, wo, sem.at[0]), pltpu.make_async_copy(i_hbm, wi, sem.at[1]),
-             pltpu.make_async_copy(a_hbm, wa, sem.at[2]), pltpu.make_async_copy(prob_hbm, prob, sem.at[3])]
-    for load in loads:
-        load.start()
+class Scatter:
+    def __init__(self, p, refs, result):
+        self.p = p
+        self.stage, self.r0, self.acc, self.r1, self.r2, self.r3, self.ssem, self.rsem = refs
+        self.result = result
+        self.own = pl.ds(pl.multiple_of(p.c * 384, 128), 384)
+        self.other = pl.ds(pl.multiple_of((1 - p.c) * 384, 128), 384)
+
+    def copy(self, src, dst, e, k, target):
+        return remote(src, dst, self.ssem.at[e, k], self.rsem.at[e, k], target)
+
+    def recv(self, e, k, ref):
+        self.copy(ref, ref, e, k, self.p.sib()).wait_recv()
+
+    def emit(self, e, left, right, extra=None):
+        if e >= 2:
+            self.shared(e - 2).wait_send()
+
+        @pl.loop(0, 3)
+        def _(n):
+            cols = block(n, 256)
+            values = right(cols)
+            self.stage[e % 2, :, :, cols] = low(dot(left(), values)).reshape(16, 48, 256)
+            if extra is not None:
+                extra(cols, values)
+        self.shared(e).start()
+
+    def shared(self, e):
+        return self.copy(self.stage.at[e % 2, :, :, self.other], self.r0.at[e % 4], e, 0, self.p.sib())
+
+    def stage0(self, e):
+        p, acc = self.p, self.acc
+        self.recv(e, 0, self.r0.at[e % 4])
+
+        def add(s):
+            acc[e, s] = self.stage[e % 2, s, :, self.own] + self.r0[e % 4, s]
+
+        for j, q in enumerate((p.q2, p.q12)):
+            @pl.loop(0, 4)
+            def _(z):
+                s = z * 4 + q
+                add(s)
+                self.copy(acc.at[e, s], self.r1.at[e, z * 2 + j], e, 16 + z * 2 + j, p.n2()).start()
+        for q in (p.q1, p.quad):
+            @pl.loop(0, 4)
+            def _(z):
+                add(z * 4 + q)
+
+    def stage1(self, e):
+        p, acc = self.p, self.acc
+
+        @pl.loop(0, 4)
+        def _(z):
+            s = z * 4 + p.q1
+            self.recv(e, 17 + z * 2, self.r1.at[e, z * 2 + 1])
+            acc[e, s] += self.r1[e, z * 2 + 1]
+            self.copy(acc.at[e, s], self.r2.at[e, z], e, 24 + z, p.n1()).start()
+
+        @pl.loop(0, 4)
+        def _(z):
+            self.recv(e, 16 + z * 2, self.r1.at[e, z * 2])
+            acc[e, z * 4 + p.quad] += self.r1[e, z * 2]
+
+    def stage2(self, e):
+        p, acc = self.p, self.acc
+        for k in range(1, 4):
+            z = p.ring(k)
+            s = z * 4 + p.quad
+            self.recv(e, 24 + z, self.r2.at[e, z])
+            acc[e, s] += self.r2[e, z]
+            self.copy(acc.at[e, s], self.r3.at[e, k - 1], e, 28 + k, p.up(k)).start()
+        self.recv(e, 24 + p.z, self.r2.at[e, p.z])
+
+    def stage3(self, e):
+        p = self.p
+        total = wide(self.acc[e, p.me]) + wide(self.r2[e, p.z])
+        for k in range(1, 4):
+            self.recv(e, 28 + k, self.r3.at[e, k - 1])
+            total = total + wide(self.r3[e, k - 1])
+        view = self.result(e, p.c)
+        view[...] = total
+        self.copy(view, view, e, 28, p.sib()).start()
+
+    def finish(self, count):
+        for e in range(count):
+            self.recv(e, 28, self.result(e, 1 - self.p.c))
+            self.copy(self.result(e, self.p.c), self.result(e, self.p.c), e, 28, self.p.sib()).wait_send()
+        for e in range(count - 2, count):
+            self.shared(e).wait_send()
+        one = self.acc.at[0, 0]
+
+        @pl.loop(0, count)
+        def _(e):
+            @pl.loop(16, 28)
+            def _(k):
+                self.copy(one, one, e, k, self.p.sib()).wait_send()
+
+            @pl.loop(29, 32)
+            def _(k):
+                self.copy(one, one, e, k, self.p.sib()).wait_send()
+
+
+def backward_kernel(inner, lens, d_pool, vec, a_hbm, i_hbm, o_hbm, k_hbm, v_hbm, prob_hbm, prob_q_hbm, x_t_hbm, q_t_hbm, ctx_t_hbm, norm_t_hbm,
+                    act_t_hbm, slope_hbm, y1_hbm, r1_hbm, y2_hbm, r2_hbm,
+                    dx_out, dvec_out, g_query, g_key, g_value, g_output, g_inner, g_outer,
+                    wa, wi, act_t, slope, d_inner, y, scale_one, scale_two, d_second, d_low, norm_t, ctx_t, x_t, q_t, k, v, prob, prob_q, ds_buf,
+                    d_vec, v_in, v_out, stage, r0, acc, r1, r2, r3, ssem, rsem, lsem, psem, vsem, xsem):
+    p = Place(inner)
+
+    def load(i, src, dst):
+        return pltpu.make_async_copy(src, dst, lsem.at[i])
+
+    loads = {
+        "y2": load(0, y2_hbm, y), "r2": load(1, r2_hbm, scale_two), "act_t": load(2, act_t_hbm, act_t),
+        "slope": load(7, slope_hbm, slope), "norm_t": load(8, norm_t_hbm, norm_t), "wi": load(9, i_hbm, wi),
+        "y1": load(10, y1_hbm, y), "r1": load(11, r1_hbm, scale_one), "ctx_t": load(12, ctx_t_hbm, ctx_t), "wa": load(13, a_hbm, wa),
+        "k": load(14, k_hbm, k), "v": load(15, v_hbm, v), "q_t": load(16, q_t_hbm, q_t), "x_t": load(17, x_t_hbm, x_t), "prob_q": load(18, prob_q_hbm, prob_q),
+    }
+    for n in range(4):
+        loads["wo%d" % n] = load(3 + n, o_hbm.at[pl.ds(n * 768, 768)], wa.at[n])
+
+    def start(*names):
+        for name in names:
+            loads[name].start()
+
+    def need(*names):
+        for name in names:
+            loads[name].wait()
+
+    def load_prob(j):
+        return pltpu.make_async_copy(prob_hbm.at[pl.ds(j * 2, 2)], prob.at[lax.rem(j, 2)], psem.at[lax.rem(j, 2)])
+
+    start("y2", "r2", "act_t", "wo0", "wo1", "wo2", "wo3", "slope", "norm_t", "wi", "r1", "ctx_t", "k", "v", "q_t", "x_t", "prob_q")
+    load_prob(0).start()
+    load_prob(1).start()
+    p.barrier()
+
+    def result(e, which):
+        cols = pl.ds(pl.multiple_of(which * 384, 128), 384)
+        if e < 4:
+            return g_outer.at[pl.ds(e * 48, 48), cols]
+        if e < 8:
+            return g_inner.at[:, pl.ds(pl.multiple_of((e - 4) * 768 + which * 384, 128), 384)]
+        return (g_output, g_query, g_key, g_value)[e - 8].at[:, cols]
+
+    sc = Scatter(p, (stage, r0, acc, r1, r2, r3, ssem, rsem), result)
     d_vec[...] = jnp.zeros_like(d_vec)
 
     def gain(row):
         return vec[row : row + 1, :768]
 
     def tally(row, value):
-        d_vec[row : row + 1, :768] += jnp.sum(value, axis=0, keepdims=True)
-
-    written = []
-
-    def emit(value, target):
-        i = len(written)
-        if i >= 2:
-            written[i - 2].wait()
-        stage[i % 2] = low(value)
-        copy = pltpu.make_async_copy(stage.at[i % 2], target, gsem.at[i % 2])
-        copy.start()
-        written.append(copy)
+        d_vec[row : row + 1] += jnp.sum(value, axis=0, keepdims=True)
 
     len_p, len_q = lens[0], lens[1]
     pool_q = d_pool[0:1] / wide(jnp.full((1, 1), len_q, jnp.int32))
     pool_p = d_pool[1:2] / wide(jnp.full((1, 1), len_p, jnp.int32))
+
+    def norm_back(d, row, yy, scale, rows):
+        tally(row, d * yy)
+        tally(row + 1, d)
+        g = d * gain(row)
+        d = (g - jnp.mean(g, axis=1, keepdims=True) - yy * jnp.mean(g * yy, axis=1, keepdims=True)) * scale
+        d_second[rows] = d
+        d_low[rows] = low(d)
+        return d
+
+    need("y2", "r2")
 
     @pl.loop(0, 3)
     def _(n):
         rows = block(n, 192)
         at = lax.broadcasted_iota(jnp.int32, (192, 1), 0) + n * 192
         d_rows = jnp.where(at < S, jnp.where(at < len_p, pool_p, 0.0), jnp.where(at - S < len_q, pool_q, 0.0))
-        y = y2[rows]
-        tally(6, d_rows * y)
-        tally(7, d_rows)
-        g = d_rows * gain(6)
-        d = (g - jnp.mean(g, axis=1, keepdims=True) - y * jnp.mean(g * y, axis=1, keepdims=True)) * r2[rows]
-        d_second[rows] = d
-        d_low[rows] = low(d)
+        d = norm_back(d_rows, 6, y[rows], scale_two[rows], rows)
         tally(3, wide(low(d)))
 
-    for n in range(4):
-        emit(dot(act_t[n * 768 : (n + 1) * 768], d_low[...]), go.at[pl.ds(n * 768, 768)])
-    loads[0].wait()
-
-    @pl.loop(0, 12)
-    def _(n):
-        cols = block(n, 256)
-        d = low(dot_nt(d_low[...], wo[cols]) * wide(slope[:, cols]))
-        d_inner[:, cols] = d
-        d_vec[8:9, cols] = jnp.sum(wide(d), axis=0, keepdims=True)
-
-    for n in range(4):
-        cols = slice(n * 768, (n + 1) * 768)
-        emit(dot(norm_t[...], d_inner[:, cols]), gi.at[:, pl.ds(n * 768, 768)])
-    loads[1].wait()
+    start("y1")
+    need("act_t")
+
+    def emit_outer(n):
+        sc.emit(n, lambda: act_t[n * 768 : (n + 1) * 768], lambda cols: d_low[:, cols])
+
+    def emit_inner(n):
+        def bias(cols, values):
+            d_vec[8 + n : 9 + n, cols] = jnp.sum(wide(values), axis=0, keepdims=True)
+        sc.emit(4 + n, lambda: norm_t[...], lambda cols: d_inner[:, pl.ds(pl.multiple_of(n * 768 + cols.start, 256), 256)], bias)
+
+    emit_outer(0)
+    emit_outer(1)
+    sc.stage0(0)
+    emit_outer(2)
+    sc.stage0(1)
+    emit_outer(3)
+    sc.stage0(2)
+    need("wo0", "wo1", "wo2", "wo3", "slope")
+
+    def inner_back(low_n, high_n):
+        @pl.loop(low_n, high_n)
+        def _(n):
+            cols = block(n, 256)
+            d_inner[:, cols] = low(dot_nt(d_low[...], wa[n // 3, block(lax.rem(n, 3), 256)]) * wide(slope[:, cols]))
+
+    inner_back(0, 6)
+    sc.stage0(3)
+    inner_back(6, 12)
+    start("wa")
+    sc.stage1(0)
+    need("norm_t")
+    emit_inner(0)
+    sc.stage1(1)
+    emit_inner(1)
+    sc.stage0(4)
+    sc.stage2(0)
+    emit_inner(2)
+    sc.stage0(5)
+    sc.stage1(2)
+    emit_inner(3)
+    sc.stage0(6)
+    sc.stage2(1)
+    need("wi", "y1", "r1")
 
     @pl.loop(0, 3)
     def _(n):
         rows = block(n, 192)
-        d_normed = d_second[rows] + dot_nt(d_inner[rows], wi[...])
-        y = y1[rows]
-        tally(4, d_normed * y)
-        tally(5, d_normed)
-        g = d_normed * gain(4)
-        d = (g - jnp.mean(g, axis=1, keepdims=True) - y * jnp.mean(g * y, axis=1, keepdims=True)) * r1[rows]
-        d_second[rows] = d
-        d_low[rows] = low(d)
+        d = norm_back(d_second[rows] + dot_nt(d_inner[rows], wi[...]), 4, y[rows], scale_one[rows], rows)
         tally(2, wide(low(d)))
 
-    emit(dot(ctx_t[...], d_low[...]), ga.at[3])
-    loads[2].wait()
+    sc.stage0(7)
+    sc.stage1(3)
+    sc.stage2(2)
+    need("ctx_t", "wa")
+    sc.emit(8, lambda: ctx_t[...], lambda cols: d_low[:, cols])
+
+    def part(i):
+        return pl.ds(i * 768, 768)
+
+    def pair_cols(i, j):
+        return pl.ds(pl.multiple_of(i * 768 + j * 128, 128), 128)
+
+    def head_rows(i, head):
+        return pl.ds(pl.multiple_of(i * 768 + head * 64, 64), 64)
 
     @pl.loop(0, 3)
     def _(n):
         rows = block(n, 192)
-        d_ctx[rows] = low(dot_nt(d_low[rows], wa[3]))
-    d_ctx_t[...] = d_ctx[...].T
-    loads[3].wait()
-
-    @pl.loop(0, 6)
-    def _(j):
-        cols = block(j, 128)
-        for (start, size, rb), probs in zip(SPANS, (prob, prob_q)):
-            rows = slice(start, start + size)
-            kp, vp = k[rows, cols], v[rows, cols]
-            dq_parts = [None] * (size // rb)
-            for h in range(2):
-                mask = head_mask(h)
-                for r in range(0, size, rb):
-                    d_p = dot_nt(d_ctx[start + r : start + r + rb, cols] * mask, vp)
-                    p = wide(probs[2 * j + h, r : r + rb])
-                    ds = low(p * (d_p - jnp.sum(p * d_p, axis=1, keepdims=True)))
-                    ds_buf[h, r : r + rb, :size] = ds
-                    part = dot(ds, kp * mask)
-                    i = r // rb
-                    dq_parts[i] = part if dq_parts[i] is None else dq_parts[i] + part
-                head = block(2 * j + h, 64)
-                t_v[head, rows] = low(dot(d_ctx_t[head, rows], probs[2 * j + h]))
-                t_k[head, rows] = low(dot(q_t[head, rows], ds_buf[h, :size, :size]) * 0.125)
-            for i, part in enumerate(dq_parts):
-                dq[start + i * rb : start + (i + 1) * rb, cols] = low(part * 0.125)
-    dk[...] = t_k[...].T
-    dv[...] = t_v[...].T
-    for n, d in enumerate((dq, dk, dv)):
-        emit(dot(x_t[...], d[...]), ga.at[n])
-    tally(0, wide(dq[...]))
-    tally(1, wide(dv[...]))
+        d_inner[rows, part(3)] = low(dot_nt(d_low[rows], wa[3]))
+    act_t[part(2)] = d_inner[:, part(3)].T
+    need("k", "v", "q_t", "prob_q")
+    sc.stage0(8)
+    sc.stage1(4)
+    sc.stage2(3)
+    sc.stage3(0)
+
+    def attention(low_j, high_j):
+        @pl.loop(low_j, high_j)
+        def _(j):
+            load_prob(j).wait()
+            slot = lax.rem(j, 2)
+            cols = block(j, 128)
+            for start, size, rb in SPANS:
+                rows = slice(start, start + size)
+                kp, vp = k[rows, cols], v[rows, cols]
+                dq_parts = [None] * (size // rb)
+                for h in range(2):
+                    probs = (lambda sl: prob[slot, h, sl]) if size == S else (lambda sl: prob_q[2 * j + h, sl])
+                    mask = head_mask(h)
+                    for r in range(0, size, rb):
+                        d_p = dot_nt(d_inner[start + r : start + r + rb, pair_cols(3, j)] * mask, vp)
+                        w = wide(probs(slice(r, r + rb)))
+                        ds = low(w * (d_p - jnp.sum(w * d_p, axis=1, keepdims=True)))
+                        ds_buf[h, r : r + rb, :size] = ds
+                        piece = dot(ds, kp * mask)
+                        i = r // rb
+                        dq_parts[i] = piece if dq_parts[i] is None else dq_parts[i] + piece
+                    head = 2 * j + h
+                    act_t[head_rows(1, head), rows] = low(dot(act_t[head_rows(2, head), rows], probs(slice(0, size))))
+                    act_t[head_rows(0, head), rows] = low(dot(q_t[head_rows(0, head), rows], ds_buf[h, :size, :size]) * 0.125)
+                for i, piece in enumerate(dq_parts):
+                    d_inner[start + i * rb : start + (i + 1) * rb, pair_cols(0, j)] = low(piece * 0.125)
+
+            @pl.when(j < 4)
+            def _():
+                load_prob(j + 2).start()
+
+    attention(0, 2)
+    sc.stage1(5)
+    sc.stage2(4)
+    sc.stage3(1)
+    attention(2, 4)
+    sc.stage1(6)
+    sc.stage2(5)
+    sc.stage3(2)
+    attention(4, 6)
+    sc.stage1(7)
+    sc.stage2(6)
+    sc.stage3(3)
+    d_inner[:, part(1)] = act_t[part(0)].T
+    d_inner[:, part(2)] = act_t[part(1)].T
+    need("x_t")
+
+    def emit_first(n):
+        row = (0, None, 1)[n]
+
+        def bias(cols, values):
+            d_vec[row : row + 1, cols] = jnp.sum(wide(values), axis=0, keepdims=True)
+        sc.emit(9 + n, lambda: x_t[...], lambda cols: d_inner[:, pl.ds(pl.multiple_of(n * 768 + cols.start, 256), 256)], None if row is None else bias)
+
+    emit_first(0)
+    sc.stage1(8)
+    emit_first(1)
+    sc.stage0(9)
+    emit_first(2)
+
+    def vector(i, src, target):
+        return remote(src, v_in.at[i], vsem.at[0, i], vsem.at[1, i], target)
+
+    def vector_recv(i):
+        vector(i, v_in.at[i], p.sib()).wait_recv()
+        return v_in[i]
+
+    vector(0, d_vec.at[:, sc.other], p.sib()).start()
+    sc.stage0(10)
+    sc.stage2(7)
 
     @pl.loop(0, 3)
     def _(n):
         rows = block(n, 192)
-        d_x[rows] = d_second[rows] + dot_nt(dq[rows], wa[0]) + dot_nt(dk[rows], wa[1]) + dot_nt(dv[rows], wa[2])
-    for copy in written[-2:]:
-        copy.wait()
-
-
-def backward_call(lens, d_pool, vec, wa, wi, wo, saved):
+        d = d_second[rows]
+        for i in range(3):
+            d = d + dot_nt(d_inner[rows, part(i)], wa[i])
+        d_low[rows] = low(d)
+    mine = pltpu.make_async_copy(d_low, dx_out.at[p.c], xsem.at[0])
+    theirs = remote(d_low, dx_out.at[p.c], xsem.at[1], xsem.at[2], p.sib())
+    mine.start()
+    theirs.start()
+    sc.stage0(11)
+    v_out[0] = d_vec[:, sc.own] + vector_recv(0)
+    vector(1, v_out.at[0], p.n2()).start()
+    sc.stage3(4)
+    sc.stage1(9)
+    v_out[1] = v_out[0] + vector_recv(1)
+    vector(2, v_out.at[1], p.n1()).start()
+    sc.stage2(8)
+    sc.stage3(5)
+    sc.stage1(10)
+    v_out[2] = v_out[1] + vector_recv(2)
+    for i in range(1, 4):
+        vector(2 + i, v_out.at[2], p.up(i)).start()
+    sc.stage2(9)
+    sc.stage3(6)
+    sc.stage1(11)
+    sc.stage2(10)
+    sc.stage3(7)
+    dvec_out[:, sc.own] = v_out[2] + vector_recv(3) + vector_recv(4) + vector_recv(5)
+    last = remote(dvec_out.at[:, sc.own], dvec_out.at[:, sc.own], vsem.at[0, 6], vsem.at[1, 6], p.sib())
+    last.start()
+    sc.stage2(11)
+    for e in range(8, 12):
+        sc.stage3(e)
+    mine.wait()
+    theirs.wait_send()
+    remote(dx_out.at[1 - p.c], dx_out.at[1 - p.c], xsem.at[1], xsem.at[2], p.sib()).wait_recv()
+    remote(dvec_out.at[:, sc.other], dvec_out.at[:, sc.other], vsem.at[0, 6], vsem.at[1, 6], p.sib()).wait_recv()
+    last.wait_send()
+    for i in range(6):
+        vector(i, v_in.at[i], p.sib()).wait_send()
+    sc.finish(12)
+
+
+def backward_call(inner, lens, d_pool, vec, wa, wi, wo, saved, cid=1):
     bf, f32 = jnp.bfloat16, jnp.float32
     sds = jax.ShapeDtypeStruct
-    outs = [sds((T, 768), f32), sds((16, 3072), f32), sds((4, 768, 768), bf), sds((768, 3072), bf), sds((3072, 768), bf)]
-    specs = [VM] * 15
-    specs[3] = ANY
+    outs = [sds((2, T, 768), bf), sds((16, 768), f32)] + [sds((48, 768), f32)] * 4 + [sds((48, 3072), f32), sds((192, 768), f32)]
+    vmem = pltpu.VMEM
+    scratch = [
+        vmem((4, 768, 768), bf), vmem((768, 3072), bf), vmem((3072, T), bf), vmem((T, 3072), bf), vmem((T, 3072), bf),
+        vmem((T, 768), f32), vmem((T, 1), f32), vmem((T, 1), f32), vmem((T, 768), f32), vmem((T, 768), bf)]
+    scratch += [vmem((768, T), bf)] * 4 + [vmem((T, 768), bf)] * 2
+    scratch += [vmem((2, 2, S, S), bf), vmem((12, Q, Q), bf), vmem((2, S, S), bf), vmem((16, 768), f32), vmem((6, 16, 384), f32), vmem((3, 16, 384), f32)]
+    scratch += [vmem((2, 16, 48, 768), bf), vmem((4, 16, 48, 384), bf)] + [vmem((12, n, 48, 384), bf) for n in (16, 8, 4, 3)]
+    dma = pltpu.SemaphoreType.DMA
+    scratch += [dma((12, 32)), dma((12, 32)), dma((19,)), dma((2,)), dma((2, 7)), dma((3,))]
     return pl.pallas_call(
-        backward_kernel,
+        functools.partial(backward_kernel, inner),
         out_shape=outs,
-        in_specs=[pl.BlockSpec(memory_space=pltpu.SMEM), VM, VM, ANY, ANY, ANY] + specs,
-        out_specs=[VM, VM, ANY, ANY, ANY],
-        scratch_shapes=[
-            pltpu.VMEM((4, 768, 768), bf), pltpu.VMEM((768, 3072), bf), pltpu.VMEM((3072, 768), bf),
-            pltpu.VMEM((12, S, S), bf), pltpu.VMEM((2, 768, 768), bf), pltpu.VMEM((T, 768), f32), pltpu.VMEM((T, 768), bf),
-            pltpu.VMEM((T, 3072), bf), pltpu.VMEM((T, 768), bf), pltpu.VMEM((768, T), bf)]
-            + [pltpu.VMEM((T, 768), bf)] * 3 + [pltpu.VMEM((768, T), bf)] * 2 + [pltpu.VMEM((2, S, S), bf),
-            pltpu.SemaphoreType.DMA((4,)), pltpu.SemaphoreType.DMA((2,))],
-        compiler_params=pltpu.CompilerParams(vmem_limit_bytes=62 << 20),
+        in_specs=[pl.BlockSpec(memory_space=pltpu.SMEM), VM, VM] + [ANY] * 17,
+        out_specs=[ANY] + [VM] * 7,
+        scratch_shapes=scratch,
+        compiler_params=pltpu.CompilerParams(collective_id=cid, has_side_effects=True, vmem_limit_bytes=63 << 20),
         name="layer_backward",
     )(lens, d_pool, vec, wa, wi, wo, *saved)
 
@@ -733,6 +827,7 @@
     inner = lax.axis_size("dp") // 16
     groups = None if inner == 1 else [[h * inner + i for i in range(inner)] for h in range(16)]
     tower = lax.axis_index("tower")
+    at = lax.axis_index("dp") // inner
     seq = passage_tokens.shape[1]
 
     def fetch(w):
@@ -754,21 +849,19 @@
     ])
     *saved, pooled = forward_call(own, x, full, ga, gi, go)
     d_pool, loss = loss_call(pooled, positives[:, None], seq)
-    d_x, d_vec, da, di, do = backward_call(own, d_pool, full, ga, gi, go, saved)
-    pv = jnp.swapaxes(d_vec[:8, :768].reshape(8, 16, 48), 0, 1)
-    pv = jnp.pad(pv, ((0, 0), (0, 0), (0, 208)))
-    pi = jnp.pad(d_vec[8].reshape(16, 1, 192), ((0, 0), (0, 7), (0, 64)))
-    rv, ra, ri, ro, query_grads, passage_grads = scatter_all(inner, CUT, jnp.concatenate([pv, pi], axis=1), da, di, do, d_x)
+    d_x, d_vec, *grads = backward_call(inner, own, d_pool, full, ga, gi, go, saved[1:])
 
     def finish(x):
         if groups is None:
             return x
         return lax.psum_scatter(x, "dp", scatter_dimension=0, tiled=True, axis_index_groups=groups)
 
-    grads = [finish(ra[i]) for i in range(4)] + [finish(ri), finish(ro)]
-    flat = [finish(rv[i, :48]) for i in range(8)] + [finish(rv[8, :192])]
-    grads += [flat[0], flat[1], flat[2], flat[8], flat[3], flat[4], flat[5], flat[6], flat[7]]
-    return (loss[0, 0], query_grads, passage_grads) + tuple(grads)
+    d_x = d_x.astype(jnp.float32)
+    flat = lax.dynamic_slice_in_dim(d_vec[:8], at * 48, 48, 1)
+    wide_bias = lax.dynamic_slice_in_dim(d_vec[8:12].reshape(3072), at * 192, 192, 0)
+    rows = [finish(flat[i]) for i in range(8)]
+    vectors = [rows[0], rows[1], rows[2], finish(wide_bias)] + rows[3:]
+    return (loss[0, 0], d_x[:, seq:], d_x[:, :seq]) + tuple(finish(g) for g in grads) + tuple(vectors)
 
 
 def solution(mesh):

time: 314 us -> 264 us (0.84)
  Pallas kernels: 279 us -> 234 us
  local copies, waits for them, and re-layouts: 28 us -> 23.8 us
    pallas_call x2 -> x1, Pallas kernels: 142 us -> 96.9 us  [backward_call(): pl.pallas_call(functools.partial(backward_kernel, inner), out_shape=outs,...]
    unnamed x14 -> x26, local copies, waits for them, and re-layouts: 7.39 us -> 4.32 us
    slice x4 -> x5, local copies, waits for them, and re-layouts: 4.11 us -> 6.29 us  [the longest x1 3.41 us: per_device(): d_x[:, :seq]]
where the time goes in v2:
time: 264 us
  Pallas kernels  234 us (89%)
  local copies, waits for them, and re-layouts  23.8 us (9%)
  other arithmetic  5.35 us (2%)
    pallas_call x1, Pallas kernels, backward_call(): pl.pallas_call(functools.partial(backward_kernel, inner), out_shape=outs,...  96.9 us
    pallas_call x1, Pallas kernels, gather_all(): pl.pallas_call(functools.partial(gather_kernel, inner, cut), out_shape=(j...  86.1 us
    pallas_call x1, Pallas kernels, forward_call(): pl.pallas_call(forward_kernel, out_shape=outs, in_specs=[pl.BlockSpec(mem...  40.4 us
    pallas_call x1, Pallas kernels, loss_call(): pl.pallas_call(lambda *refs: loss_kernel(refs[0], refs[1], float(seq), *r...  10.5 us
    pad x9, local copies, waits for them, and re-layouts, per_device(): jnp.pad(w, (0, 256 - w.shape[0]))  6.07 us

profile of v2, /device:TPU:0, one launch (start us, length us, event | category | flops | bytes accessed | tf_op | source)
XLA Modules:
  0.0 263.8 jit_solution(16339519229543680414)
XLA Ops:
  0.7 0.0 copy-start
  0.7 0.0 copy-start.3
  0.7 0.8 pad.45
  1.5 0.7 pad.46
  2.1 0.7 pad.47
  2.8 0.7 pad.48
  3.5 0.7 pad.49
  4.2 0.7 pad.50
  4.8 0.7 pad.51
  5.5 0.7 pad.52
  6.2 0.7 pad.53
  6.9 0.6 pad.54.v_in
  7.5 1.7 pad_maximum_fusion.1.a_in
  9.2 1.3 pad.55.len_in
  10.5 86.1 %gather_weights.1 = (bf16[16,16,256]{2,1,0:T(8,128)(2,1)}, bf16[4,768,768]{2,1,0:T(8,128)(2,1)}, bf16[768,3072]{1,0:T(8,128)(2,1)}, bf16[3072,768]{1,0:T(8,128)(2,1)}, s32[2,8,128]{2,1,0:T(8,128)}) custom-call(bf16[16,256]{1,0:T(8,128)(2,1)} %pad.54.v_in, bf16[4,48,768]{2,1,0:T(8,128)(2,1)} %pad_maximum_fusion.1.a_in, bf16[48,3072]{1,0:T(8,128)(2,1)} %i_in.1, ...), custom_call_target="tpu_custom_call" | custom-call | tf_op jit(solution)/shard_map/gather_weights/pallas_call | solution.py:204
  96.6 0.7 slice.60
  97.3 0.6 constant_dynamic-slice_fusion
  97.9 1.9 pad_add_fusion.lens
  99.8 0.0 copy-done
  99.8 0.0 copy-done.3
  99.8 0.1 dynamic-slice_bitcast_fusion
  99.9 1.0 pad_maximum_fusion.x
  100.9 0.8 slice_bitcast_fusion
  101.6 0.1 reshape.46
  101.7 0.9 slice_reduce_fusion
  102.6 0.1 reshape_squeeze.3
  102.8 0.7 pad_convert_fusion.vec
  103.5 40.4 %layer_forward.1 = (bf16[576,768]{1,0:T(8,128)(2,1)}, bf16[576,768]{1,0:T(8,128)(2,1)}, bf16[576,768]{1,0:T(8,128)(2,1)}, bf16[12,512,512]{2,1,0:T(8,128)(2,1)},...) custom-call(s32[2]{0:T(128)} %pad_add_fusion.lens, ...), custom_call_target="tpu_custom_call" | custom-call | tf_op jit(solution)/shard_map/layer_forward/pallas_call | solution.py:350
  143.8 0.0 copy-done.9
  143.8 0.7 copy.40.refs_1_
  144.5 10.5 %pair_loss.1 = (f32[2,768]{1,0:T(2,128)}, f32[8,128]{1,0:T(8,128)}) custom-call(f32[2,768]{1,0:T(2,128)} %get-tuple-element.53.refs_0_, s32[32,1]{1,0:T(8,128)} %copy.40.refs_1_), custom_call_target="tpu_custom_call" | custom-call | tf_op jit(solution)/shard_map/pair_loss/pallas_call | solution.py:801
  155.0 1.2 slice.67
  156.2 96.9 %layer_backward.1 = (bf16[2,576,768]{2,1,0:T(8,128)(2,1)}, f32[16,768]{1,0:T(8,128)}, f32[48,768]{1,0:T(8,128)}, f32[48,768]{1,0:T(8,128)}, f32[48,768]{1,0:T(8,...) custom-call(s32[2]{0:T(128)} %pad_add_fusion.lens, f32[2,768]{1,0:T(2,128)} %get-tuple-element.55.d_pool, ...), custom_call_target="tpu_custom_call" | custom-call | tf_op jit(solution)/shard_map/layer_backward/pallas_call | solution.py:746
  253.1 1.7 slice.80
  254.8 0.0 copy-start.4
  254.8 0.0 copy-start.2
  254.8 3.4 %slice.81 = f32[2,512,768]{2,1,0:T(8,128)} slice(bf16[2,576,768]{2,1,0:T(8,128)(2,1)} %get-tuple-element.70), slice={[0:2], [0:512], [0:768]} | slice | bytes 6291456 | tf_op jit(solution)/shard_map/slice | solution.py:864
  258.2 0.0 copy-done.8
  258.3 0.1 constant_dynamic-slice_fusion.1
  258.3 0.5 slice_bitcast_fusion.1
  258.9 0.6 dynamic_slice.22
  259.5 0.7 copy.47
  260.2 0.7 copy.48
  260.9 0.7 copy.49
  261.5 0.7 copy.50
  262.2 0.8 copy.51
  263.0 0.0 copy-done.1
  263.0 0.8 copy.52
  (27 shorter events, 0.2 us)
Async XLA Ops:
  0.7 99.1 %copy-start = (bf16[2,64,768]{2,1,0:T(8,128)(2,1)S(1)}, bf16[2,64,768]{2,1,0:T(8,128)(2,1)}, u32[]{:S(2)}) copy-start(bf16[2,64,768]{2,1,0:T(8,128)(2,1)} %param.19) | copy-start | bytes 589828
  0.7 99.1 %copy-start.3 = (bf16[2,512,768]{2,1,0:T(8,128)(2,1)S(1)}, bf16[2,512,768]{2,1,0:T(8,128)(2,1)}, u32[]{:S(2)}) copy-start(bf16[2,512,768]{2,1,0:T(8,128)(2,1)} %param.20) | copy-start | bytes 4718596
  103.4 40.4 %copy-start.9 = (s32[32]{0:T(128)S(1)}, s32[32]{0:T(128)}, u32[]{:S(2)}) copy-start(s32[32]{0:T(128)} %param.22) | copy-start | bytes 388
  254.8 3.4 %copy-start.8 = (f32[16,768]{1,0:T(8,128)S(1)}, f32[16,768]{1,0:T(8,128)}, u32[]{:S(2)}) copy-start(f32[16,768]{1,0:T(8,128)} %get-tuple-element.77) | copy-start | bytes 147460
  254.8 4.7 %copy-start.7 = (f32[48,768]{1,0:T(8,128)S(1)}, f32[48,768]{1,0:T(8,128)}, u32[]{:S(2)}) copy-start(f32[48,768]{1,0:T(8,128)} %get-tuple-element.109) | copy-start | bytes 442372
  254.8 5.4 %copy-start.6 = (f32[48,768]{1,0:T(8,128)S(1)}, f32[48,768]{1,0:T(8,128)}, u32[]{:S(2)}) copy-start(f32[48,768]{1,0:T(8,128)} %get-tuple-element.110) | copy-start | bytes 442372
  254.8 6.1 %copy-start.5 = (f32[48,768]{1,0:T(8,128)S(1)}, f32[48,768]{1,0:T(8,128)}, u32[]{:S(2)}) copy-start(f32[48,768]{1,0:T(8,128)} %get-tuple-element.111) | copy-start | bytes 442372
  254.8 6.7 %copy-start.4 = (f32[48,768]{1,0:T(8,128)S(1)}, f32[48,768]{1,0:T(8,128)}, u32[]{:S(2)}) copy-start(f32[48,768]{1,0:T(8,128)} %get-tuple-element.112) | copy-start | bytes 442372
  254.8 7.4 %copy-start.2 = (f32[48,3072]{1,0:T(8,128)S(1)}, f32[48,3072]{1,0:T(8,128)}, u32[]{:S(2)}) copy-start(f32[48,3072]{1,0:T(8,128)} %get-tuple-element.113) | copy-start | bytes 1769476
  258.2 4.8 %copy-start.1 = (f32[192,768]{1,0:T(8,128)S(1)}, f32[192,768]{1,0:T(8,128)}, u32[]{:S(2)}) copy-start(f32[192,768]{1,0:T(8,128)} %get-tuple-element.114) | copy-start | bytes 1769476

commit v3 on v2

v3 whole, which is shorter than its diff:
```python
import functools

import jax
import jax.numpy as jnp
from jax import lax
from jax.experimental import pallas as pl
from jax.experimental.pallas import tpu as pltpu
from jax.sharding import PartitionSpec as P

MESH = pl.DeviceIdType.MESH
ANY = pl.BlockSpec(memory_space=pl.ANY)
VM = pl.BlockSpec(memory_space=pltpu.VMEM)


class Place:
    def __init__(self, inner):
        dp = lax.axis_index("dp")
        self.c = lax.axis_index("tower")
        self.inner = inner
        self.low = lax.rem(dp, inner)
        self.me = dp // inner
        self.z = self.me // 4
        self.quad = lax.rem(self.me, 4)
        s1 = 1 + self.c
        s2 = 2 - self.c
        b1 = lax.rem(self.quad // s1, 2)
        b2 = lax.rem(self.quad // s2, 2)
        self.q1 = self.quad + s1 * (1 - 2 * b1)
        self.q2 = self.quad + s2 * (1 - 2 * b2)
        self.q12 = 3 - self.quad
        self.quads = (self.quad, self.q1, self.q2, self.q12)

    def ring(self, k):
        return lax.rem(self.z + k, 4)

    def dev(self, group):
        return {"dp": group * self.inner + self.low, "tower": self.c}

    def n1(self):
        return self.dev(self.z * 4 + self.q1)

    def n2(self):
        return self.dev(self.z * 4 + self.q2)

    def up(self, k):
        return self.dev(self.ring(k) * 4 + self.quad)

    def sib(self):
        return {"dp": self.me * self.inner + self.low, "tower": 1 - self.c}

    def barrier(self):
        sem = pltpu.get_barrier_semaphore()
        for target in (self.up(1), self.up(2), self.up(3), self.n1(), self.n2(), self.sib()):
            pl.semaphore_signal(sem, inc=1, device_id=target, device_id_type=MESH)
        pl.semaphore_wait(sem, 6)


def remote(src, dst, send_sem, recv_sem, target):
    return pltpu.make_async_remote_copy(
        src_ref=src, dst_ref=dst, send_sem=send_sem, recv_sem=recv_sem, device_id=target, device_id_type=MESH
    )


S, Q = 512, 64
T = S + Q


def dot(left, right):
    return jnp.dot(left, right, preferred_element_type=jnp.float32)


def dot_nt(left, right):
    return lax.dot_general(left, right, (((1,), (1,)), ((), ())), preferred_element_type=jnp.float32)


def block(index, size):
    return pl.ds(pl.multiple_of(index * size, size), size)


def low(x):
    return x.astype(jnp.bfloat16)


def wide(x):
    return x.astype(jnp.float32)


def head_mask(h):
    lane = lax.broadcasted_iota(jnp.int32, (1, 128), 1)
    return low(jnp.where(lane // 64 == h, 1.0, 0.0))


SPANS = ((0, S, 256), (S, Q, Q))


class Gather:
    def __init__(self, p, shards, wa, wi, wo, ssem, rsem, lsem):
        self.p, self.shards, self.wa, self.wi, self.wo = p, shards, wa, wi, wo
        self.ssem, self.rsem, self.lsem = ssem, rsem, lsem

    def cols(self, t, which):
        start = which * 384 if t < 4 or t > 7 else (t - 4) * 768 + which * 384
        return pl.ds(pl.multiple_of(start, 128), 384)

    def shard(self, t):
        ref = self.shards[t] if t < 4 else self.shards[4 if t < 8 else 5]
        return ref.at[:, self.cols(t, self.p.c)]

    def one(self, t, z):
        q, cols = self.p.quad, self.cols(t, self.p.c)
        if t < 4:
            return self.wa.at[t, z, q, :, cols]
        return (self.wi if t < 8 else self.wo).at[z, q, :, cols]

    def four(self, t, q, which):
        cols = self.cols(t, which)
        if t < 4:
            return self.wa.at[t, :, q, :, cols]
        if t < 8:
            return self.wi.at[:, q, :, cols]
        return self.wo.at[self.p.ring(12 - t), q, :, cols]

    def copy(self, src, dst, t, k, target):
        return remote(src, dst, self.ssem.at[t, k], self.rsem.at[t, k], target)

    def recv(self, t, k, ref):
        self.copy(ref, ref, t, k, self.p.sib()).wait_recv()

    def push(self, t, q, k, target):
        view = self.four(t, q, self.p.c)
        self.copy(view, view, t, k, target).start()

    def steps(self, t):
        return range(1, 4) if t < 8 else range(t - 8, t - 7) if t > 8 else ()

    def local(self, t):
        return pltpu.make_async_copy(self.shard(t), self.one(t, self.p.z), self.lsem.at[t])

    def stage_own(self, t):
        if t <= 8:
            self.local(t).start()
        for k in self.steps(t):
            self.copy(self.shard(t), self.one(t, self.p.z), t, k, self.p.up(k)).start()

    def stage_z(self, t):
        p = self.p
        if t <= 8:
            self.local(t).wait()
        for k in self.steps(t):
            self.recv(t, k, self.one(t, p.ring(4 - k)))
        self.push(t, p.quad, 4, p.n1())
        self.push(t, p.quad, 5, p.n2())
        self.push(t, p.quad, 8, p.sib())

    def stage_one(self, t):
        p = self.p
        self.recv(t, 4, self.four(t, p.q1, p.c))
        self.push(t, p.q1, 6, p.n2())
        self.push(t, p.q1, 9, p.sib())

    def stage_two(self, t):
        p = self.p
        for k, q in ((5, p.q2), (6, p.q12)):
            self.recv(t, k, self.four(t, q, p.c))
            self.push(t, q, k + 5, p.sib())

    def stage_sib(self, t):
        p = self.p
        for k, q in ((8, p.quad), (9, p.q2), (10, p.q1), (11, p.q12)):
            self.recv(t, k, self.four(t, q, 1 - p.c))

    def tick(self, i):
        for lag, stage in ((0, self.stage_z), (-AHEAD, self.stage_own), (1, self.stage_one), (2, self.stage_two), (3, self.stage_sib)):
            if 0 <= i - lag < 12:
                stage(i - lag)

    def finish(self):
        for t in range(12):
            for k in self.steps(t):
                self.copy(self.shard(t), self.one(t, self.p.z), t, k, self.p.sib()).wait_send()
            view = self.four(t, self.p.quad, self.p.c)
            for k in (4, 5, 6, 8, 9, 10, 11):
                self.copy(view, view, t, k, self.p.sib()).wait_send()


def expand_vectors(shards, vec):
    def split(size, shape, axis):
        at = wide(lax.broadcasted_iota(jnp.int32, shape, axis))
        which = jnp.floor((at + 0.5) * (1.0 / size))
        return which, at - which * size

    lane, _ = split(48, (1, 640), 1)
    spread = jnp.concatenate([jnp.where(lane == i, shards, 0.0) for i in range(8)])
    _, at_row = split(48, (640, 1), 0)
    owner, at_col = split(48, (1, 768), 1)
    rows = dot(low(spread), low(jnp.where(at_row == at_col, 1.0, 0.0)))
    own = wide(lax.broadcasted_iota(jnp.int32, (16, 1), 0))
    for i in range(8):
        vec[i : i + 1, :768] = jnp.sum(jnp.where(owner == own, rows[16 * i : 16 * i + 16], 0.0), axis=0, keepdims=True)
    at_row = wide(lax.broadcasted_iota(jnp.int32, (256, 1), 0))
    for n in range(4):
        owner, at_col = split(192, (1, 768), 1)
        rows = dot(low(shards[:, 384:]), low(jnp.where(at_row == at_col, 1.0, 0.0)))
        vec[8:9, n * 768 : (n + 1) * 768] = jnp.sum(jnp.where(owner + 4.0 * n == own, rows, 0.0), axis=0, keepdims=True)


def forward_kernel(inner, seq, lengths, v_shard, targets, w_query, w_key, w_value, w_output, w_inner, w_outer, query_tokens, passage_tokens,
                   d_pool, loss, lens, vec, wa_out, wi_out, wo_out,
                   k_out, v_out, prob_out, prob_q_out, x_t_out, q_t_out, ctx_t_out, norm_t_out, act_t_out, slope_out, y1_out, r1_out, y2_out, r2_out,
                   wa, wi, wo, x, q, k, v, prob, prob_q, ctx, normed, act, act_t, slope, x_t, q_t, ctx_t, norm_t, y1, r1, y2, r2, pooled, rows, vectors, len_buf,
                   ssem, rsem, lsem, vsem, osem, psem, xsem):
    p = Place(inner)
    pairs = targets.shape[0]
    me = lax.axis_index("dp") * 2 + p.c

    def device(at):
        return {"dp": at // 2, "tower": lax.rem(at, 2)}

    x_loads = [pltpu.make_async_copy(passage_tokens.at[p.c], x.at[pl.ds(0, S)], xsem.at[0]), pltpu.make_async_copy(query_tokens.at[p.c], x.at[pl.ds(S, Q)], xsem.at[1])]
    for copy in x_loads:
        copy.start()
    barrier = pltpu.get_barrier_semaphore()

    @pl.loop(1, pairs)
    def _(i):
        pl.semaphore_signal(barrier, inc=1, device_id=device(lax.rem(me + i, pairs)), device_id_type=MESH)
    lane = lax.broadcasted_iota(jnp.int32, (8, 128), 1)
    len_buf[p.c] = jnp.where(lane == 0, lengths[0, 0].astype(jnp.float32), lengths[0, 1].astype(jnp.float32))
    vectors[p.z, p.quad] = v_shard[...]
    pl.semaphore_wait(barrier, pairs - 1)

    gather = Gather(p, (w_query, w_key, w_value, w_output, w_inner, w_outer), wa, wi, wo, ssem, rsem, lsem)
    for t in range(AHEAD):
        gather.stage_own(t)
    len_copy = remote(len_buf.at[p.c], len_buf.at[p.c], xsem.at[2], xsem.at[3], p.sib())
    len_copy.start()

    def vector(i, q, target):
        view = vectors.at[p.z, p.quad] if i < 4 else vectors.at[:, q]
        return remote(view, view, vsem.at[0, i], vsem.at[1, i], target)

    for i in range(1, 4):
        vector(i, None, p.up(i)).start()
    saves = []

    def save(src, dst):
        copy = pltpu.make_async_copy(src, dst, osem.at[len(saves)])
        copy.start()
        saves.append(copy)

    for copy in x_loads:
        copy.wait()
    x_t[...] = x[...].T
    save(x_t, x_t_out)
    gather.tick(0)
    for i in range(1, 4):
        view = vectors.at[p.ring(4 - i), p.quad]
        remote(view, view, vsem.at[0, i], vsem.at[1, i], p.sib()).wait_recv()
    vector(4, p.quad, p.n1()).start()
    vector(5, p.quad, p.n2()).start()
    gather.tick(1)
    vector(4, p.q1, p.sib()).wait_recv()
    vector(6, p.q1, p.n2()).start()
    gather.tick(2)
    vector(5, p.q2, p.sib()).wait_recv()
    vector(6, p.q12, p.sib()).wait_recv()
    expand_vectors(jnp.concatenate([vectors[i // 4, i % 4] for i in range(16)]), vec)
    remote(len_buf.at[1 - p.c], len_buf.at[1 - p.c], xsem.at[2], xsem.at[3], p.sib()).wait_recv()
    len_q, len_p = [jnp.sum(jnp.where(lane[:1] == p.c, len_buf[i, 0:1], 0.0), axis=1, keepdims=True) for i in range(2)]
    lens[0:1] = jnp.broadcast_to(len_p, (1, 128))
    lens[1:2] = jnp.broadcast_to(len_q, (1, 128))
    lens[2:8] = jnp.zeros((6, 128), jnp.float32)

    def project(m, out, row):
        @pl.loop(0, 3)
        def _(n):
            cols = block(n, 256)
            acc = dot(x[...], wa[m, :, :, :, cols].reshape(768, 256))
            if row is not None:
                acc = acc + vec[row : row + 1, cols]
            out[:, cols] = low(acc)

    gather.tick(3)
    project(0, q, 0)
    gather.tick(4)
    project(1, k, None)
    q_t[...] = q[...].T
    save(q_t, q_t_out)
    save(k, k_out)
    gather.tick(5)
    project(2, v, 1)
    save(v, v_out)

    def store_prob(j):
        return pltpu.make_async_copy(prob.at[lax.rem(j, 2)], prob_out.at[pl.ds(j * 2, 2)], psem.at[lax.rem(j, 2)])

    def attention(low_j, high_j):
        @pl.loop(low_j, high_j)
        def _(j):
            cols = block(j, 128)
            slot = lax.rem(j, 2)

            @pl.when(j >= 2)
            def _():
                store_prob(j - 2).wait()

            for (start, size, rb), length in zip(SPANS, (len_p, len_q)):
                span = slice(start, start + size)
                kp, vp = k[span, cols], v[span, cols]
                valid = wide(lax.broadcasted_iota(jnp.int32, (1, size), 1)) < length
                for r in range(0, size, rb):
                    qp = q[start + r : start + r + rb, cols]
                    total = None
                    for h in range(2):
                        mask = head_mask(h)
                        scores = dot_nt(qp * (mask * 0.125), kp)
                        scores = jnp.where(valid, scores, -1e9)
                        e = jnp.exp(scores - jnp.max(scores, axis=1, keepdims=True))
                        w = low(e * (1.0 / jnp.sum(e, axis=1, keepdims=True)))
                        if size == S:
                            prob[slot, h, r : r + rb] = w
                        else:
                            prob_q[2 * j + h] = w
                        piece = dot(w, vp * mask)
                        total = piece if total is None else total + piece
                    ctx[start + r : start + r + rb, cols] = low(total)
            store_prob(j).start()

    gather.tick(6)
    save(wa, wa_out)
    attention(0, 2)
    gather.tick(7)
    attention(2, 4)
    gather.tick(8)
    attention(4, 6)
    save(prob_q, prob_q_out)
    ctx_t[...] = ctx[...].T
    save(ctx_t, ctx_t_out)

    def gain(row):
        return vec[row : row + 1, :768]

    @pl.loop(0, 3)
    def _(n):
        span = block(n, 192)
        first = wide(x[span]) + (dot(ctx[span], wa[3].reshape(768, 768)) + gain(2))
        center = first - jnp.mean(first, axis=1, keepdims=True)
        scale = lax.rsqrt(jnp.mean(center * center, axis=1, keepdims=True) + 1e-12)
        y = center * scale
        y1[span] = y
        r1[span] = scale
        normed[span] = low(y * gain(4) + gain(5))
    save(y1, y1_out)
    save(r1, r1_out)
    norm_t[...] = normed[...].T
    save(norm_t, norm_t_out)

    def hidden(low_n, high_n):
        @pl.loop(low_n, high_n)
        def _(n):
            cols = block(n, 256)
            u = dot(normed[...], wi[:, :, :, cols].reshape(768, 256)) + vec[8:9, cols]
            cdf = 0.5 * (1.0 + lax.erf(u * 0.7071067811865476))
            act[:, cols] = low(u * cdf)
            slope[:, cols] = low(cdf + u * (0.3989422804014327 * jnp.exp(-0.5 * u * u)))

    gather.tick(9)
    hidden(0, 9)
    gather.tick(10)
    save(wi, wi_out)
    hidden(9, 12)
    save(slope, slope_out)

    for b in range(4):
        turned = act[:, b * 768 : (b + 1) * 768].T
        for s in range(4):
            for n in range(4):
                row = n * 768 + (b * 4 + s) * 48
                act_t[row : row + 48] = turned[s * 192 + n * 48 : s * 192 + n * 48 + 48]
    save(act_t, act_t_out)
    pooled[...] = jnp.zeros_like(pooled)

    def outer(i):
        plane = p.ring(4 - i)

        @pl.loop(0, 3)
        def _(n):
            span = block(n, 192)
            add = dot(act[span, pl.ds(pl.multiple_of(plane * 768, 128), 768)], wo[plane].reshape(768, 768))
            if i == 0:
                add = add + (y1[span] * gain(4) + gain(5) + gain(3))
            else:
                add = add + y2[span]
            if i < 3:
                y2[span] = add
                return
            center = add - jnp.mean(add, axis=1, keepdims=True)
            scale = lax.rsqrt(jnp.mean(center * center, axis=1, keepdims=True) + 1e-12)
            y = center * scale
            y2[span] = y
            r2[span] = scale
            out = y * gain(6) + gain(7)
            at = wide(lax.broadcasted_iota(jnp.int32, (192, 1), 0) + n * 192)
            for row, keep in ((0, (at >= S) & (at - S < len_q)), (1, (at < S) & (at < len_p))):
                pooled[row : row + 1] += jnp.sum(jnp.where(keep, out, 0.0), axis=0, keepdims=True)

    for i in range(4):
        gather.tick(11 + i)
        outer(i)
    save(y2, y2_out)
    save(r2, r2_out)
    save(wo, wo_out)

    mine = jnp.concatenate([pooled[0:1] / len_q, pooled[1:2] / len_p])
    root = jnp.sqrt(jnp.sum(mine * mine, axis=1, keepdims=True) + 1e-6)
    unit = mine / root
    rows[me] = unit

    @pl.loop(1, pairs)
    def _(i):
        remote(rows.at[me], rows.at[me], xsem.at[4], xsem.at[5], device(lax.rem(me + i, pairs))).start()
    rest = rows.at[pl.ds(0, pairs - 1)]
    remote(rest, rest, xsem.at[4], xsem.at[5], p.sib()).wait_recv()
    exact = lax.Precision.HIGHEST
    qs, ps = rows[:, 0, :], rows[:, 1, :]
    logits = lax.dot_general(qs, ps, (((1,), (1,)), ((), ())), precision=exact, preferred_element_type=jnp.float32) / 0.01
    hit = targets[...] == lax.broadcasted_iota(jnp.int32, (pairs, pairs), 1)
    top = jnp.max(logits, axis=1, keepdims=True)
    lse = jnp.log(jnp.sum(jnp.exp(logits - top), axis=1, keepdims=True)) + top
    picked = jnp.sum(jnp.where(hit, logits, 0.0), axis=1, keepdims=True)
    loss[...] = jnp.broadcast_to(jnp.sum(lse - picked, axis=0, keepdims=True) / pairs, loss.shape)
    d_logits = seq * (jnp.exp(logits - lse) - jnp.where(hit, 1.0, 0.0))
    d_q = jnp.dot(d_logits, ps, precision=exact, preferred_element_type=jnp.float32) / 0.01
    d_p = lax.dot_general(d_logits, qs, (((0,), (0,)), ((), ())), precision=exact, preferred_element_type=jnp.float32) / 0.01
    own = lax.broadcasted_iota(jnp.int32, (pairs, 1), 0) == me
    for row, d in enumerate((d_q, d_p)):
        d_unit = jnp.sum(jnp.where(own, d, 0.0), axis=0, keepdims=True)
        u = unit[row : row + 1]
        d_pool[row : row + 1] = (d_unit - u * jnp.sum(u * d_unit, axis=1, keepdims=True)) / root[row : row + 1]

    remote(rest, rest, xsem.at[4], xsem.at[5], p.sib()).wait_send()
    gather.finish()
    len_copy.wait_send()
    for i in range(1, 7):
        vector(i, p.quad, p.sib()).wait_send()
    for copy in saves:
        copy.wait()
    store_prob(4).wait()
    store_prob(5).wait()


AHEAD = 2


def forward_call(inner, seq, lengths, v_shard, targets, weights, query_tokens, passage_tokens, cid=0):
    bf, f32 = jnp.bfloat16, jnp.float32
    sds, vmem, dma = jax.ShapeDtypeStruct, pltpu.VMEM, pltpu.SemaphoreType.DMA
    pairs = targets.shape[0]
    stored = [((T, 768), bf)] * 2 + [((12, S, S), bf), ((12, Q, Q), bf)] + [((768, T), bf)] * 4 + [
        ((3072, T), bf), ((T, 3072), bf), ((T, 768), f32), ((T, 1), f32), ((T, 768), f32), ((T, 1), f32)]
    full = [((4, 4, 4, 48, 768), bf), ((4, 4, 48, 3072), bf), ((4, 4, 192, 768), bf)]
    outs = [((2, 768), f32), ((8, 128), f32), ((8, 128), f32), ((16, 3072), f32)] + full + stored
    rows = (T, 768)
    scratch = [vmem(*w) for w in full] + [vmem(rows, bf)] * 4 + [vmem((2, 2, S, S), bf), vmem((12, Q, Q), bf)] + [vmem(rows, bf)] * 2
    scratch += [vmem((T, 3072), bf), vmem((3072, T), bf), vmem((T, 3072), bf)] + [vmem((768, T), bf)] * 4
    scratch += [vmem(rows, f32), vmem((T, 1), f32), vmem(rows, f32), vmem((T, 1), f32), vmem((2, 768), f32)]
    scratch += [vmem((pairs, 2, 768), f32), vmem((4, 4, 1, 640), f32), vmem((2, 8, 128), f32)]
    scratch += [dma((12, 12)), dma((12, 12)), dma((9,)), dma((2, 7)), dma((17,)), dma((2,)), dma((6,))]
    return pl.pallas_call(
        functools.partial(forward_kernel, inner, seq),
        out_shape=[sds(*o) for o in outs],
        in_specs=[pl.BlockSpec(memory_space=pltpu.SMEM), VM, VM] + [ANY] * 8,
        out_specs=[VM] * 4 + [ANY] * 17,
        scratch_shapes=scratch,
        compiler_params=pltpu.CompilerParams(collective_id=cid, has_side_effects=True, vmem_limit_bytes=62 << 20),
        name="layer_forward",
    )(lengths, v_shard, targets, *weights, query_tokens, passage_tokens)


class Scatter:
    def __init__(self, p, refs, result):
        self.p = p
        self.stage, self.r0, self.acc, self.r1, self.r2, self.r3, self.ssem, self.rsem = refs
        self.result = result
        self.own = pl.ds(pl.multiple_of(p.c * 384, 128), 384)
        self.other = pl.ds(pl.multiple_of((1 - p.c) * 384, 128), 384)

    def copy(self, src, dst, e, k, target):
        return remote(src, dst, self.ssem.at[e, k], self.rsem.at[e, k], target)

    def recv(self, e, k, ref):
        self.copy(ref, ref, e, k, self.p.sib()).wait_recv()

    def emit(self, e, left, right, extra=None):
        if e >= 2:
            self.shared(e - 2).wait_send()

        @pl.loop(0, 3)
        def _(n):
            cols = block(n, 256)
            values = right(cols)
            self.stage[e % 2, :, :, :, cols] = low(dot(left(), values)).reshape(4, 4, 48, 256)
            if extra is not None:
                extra(cols, values)
        self.shared(e).start()

    def shared(self, e):
        return self.copy(self.stage.at[e % 2, :, :, :, self.other], self.r0.at[e % 4], e, 0, self.p.sib())

    def stage0(self, e):
        p, acc = self.p, self.acc
        self.recv(e, 0, self.r0.at[e % 4])
        for j, q in enumerate((p.q2, p.q12, p.q1, p.quad)):
            acc[e, :, q] = self.stage[e % 2, :, q, :, self.own] + self.r0[e % 4, :, q]
            if j < 2:
                self.copy(acc.at[e, :, q], self.r1.at[e, j], e, 1 + j, p.n2()).start()

    def stage1(self, e):
        p, acc = self.p, self.acc
        self.recv(e, 2, self.r1.at[e, 1])
        acc[e, :, p.q1] += self.r1[e, 1]
        self.copy(acc.at[e, :, p.q1], self.r2.at[e], e, 3, p.n1()).start()
        self.recv(e, 1, self.r1.at[e, 0])
        acc[e, :, p.quad] += self.r1[e, 0]

    def stage2(self, e):
        p, acc = self.p, self.acc
        self.recv(e, 3, self.r2.at[e])
        acc[e, :, p.quad] += self.r2[e]
        for k in range(1, 4):
            self.copy(acc.at[e, p.ring(k), p.quad], self.r3.at[e, k - 1], e, 3 + k, p.up(k)).start()

    def stage3(self, e):
        p = self.p
        total = wide(self.acc[e, p.z, p.quad])
        for k in range(1, 4):
            self.recv(e, 3 + k, self.r3.at[e, k - 1])
            total = total + wide(self.r3[e, k - 1])
        view = self.result(e, p.c)
        view[...] = total
        self.copy(view, view, e, 7, p.sib()).start()

    def finish(self, count):
        for e in range(count):
            self.recv(e, 7, self.result(e, 1 - self.p.c))
            self.copy(self.result(e, self.p.c), self.result(e, self.p.c), e, 7, self.p.sib()).wait_send()
        for e in range(count - 2, count):
            self.shared(e).wait_send()
        four, one = self.r2.at[0], self.r3.at[0, 0]

        @pl.loop(0, count)
        def _(e):
            for k in range(1, 7):
                view = four if k < 4 else one
                self.copy(view, view, e, k, self.p.sib()).wait_send()


def backward_kernel(inner, lens, d_pool, vec, a_hbm, i_hbm, o_hbm, k_hbm, v_hbm, prob_hbm, prob_q_hbm, x_t_hbm, q_t_hbm, ctx_t_hbm, norm_t_hbm,
                    act_t_hbm, slope_hbm, y1_hbm, r1_hbm, y2_hbm, r2_hbm,
                    dx_out, dvec_out, g_query, g_key, g_value, g_output, g_inner, g_outer,
                    wa, wi, act_t, slope, d_inner, y, scale_one, scale_two, d_second, d_low, norm_t, ctx_t, x_t, q_t, k, v, prob, prob_q, ds_buf,
                    d_vec, v_in, v_out, stage, r0, acc, r1, r2, r3, ssem, rsem, lsem, psem, vsem, xsem):
    p = Place(inner)

    def load(i, src, dst):
        return pltpu.make_async_copy(src, dst, lsem.at[i])

    loads = {
        "y2": load(0, y2_hbm, y), "r2": load(1, r2_hbm, scale_two), "act_t": load(2, act_t_hbm, act_t),
        "slope": load(7, slope_hbm, slope), "norm_t": load(8, norm_t_hbm, norm_t), "wi": load(9, i_hbm, wi),
        "y1": load(10, y1_hbm, y), "r1": load(11, r1_hbm, scale_one), "ctx_t": load(12, ctx_t_hbm, ctx_t), "wa": load(13, a_hbm, wa),
        "k": load(14, k_hbm, k), "v": load(15, v_hbm, v), "q_t": load(16, q_t_hbm, q_t), "x_t": load(17, x_t_hbm, x_t), "prob_q": load(18, prob_q_hbm, prob_q),
    }
    for n in range(4):
        loads["wo%d" % n] = load(3 + n, o_hbm.at[pl.ds(n * 768, 768)], wa.at[n])

    def start(*names):
        for name in names:
            loads[name].start()

    def need(*names):
        for name in names:
            loads[name].wait()

    def load_prob(j):
        return pltpu.make_async_copy(prob_hbm.at[pl.ds(j * 2, 2)], prob.at[lax.rem(j, 2)], psem.at[lax.rem(j, 2)])

    start("y2", "r2", "act_t", "wo0", "wo1", "wo2", "wo3", "slope", "norm_t", "wi", "r1", "ctx_t", "k", "v", "q_t", "x_t", "prob_q")
    load_prob(0).start()
    load_prob(1).start()
    p.barrier()

    def result(e, which):
        cols = pl.ds(pl.multiple_of(which * 384, 128), 384)
        if e < 4:
            return g_outer.at[pl.ds(e * 48, 48), cols]
        if e < 8:
            return g_inner.at[:, pl.ds(pl.multiple_of((e - 4) * 768 + which * 384, 128), 384)]
        return (g_output, g_query, g_key, g_value)[e - 8].at[:, cols]

    sc = Scatter(p, (stage, r0, acc, r1, r2, r3, ssem, rsem), result)
    d_vec[...] = jnp.zeros_like(d_vec)

    def gain(row):
        return vec[row : row + 1, :768]

    def tally(row, value):
        d_vec[row : row + 1] += jnp.sum(value, axis=0, keepdims=True)

    len_p, len_q = lens[0:1, 0:1], lens[1:2, 0:1]
    pool_q = d_pool[0:1] / len_q
    pool_p = d_pool[1:2] / len_p

    def norm_back(d, row, yy, scale, rows):
        tally(row, d * yy)
        tally(row + 1, d)
        g = d * gain(row)
        d = (g - jnp.mean(g, axis=1, keepdims=True) - yy * jnp.mean(g * yy, axis=1, keepdims=True)) * scale
        d_second[rows] = d
        d_low[rows] = low(d)
        return d

    need("y2", "r2")

    @pl.loop(0, 3)
    def _(n):
        rows = block(n, 192)
        at = wide(lax.broadcasted_iota(jnp.int32, (192, 1), 0) + n * 192)
        d_rows = jnp.where(at < S, jnp.where(at < len_p, pool_p, 0.0), jnp.where(at - S < len_q, pool_q, 0.0))
        d = norm_back(d_rows, 6, y[rows], scale_two[rows], rows)
        tally(3, wide(low(d)))

    start("y1")
    need("act_t")

    def emit_outer(n):
        sc.emit(n, lambda: act_t[n * 768 : (n + 1) * 768], lambda cols: d_low[:, cols])

    def emit_inner(n):
        def bias(cols, values):
            d_vec[8 + n : 9 + n, cols] = jnp.sum(wide(values), axis=0, keepdims=True)
        sc.emit(4 + n, lambda: norm_t[...], lambda cols: d_inner[:, pl.ds(pl.multiple_of(n * 768 + cols.start, 256), 256)], bias)

    emit_outer(0)
    emit_outer(1)
    sc.stage0(0)
    emit_outer(2)
    sc.stage0(1)
    emit_outer(3)
    sc.stage0(2)
    need("wo0", "wo1", "wo2", "wo3", "slope")

    def inner_back(low_n, high_n):
        @pl.loop(low_n, high_n)
        def _(n):
            cols = block(n, 256)
            d_inner[:, cols] = low(dot_nt(d_low[...], wa[n // 3, block(lax.rem(n, 3), 256)]) * wide(slope[:, cols]))

    inner_back(0, 6)
    sc.stage0(3)
    inner_back(6, 12)
    start("wa")
    sc.stage1(0)
    need("norm_t")
    emit_inner(0)
    sc.stage1(1)
    emit_inner(1)
    sc.stage0(4)
    sc.stage2(0)
    emit_inner(2)
    sc.stage0(5)
    sc.stage1(2)
    emit_inner(3)
    sc.stage0(6)
    sc.stage2(1)
    need("wi", "y1", "r1")

    @pl.loop(0, 3)
    def _(n):
        rows = block(n, 192)
        d = norm_back(d_second[rows] + dot_nt(d_inner[rows], wi[...]), 4, y[rows], scale_one[rows], rows)
        tally(2, wide(low(d)))

    sc.stage0(7)
    sc.stage1(3)
    sc.stage2(2)
    need("ctx_t", "wa")
    sc.emit(8, lambda: ctx_t[...], lambda cols: d_low[:, cols])

    def part(i):
        return pl.ds(i * 768, 768)

    def pair_cols(i, j):
        return pl.ds(pl.multiple_of(i * 768 + j * 128, 128), 128)

    def head_rows(i, head):
        return pl.ds(pl.multiple_of(i * 768 + head * 64, 64), 64)

    @pl.loop(0, 3)
    def _(n):
        rows = block(n, 192)
        d_inner[rows, part(3)] = low(dot_nt(d_low[rows], wa[3]))
    act_t[part(2)] = d_inner[:, part(3)].T
    need("k", "v", "q_t", "prob_q")
    sc.stage0(8)
    sc.stage1(4)
    sc.stage2(3)
    sc.stage3(0)

    def attention(low_j, high_j):
        @pl.loop(low_j, high_j)
        def _(j):
            load_prob(j).wait()
            slot = lax.rem(j, 2)
            cols = block(j, 128)
            for start, size, rb in SPANS:
                rows = slice(start, start + size)
                kp, vp = k[rows, cols], v[rows, cols]
                dq_parts = [None] * (size // rb)
                for h in range(2):
                    probs = (lambda sl: prob[slot, h, sl]) if size == S else (lambda sl: prob_q[2 * j + h, sl])
                    mask = head_mask(h)
                    for r in range(0, size, rb):
                        d_p = dot_nt(d_inner[start + r : start + r + rb, pair_cols(3, j)] * mask, vp)
                        w = wide(probs(slice(r, r + rb)))
                        ds = low(w * (d_p - jnp.sum(w * d_p, axis=1, keepdims=True)))
                        ds_buf[h, r : r + rb, :size] = ds
                        piece = dot(ds, kp * mask)
                        i = r // rb
                        dq_parts[i] = piece if dq_parts[i] is None else dq_parts[i] + piece
                    head = 2 * j + h
                    act_t[head_rows(1, head), rows] = low(dot(act_t[head_rows(2, head), rows], probs(slice(0, size))))
                    act_t[head_rows(0, head), rows] = low(dot(q_t[head_rows(0, head), rows], ds_buf[h, :size, :size]) * 0.125)
                for i, piece in enumerate(dq_parts):
                    d_inner[start + i * rb : start + (i + 1) * rb, pair_cols(0, j)] = low(piece * 0.125)

            @pl.when(j < 4)
            def _():
                load_prob(j + 2).start()

    attention(0, 2)
    sc.stage1(5)
    sc.stage2(4)
    sc.stage3(1)
    attention(2, 4)
    sc.stage1(6)
    sc.stage2(5)
    sc.stage3(2)
    attention(4, 6)
    sc.stage1(7)
    sc.stage2(6)
    sc.stage3(3)
    d_inner[:, part(1)] = act_t[part(0)].T
    d_inner[:, part(2)] = act_t[part(1)].T
    need("x_t")

    def emit_first(n):
        row = (0, None, 1)[n]

        def bias(cols, values):
            d_vec[row : row + 1, cols] = jnp.sum(wide(values), axis=0, keepdims=True)
        sc.emit(9 + n, lambda: x_t[...], lambda cols: d_inner[:, pl.ds(pl.multiple_of(n * 768 + cols.start, 256), 256)], None if row is None else bias)

    emit_first(0)
    sc.stage1(8)
    emit_first(1)
    sc.stage0(9)
    emit_first(2)

    def vector(i, src, target):
        return remote(src, v_in.at[i], vsem.at[0, i], vsem.at[1, i], target)

    def vector_recv(i):
        vector(i, v_in.at[i], p.sib()).wait_recv()
        return v_in[i]

    vector(0, d_vec.at[:, sc.other], p.sib()).start()
    sc.stage0(10)
    sc.stage2(7)

    @pl.loop(0, 3)
    def _(n):
        rows = block(n, 192)
        d = d_second[rows]
        for i in range(3):
            d = d + dot_nt(d_inner[rows, part(i)], wa[i])
        d_low[rows] = low(d)
    mine = pltpu.make_async_copy(d_low, dx_out.at[p.c], xsem.at[0])
    theirs = remote(d_low, dx_out.at[p.c], xsem.at[1], xsem.at[2], p.sib())
    mine.start()
    theirs.start()
    sc.stage0(11)
    v_out[0] = d_vec[:, sc.own] + vector_recv(0)
    vector(1, v_out.at[0], p.n2()).start()
    sc.stage3(4)
    sc.stage1(9)
    v_out[1] = v_out[0] + vector_recv(1)
    vector(2, v_out.at[1], p.n1()).start()
    sc.stage2(8)
    sc.stage3(5)
    sc.stage1(10)
    v_out[2] = v_out[1] + vector_recv(2)
    for i in range(1, 4):
        vector(2 + i, v_out.at[2], p.up(i)).start()
    sc.stage2(9)
    sc.stage3(6)
    sc.stage1(11)
    sc.stage2(10)
    sc.stage3(7)
    dvec_out[:, sc.own] = v_out[2] + vector_recv(3) + vector_recv(4) + vector_recv(5)
    last = remote(dvec_out.at[:, sc.own], dvec_out.at[:, sc.own], vsem.at[0, 6], vsem.at[1, 6], p.sib())
    last.start()
    sc.stage2(11)
    for e in range(8, 12):
        sc.stage3(e)
    mine.wait()
    theirs.wait_send()
    remote(dx_out.at[1 - p.c], dx_out.at[1 - p.c], xsem.at[1], xsem.at[2], p.sib()).wait_recv()
    remote(dvec_out.at[:, sc.other], dvec_out.at[:, sc.other], vsem.at[0, 6], vsem.at[1, 6], p.sib()).wait_recv()
    last.wait_send()
    for i in range(6):
        vector(i, v_in.at[i], p.sib()).wait_send()
    sc.finish(12)


def backward_call(inner, lens, d_pool, vec, wa, wi, wo, saved, cid=1):
    bf, f32 = jnp.bfloat16, jnp.float32
    sds = jax.ShapeDtypeStruct
    outs = [sds((2, T, 768), bf), sds((16, 768), f32)] + [sds((48, 768), f32)] * 4 + [sds((48, 3072), f32), sds((192, 768), f32)]
    vmem = pltpu.VMEM
    scratch = [
        vmem((4, 768, 768), bf), vmem((768, 3072), bf), vmem((3072, T), bf), vmem((T, 3072), bf), vmem((T, 3072), bf),
        vmem((T, 768), f32), vmem((T, 1), f32), vmem((T, 1), f32), vmem((T, 768), f32), vmem((T, 768), bf)]
    scratch += [vmem((768, T), bf)] * 4 + [vmem((T, 768), bf)] * 2
    scratch += [vmem((2, 2, S, S), bf), vmem((12, Q, Q), bf), vmem((2, S, S), bf), vmem((16, 768), f32), vmem((6, 16, 384), f32), vmem((3, 16, 384), f32)]
    scratch += [vmem((2, 4, 4, 48, 768), bf), vmem((4, 4, 4, 48, 384), bf), vmem((12, 4, 4, 48, 384), bf), vmem((12, 2, 4, 48, 384), bf), vmem((12, 4, 48, 384), bf), vmem((12, 3, 48, 384), bf)]
    dma = pltpu.SemaphoreType.DMA
    scratch += [dma((12, 8)), dma((12, 8)), dma((19,)), dma((2,)), dma((2, 7)), dma((3,))]
    return pl.pallas_call(
        functools.partial(backward_kernel, inner),
        out_shape=outs,
        in_specs=[VM] * 3 + [ANY] * 17,
        out_specs=[ANY] + [VM] * 7,
        scratch_shapes=scratch,
        compiler_params=pltpu.CompilerParams(collective_id=cid, has_side_effects=True, vmem_limit_bytes=63 << 20),
        name="layer_backward",
    )(lens, d_pool, vec, wa, wi, wo, *saved)


def per_device(
    query_tokens, passage_tokens, lengths, positives,
    query_weight, key_weight, value_weight, output_weight, inner_weight, outer_weight,
    query_bias, value_bias, output_bias, inner_bias, outer_bias,
    first_gain, first_shift, second_gain, second_shift,
):
    inner = lax.axis_size("dp") // 16
    groups = None if inner == 1 else [[h * inner + i for i in range(inner)] for h in range(16)]
    at = lax.axis_index("dp") // inner
    seq = passage_tokens.shape[1]

    def fetch(w):
        if groups is None:
            return w
        return lax.all_gather(w, "dp", axis=0, tiled=True, axis_index_groups=groups)

    weights = [fetch(w) for w in (query_weight, key_weight, value_weight, output_weight, inner_weight, outer_weight)]
    vectors = (query_bias, value_bias, output_bias, outer_bias, first_gain, first_shift, second_gain, second_shift, inner_bias)
    v_shard = jnp.concatenate([fetch(w) for w in vectors] + [jnp.zeros((64,), query_bias.dtype)])
    d_pool, loss, lens, vec, wa, wi, wo, *saved = forward_call(
        inner, float(seq), lengths, v_shard.astype(jnp.float32)[None], positives[:, None], weights, query_tokens, passage_tokens)
    wa, wi, wo = wa.reshape(4, 768, 768), wi.reshape(768, 3072), wo.reshape(3072, 768)
    d_x, d_vec, *grads = backward_call(inner, lens, d_pool, vec, wa, wi, wo, saved)

    def finish(x):
        if groups is None:
            return x
        return lax.psum_scatter(x, "dp", scatter_dimension=0, tiled=True, axis_index_groups=groups)

    d_x = d_x.astype(jnp.float32)
    flat = lax.dynamic_slice_in_dim(d_vec[:8], at * 48, 48, 1)
    wide_bias = lax.dynamic_slice_in_dim(d_vec[8:12].reshape(3072), at * 192, 192, 0)
    rows = [finish(flat[i]) for i in range(8)]
    tail = [rows[0], rows[1], rows[2], finish(wide_bias)] + rows[3:]
    return (loss[0, 0], d_x[:, seq:], d_x[:, :seq]) + tuple(finish(g) for g in grads) + tuple(tail)


def solution(mesh):
    rows3, rows2, rows1 = P("dp", None, None), P("dp", None), P("dp")
    return jax.shard_map(
        per_device,
        mesh=mesh,
        in_specs=(rows3, rows3, P("tower", "dp"), P()) + (rows2,) * 6 + (rows1,) * 9,
        out_specs=(P(), rows3, rows3) + (rows2,) * 6 + (rows1,) * 9,
        check_vma=False,
    )
```

time: 264 us -> 201 us (0.76)
  Pallas kernels: 234 us -> 184 us
  local copies, waits for them, and re-layouts: 23.8 us -> 14.8 us
  other arithmetic: 5.35 us -> 0.58 us
    pallas_call x3 -> x1, Pallas kernels: 137 us -> 94.1 us  [forward_call(): pl.pallas_call(functools.partial(forward_kernel, inner, seq), out_shape=[...]
    pad x11 -> x0, local copies, waits for them, and re-layouts: 7.92 us -> none  [the longest x9 6.07 us: per_device(): jnp.pad(w, (0, 256 - w.shape[0]))]
    pallas_call x1, Pallas kernels: 96.9 us -> 90 us  [backward_call(): pl.pallas_call(functools.partial(backward_kernel, inner), out_shape=outs,...]
    another operation x2 -> x0, other arithmetic: 3.62 us -> none  [the longest x1 1.88 us: per_device(): own = jnp.stack([pair[1], pair[0]])]
where the time goes in v3:
time: 201 us; the launch traced here: 200 us
  Pallas kernels  184 us (92%)
  local copies, waits for them, and re-layouts  14.8 us (7%)
    pallas_call x1, Pallas kernels, forward_call(): pl.pallas_call(functools.partial(forward_kernel, inner, seq), out_shape=[...  94.1 us
    pallas_call x1, Pallas kernels, backward_call(): pl.pallas_call(functools.partial(backward_kernel, inner), out_shape=outs,...  90 us
    unnamed x20, local copies, waits for them, and re-layouts  4.3 us

profile of v3, /device:TPU:0, one launch (start us, length us, event | category | flops | bytes accessed | tf_op | source)
XLA Modules:
  0.0 200.2 jit_solution(6135929644110065898)
XLA Ops:
  0.7 0.7 concatenate.36
  1.3 0.9 concatenate.37
  2.2 0.6 convert_element_type.13.v_shard
  2.8 1.3 copy.37.targets
  4.1 94.1 %layer_forward.1 = (f32[2,768]{1,0:T(2,128)}, f32[8,128]{1,0:T(8,128)}, f32[8,128]{1,0:T(8,128)}, f32[16,3072]{1,0:T(8,128)}, bf16[4,4,4,48,768]{4,3,2,1,0:T(8,1...) custom-call(s32[1,2]{1,0:T(1,128)} %lengths.1, ...), custom_call_target="tpu_custom_call" | custom-call | tf_op jit(solution)/shard_map/layer_forward/pallas_call | solution.py:469
  98.2 1.2 slice.39
  99.4 90.0 %layer_backward.1 = (bf16[2,576,768]{2,1,0:T(8,128)(2,1)}, f32[16,768]{1,0:T(8,128)}, f32[48,768]{1,0:T(8,128)}, f32[48,768]{1,0:T(8,128)}, f32[48,768]{1,0:T(8,...) custom-call(f32[8,128]{1,0:T(8,128)} %get-tuple-element.48.lens, ...), custom_call_target="tpu_custom_call" | custom-call | tf_op jit(solution)/shard_map/layer_backward/pallas_call | solution.py:839
  189.4 0.0 copy-start.6
  189.4 0.0 copy-start.5
  189.4 1.7 slice.52
  191.2 0.0 copy-start.4
  191.2 0.0 copy-start.3
  191.2 0.0 copy-start.2
  191.2 0.0 copy-start.1
  191.2 0.0 copy-start
  191.2 3.4 %slice.53 = f32[2,512,768]{2,1,0:T(8,128)} slice(bf16[2,576,768]{2,1,0:T(8,128)(2,1)} %get-tuple-element.68), slice={[0:2], [0:512], [0:768]} | slice | bytes 6291456 | tf_op jit(solution)/shard_map/slice | solution.py:884
  194.6 0.0 copy-done.6
  194.6 0.1 constant_dynamic-slice_fusion
  194.7 0.5 slice_bitcast_fusion
  195.2 0.6 dynamic_slice.7
  195.9 0.0 copy-done.5
  195.9 0.7 copy.44
  196.6 0.0 copy-done.4
  196.6 0.7 copy.45
  197.2 0.0 copy-done.3
  197.2 0.7 copy.46
  197.9 0.0 copy-done.2
  197.9 0.7 copy.47
  198.5 0.0 copy-done.1
  198.5 0.8 copy.48
  199.4 0.0 copy-done
  199.4 0.8 copy.49
  (4 shorter events, 0.0 us)
Async XLA Ops:
  189.4 5.2 %copy-start.6 = (f32[16,768]{1,0:T(8,128)S(1)}, f32[16,768]{1,0:T(8,128)}, u32[]{:S(2)}) copy-start(f32[16,768]{1,0:T(8,128)} %get-tuple-element.75) | copy-start | bytes 147460
  189.4 6.5 %copy-start.5 = (f32[48,768]{1,0:T(8,128)S(1)}, f32[48,768]{1,0:T(8,128)}, u32[]{:S(2)}) copy-start(f32[48,768]{1,0:T(8,128)} %get-tuple-element.105) | copy-start | bytes 442372
  191.2 5.4 %copy-start.4 = (f32[48,768]{1,0:T(8,128)S(1)}, f32[48,768]{1,0:T(8,128)}, u32[]{:S(2)}) copy-start(f32[48,768]{1,0:T(8,128)} %get-tuple-element.106) | copy-start | bytes 442372
  191.2 6.1 %copy-start.3 = (f32[48,768]{1,0:T(8,128)S(1)}, f32[48,768]{1,0:T(8,128)}, u32[]{:S(2)}) copy-start(f32[48,768]{1,0:T(8,128)} %get-tuple-element.107) | copy-start | bytes 442372
  191.2 6.7 %copy-start.2 = (f32[48,768]{1,0:T(8,128)S(1)}, f32[48,768]{1,0:T(8,128)}, u32[]{:S(2)}) copy-start(f32[48,768]{1,0:T(8,128)} %get-tuple-element.108) | copy-start | bytes 442372
  191.2 7.4 %copy-start.1 = (f32[48,3072]{1,0:T(8,128)S(1)}, f32[48,3072]{1,0:T(8,128)}, u32[]{:S(2)}) copy-start(f32[48,3072]{1,0:T(8,128)} %get-tuple-element.109) | copy-start | bytes 1769476
  191.2 8.2 %copy-start = (f32[192,768]{1,0:T(8,128)S(1)}, f32[192,768]{1,0:T(8,128)}, u32[]{:S(2)}) copy-start(f32[192,768]{1,0:T(8,128)} %get-tuple-element.110) | copy-start | bytes 1769476

commit v4 on v3

--- a/solution.py
+++ b/solution.py
@@ -106,8 +106,8 @@
         ref = self.shards[t] if t < 4 else self.shards[4 if t < 8 else 5]
         return ref.at[:, self.cols(t, self.p.c)]
 
-    def one(self, t, z):
-        q, cols = self.p.quad, self.cols(t, self.p.c)
+    def one(self, t, z, q):
+        cols = self.cols(t, self.p.c)
         if t < 4:
             return self.wa.at[t, z, q, :, cols]
         return (self.wi if t < 8 else self.wo).at[z, q, :, cols]
@@ -134,28 +134,52 @@
         return range(1, 4) if t < 8 else range(t - 8, t - 7) if t > 8 else ()
 
     def local(self, t):
-        return pltpu.make_async_copy(self.shard(t), self.one(t, self.p.z), self.lsem.at[t])
+        return pltpu.make_async_copy(self.shard(t), self.one(t, self.p.z, self.p.quad), self.lsem.at[t])
+
+    def push_one(self, t, z, q, k, target):
+        view = self.one(t, z, q)
+        self.copy(view, view, t, k, target).start()
+
+    def direct(self, t):
+        return t not in TURNED
 
     def stage_own(self, t):
+        p = self.p
         if t <= 8:
             self.local(t).start()
         for k in self.steps(t):
-            self.copy(self.shard(t), self.one(t, self.p.z), t, k, self.p.up(k)).start()
+            self.copy(self.shard(t), self.one(t, p.z, p.quad), t, k, p.up(k)).start()
+        if t <= 8:
+            self.copy(self.shard(t), self.one(t, p.z, p.quad), t, 4, p.n1()).start()
+            self.copy(self.shard(t), self.one(t, p.z, p.quad), t, 5, p.n2()).start()
 
     def stage_z(self, t):
         p = self.p
+        if not self.direct(t):
+            self.recv(t, 4, self.one(t, p.z, p.q1))
+            for k in range(1, 4):
+                self.push_one(t, p.z, p.q1, 11 + k, p.up(k))
+            self.push_one(t, p.z, p.q1, 6, p.n2())
+        for k in self.steps(t):
+            z = p.ring(4 - k)
+            self.recv(t, k, self.one(t, z, p.quad))
+            if self.direct(t):
+                self.push_one(t, z, p.quad, 4, p.n1())
+            self.push_one(t, z, p.quad, 5, p.n2())
         if t <= 8:
             self.local(t).wait()
-        for k in self.steps(t):
-            self.recv(t, k, self.one(t, p.ring(4 - k)))
-        self.push(t, p.quad, 4, p.n1())
-        self.push(t, p.quad, 5, p.n2())
         self.push(t, p.quad, 8, p.sib())
 
     def stage_one(self, t):
         p = self.p
-        self.recv(t, 4, self.four(t, p.q1, p.c))
-        self.push(t, p.q1, 6, p.n2())
+        if self.direct(t):
+            self.recv(t, 4, self.four(t, p.q1, p.c))
+            self.push(t, p.q1, 6, p.n2())
+        else:
+            for k in range(1, 4):
+                z = p.ring(4 - k)
+                self.recv(t, 11 + k, self.one(t, z, p.q1))
+                self.push_one(t, z, p.q1, 6, p.n2())
         self.push(t, p.q1, 9, p.sib())
 
     def stage_two(self, t):
@@ -170,47 +194,43 @@
             self.recv(t, k, self.four(t, q, 1 - p.c))
 
     def tick(self, i):
-        for lag, stage in ((0, self.stage_z), (-AHEAD, self.stage_own), (1, self.stage_one), (2, self.stage_two), (3, self.stage_sib)):
+        for lag, stage in ((0, self.stage_z), (-AHEAD, self.stage_own), (LAGS[0], self.stage_one), (LAGS[1], self.stage_two), (LAGS[2], self.stage_sib)):
             if 0 <= i - lag < 12:
                 stage(i - lag)
 
     def finish(self):
+        p = self.p
         for t in range(12):
+            single, view = self.one(t, p.z, p.quad), self.four(t, p.quad, p.c)
             for k in self.steps(t):
-                self.copy(self.shard(t), self.one(t, self.p.z), t, k, self.p.sib()).wait_send()
-            view = self.four(t, self.p.quad, self.p.c)
+                self.copy(single, single, t, k, p.sib()).wait_send()
             for k in (4, 5, 6, 8, 9, 10, 11):
-                self.copy(view, view, t, k, self.p.sib()).wait_send()
+                shape = single if k == 4 and not self.direct(t) else view
+                self.copy(shape, shape, t, k, p.sib()).wait_send()
+            for k in () if self.direct(t) else (12, 13, 14):
+                self.copy(single, single, t, k, p.sib()).wait_send()
 
 
 def expand_vectors(shards, vec):
-    def split(size, shape, axis):
-        at = wide(lax.broadcasted_iota(jnp.int32, shape, axis))
-        which = jnp.floor((at + 0.5) * (1.0 / size))
-        return which, at - which * size
-
-    lane, _ = split(48, (1, 640), 1)
-    spread = jnp.concatenate([jnp.where(lane == i, shards, 0.0) for i in range(8)])
-    _, at_row = split(48, (640, 1), 0)
-    owner, at_col = split(48, (1, 768), 1)
-    rows = dot(low(spread), low(jnp.where(at_row == at_col, 1.0, 0.0)))
-    own = wide(lax.broadcasted_iota(jnp.int32, (16, 1), 0))
-    for i in range(8):
-        vec[i : i + 1, :768] = jnp.sum(jnp.where(owner == own, rows[16 * i : 16 * i + 16], 0.0), axis=0, keepdims=True)
-    at_row = wide(lax.broadcasted_iota(jnp.int32, (256, 1), 0))
+    at = wide(lax.broadcasted_iota(jnp.int32, (1, 768), 1))
+    owner = jnp.floor((at + 0.5) * (1.0 / 48))
+    lane = wide(lax.broadcasted_iota(jnp.int32, (128, 1), 0))
+    rows = dot(shards.reshape(256, 128), low(jnp.where(lane == at - owner * 48, 1.0, 0.0))).reshape(16, 16, 768)
+    shard = wide(lax.broadcasted_iota(jnp.int32, (16, 1, 1), 0))
+    vec[:8, :768] = jnp.sum(jnp.where(owner[None] == shard, rows[:, :8], 0.0), axis=0)
+    piece = wide(lax.broadcasted_iota(jnp.int32, (4, 4, 1), 0) * 4 + lax.broadcasted_iota(jnp.int32, (4, 4, 1), 1))
     for n in range(4):
-        owner, at_col = split(192, (1, 768), 1)
-        rows = dot(low(shards[:, 384:]), low(jnp.where(at_row == at_col, 1.0, 0.0)))
-        vec[8:9, n * 768 : (n + 1) * 768] = jnp.sum(jnp.where(owner + 4.0 * n == own, rows, 0.0), axis=0, keepdims=True)
-
-
-def forward_kernel(inner, seq, lengths, v_shard, targets, w_query, w_key, w_value, w_output, w_inner, w_outer, query_tokens, passage_tokens,
+        mine = jnp.sum(jnp.where(owner[None] == piece, rows[4 * n : 4 * n + 4, 8:12], 0.0), axis=0)
+        vec[8:9, n * 768 : (n + 1) * 768] = jnp.sum(mine, axis=0, keepdims=True)
+
+
+def forward_kernel(inner, seq, lengths, targets, b_query, b_value, b_output, b_outer, gain_one, shift_one, gain_two, shift_two, b_inner, w_query, w_key, w_value, w_output, w_inner, w_outer, query_tokens, passage_tokens,
                    d_pool, loss, lens, vec, wa_out, wi_out, wo_out,
                    k_out, v_out, prob_out, prob_q_out, x_t_out, q_t_out, ctx_t_out, norm_t_out, act_t_out, slope_out, y1_out, r1_out, y2_out, r2_out,
-                   wa, wi, wo, x, q, k, v, prob, prob_q, ctx, normed, act, act_t, slope, x_t, q_t, ctx_t, norm_t, y1, r1, y2, r2, pooled, rows, vectors, len_buf,
+                   wa, wi, wo, x, q, k, v, prob, prob_q, ctx, normed, act, act_t, slope, x_t, q_t, ctx_t, norm_t, y1, r1, y2, r2, pooled, rows, packed, vectors, len_buf,
                    ssem, rsem, lsem, vsem, osem, psem, xsem):
     p = Place(inner)
-    pairs = targets.shape[0]
+    pairs = targets.shape[1]
     me = lax.axis_index("dp") * 2 + p.c
 
     def device(at):
@@ -226,7 +246,13 @@
         pl.semaphore_signal(barrier, inc=1, device_id=device(lax.rem(me + i, pairs)), device_id_type=MESH)
     lane = lax.broadcasted_iota(jnp.int32, (8, 128), 1)
     len_buf[p.c] = jnp.where(lane == 0, lengths[0, 0].astype(jnp.float32), lengths[0, 1].astype(jnp.float32))
-    vectors[p.z, p.quad] = v_shard[...]
+    packed[...] = jnp.zeros((16, 128), jnp.float32)
+    for i, ref in enumerate((b_query, b_value, b_output, b_outer, gain_one, shift_one, gain_two, shift_two)):
+        packed[i : i + 1, :48] = wide(ref[...])
+    last = wide(b_inner[...]).reshape(1, 192)
+    for i in range(4):
+        packed[8 + i : 9 + i, :48] = last[:, i * 48 : i * 48 + 48]
+    vectors[p.z, p.quad] = low(packed[...])
     pl.semaphore_wait(barrier, pairs - 1)
 
     gather = Gather(p, (w_query, w_key, w_value, w_output, w_inner, w_outer), wa, wi, wo, ssem, rsem, lsem)
@@ -261,10 +287,11 @@
     gather.tick(1)
     vector(4, p.q1, p.sib()).wait_recv()
     vector(6, p.q1, p.n2()).start()
-    gather.tick(2)
+    for i in range(2, LAGS[2]):
+        gather.tick(i)
     vector(5, p.q2, p.sib()).wait_recv()
     vector(6, p.q12, p.sib()).wait_recv()
-    expand_vectors(jnp.concatenate([vectors[i // 4, i % 4] for i in range(16)]), vec)
+    expand_vectors(vectors[...], vec)
     remote(len_buf.at[1 - p.c], len_buf.at[1 - p.c], xsem.at[2], xsem.at[3], p.sib()).wait_recv()
     len_q, len_p = [jnp.sum(jnp.where(lane[:1] == p.c, len_buf[i, 0:1], 0.0), axis=1, keepdims=True) for i in range(2)]
     lens[0:1] = jnp.broadcast_to(len_p, (1, 128))
@@ -280,14 +307,14 @@
                 acc = acc + vec[row : row + 1, cols]
             out[:, cols] = low(acc)
 
-    gather.tick(3)
+    gather.tick(LAGS[2] + 0)
     project(0, q, 0)
-    gather.tick(4)
+    gather.tick(LAGS[2] + 1)
     project(1, k, None)
     q_t[...] = q[...].T
     save(q_t, q_t_out)
     save(k, k_out)
-    gather.tick(5)
+    gather.tick(LAGS[2] + 2)
     project(2, v, 1)
     save(v, v_out)
 
@@ -326,12 +353,12 @@
                     ctx[start + r : start + r + rb, cols] = low(total)
             store_prob(j).start()
 
-    gather.tick(6)
+    gather.tick(LAGS[2] + 3)
     save(wa, wa_out)
     attention(0, 2)
-    gather.tick(7)
+    gather.tick(LAGS[2] + 4)
     attention(2, 4)
-    gather.tick(8)
+    gather.tick(LAGS[2] + 5)
     attention(4, 6)
     save(prob_q, prob_q_out)
     ctx_t[...] = ctx[...].T
@@ -364,9 +391,9 @@
             act[:, cols] = low(u * cdf)
             slope[:, cols] = low(cdf + u * (0.3989422804014327 * jnp.exp(-0.5 * u * u)))
 
-    gather.tick(9)
+    gather.tick(LAGS[2] + 6)
     hidden(0, 9)
-    gather.tick(10)
+    gather.tick(LAGS[2] + 7)
     save(wi, wi_out)
     hidden(9, 12)
     save(slope, slope_out)
@@ -405,11 +432,8 @@
                 pooled[row : row + 1] += jnp.sum(jnp.where(keep, out, 0.0), axis=0, keepdims=True)
 
     for i in range(4):
-        gather.tick(11 + i)
+        gather.tick(LAGS[2] + 8 + i)
         outer(i)
-    save(y2, y2_out)
-    save(r2, r2_out)
-    save(wo, wo_out)
 
     mine = jnp.concatenate([pooled[0:1] / len_q, pooled[1:2] / len_p])
     root = jnp.sqrt(jnp.sum(mine * mine, axis=1, keepdims=True) + 1e-6)
@@ -419,43 +443,47 @@
     @pl.loop(1, pairs)
     def _(i):
         remote(rows.at[me], rows.at[me], xsem.at[4], xsem.at[5], device(lax.rem(me + i, pairs))).start()
+    save(y2, y2_out)
+    save(r2, r2_out)
+    save(wo, wo_out)
+    gather.finish()
+    len_copy.wait_send()
+    for i in range(1, 7):
+        vector(i, p.quad, p.sib()).wait_send()
+    store_prob(4).wait()
+    store_prob(5).wait()
     rest = rows.at[pl.ds(0, pairs - 1)]
     remote(rest, rest, xsem.at[4], xsem.at[5], p.sib()).wait_recv()
     exact = lax.Precision.HIGHEST
     qs, ps = rows[:, 0, :], rows[:, 1, :]
-    logits = lax.dot_general(qs, ps, (((1,), (1,)), ((), ())), precision=exact, preferred_element_type=jnp.float32) / 0.01
-    hit = targets[...] == lax.broadcasted_iota(jnp.int32, (pairs, pairs), 1)
-    top = jnp.max(logits, axis=1, keepdims=True)
-    lse = jnp.log(jnp.sum(jnp.exp(logits - top), axis=1, keepdims=True)) + top
-    picked = jnp.sum(jnp.where(hit, logits, 0.0), axis=1, keepdims=True)
-    loss[...] = jnp.broadcast_to(jnp.sum(lse - picked, axis=0, keepdims=True) / pairs, loss.shape)
+    logits = lax.dot_general(ps, qs, (((1,), (1,)), ((), ())), precision=exact, preferred_element_type=jnp.float32) / 0.01
+    hit = targets[...] == lax.broadcasted_iota(jnp.int32, (pairs, pairs), 0)
+    top = jnp.max(logits, axis=0, keepdims=True)
+    lse = jnp.log(jnp.sum(jnp.exp(logits - top), axis=0, keepdims=True)) + top
+    picked = jnp.sum(jnp.where(hit, logits, 0.0), axis=0, keepdims=True)
+    loss[...] = jnp.broadcast_to(jnp.sum(lse - picked, axis=1, keepdims=True) / pairs, loss.shape)
     d_logits = seq * (jnp.exp(logits - lse) - jnp.where(hit, 1.0, 0.0))
-    d_q = jnp.dot(d_logits, ps, precision=exact, preferred_element_type=jnp.float32) / 0.01
-    d_p = lax.dot_general(d_logits, qs, (((0,), (0,)), ((), ())), precision=exact, preferred_element_type=jnp.float32) / 0.01
+    d_p = jnp.dot(d_logits, qs, precision=exact, preferred_element_type=jnp.float32) / 0.01
+    d_q = lax.dot_general(d_logits, ps, (((0,), (0,)), ((), ())), precision=exact, preferred_element_type=jnp.float32) / 0.01
     own = lax.broadcasted_iota(jnp.int32, (pairs, 1), 0) == me
     for row, d in enumerate((d_q, d_p)):
         d_unit = jnp.sum(jnp.where(own, d, 0.0), axis=0, keepdims=True)
         u = unit[row : row + 1]
         d_pool[row : row + 1] = (d_unit - u * jnp.sum(u * d_unit, axis=1, keepdims=True)) / root[row : row + 1]
-
     remote(rest, rest, xsem.at[4], xsem.at[5], p.sib()).wait_send()
-    gather.finish()
-    len_copy.wait_send()
-    for i in range(1, 7):
-        vector(i, p.quad, p.sib()).wait_send()
     for copy in saves:
         copy.wait()
-    store_prob(4).wait()
-    store_prob(5).wait()
 
 
 AHEAD = 2
-
-
-def forward_call(inner, seq, lengths, v_shard, targets, weights, query_tokens, passage_tokens, cid=0):
+LAGS = (1, 3, 4)
+TURNED = ()
+
+
+def forward_call(inner, seq, lengths, targets, vectors, weights, query_tokens, passage_tokens, cid=0):
     bf, f32 = jnp.bfloat16, jnp.float32
     sds, vmem, dma = jax.ShapeDtypeStruct, pltpu.VMEM, pltpu.SemaphoreType.DMA
-    pairs = targets.shape[0]
+    pairs = targets.shape[1]
     stored = [((T, 768), bf)] * 2 + [((12, S, S), bf), ((12, Q, Q), bf)] + [((768, T), bf)] * 4 + [
         ((3072, T), bf), ((T, 3072), bf), ((T, 768), f32), ((T, 1), f32), ((T, 768), f32), ((T, 1), f32)]
     full = [((4, 4, 4, 48, 768), bf), ((4, 4, 48, 3072), bf), ((4, 4, 192, 768), bf)]
@@ -464,17 +492,17 @@
     scratch = [vmem(*w) for w in full] + [vmem(rows, bf)] * 4 + [vmem((2, 2, S, S), bf), vmem((12, Q, Q), bf)] + [vmem(rows, bf)] * 2
     scratch += [vmem((T, 3072), bf), vmem((3072, T), bf), vmem((T, 3072), bf)] + [vmem((768, T), bf)] * 4
     scratch += [vmem(rows, f32), vmem((T, 1), f32), vmem(rows, f32), vmem((T, 1), f32), vmem((2, 768), f32)]
-    scratch += [vmem((pairs, 2, 768), f32), vmem((4, 4, 1, 640), f32), vmem((2, 8, 128), f32)]
-    scratch += [dma((12, 12)), dma((12, 12)), dma((9,)), dma((2, 7)), dma((17,)), dma((2,)), dma((6,))]
+    scratch += [vmem((pairs, 2, 768), f32), vmem((16, 128), f32), vmem((4, 4, 16, 128), bf), vmem((2, 8, 128), f32)]
+    scratch += [dma((12, 16)), dma((12, 16)), dma((9,)), dma((2, 7)), dma((17,)), dma((2,)), dma((6,))]
     return pl.pallas_call(
         functools.partial(forward_kernel, inner, seq),
         out_shape=[sds(*o) for o in outs],
-        in_specs=[pl.BlockSpec(memory_space=pltpu.SMEM), VM, VM] + [ANY] * 8,
+        in_specs=[pl.BlockSpec(memory_space=pltpu.SMEM)] + [VM] * 10 + [ANY] * 8,
         out_specs=[VM] * 4 + [ANY] * 17,
         scratch_shapes=scratch,
         compiler_params=pltpu.CompilerParams(collective_id=cid, has_side_effects=True, vmem_limit_bytes=62 << 20),
         name="layer_forward",
-    )(lengths, v_shard, targets, *weights, query_tokens, passage_tokens)
+    )(lengths, targets, *vectors, *weights, query_tokens, passage_tokens)
 
 
 class Scatter:
@@ -557,7 +585,7 @@
 
 def backward_kernel(inner, lens, d_pool, vec, a_hbm, i_hbm, o_hbm, k_hbm, v_hbm, prob_hbm, prob_q_hbm, x_t_hbm, q_t_hbm, ctx_t_hbm, norm_t_hbm,
                     act_t_hbm, slope_hbm, y1_hbm, r1_hbm, y2_hbm, r2_hbm,
-                    dx_out, dvec_out, g_query, g_key, g_value, g_output, g_inner, g_outer,
+                    dxq_out, dxp_out, dvec_out, g_query, g_key, g_value, g_output, g_inner, g_outer,
                     wa, wi, act_t, slope, d_inner, y, scale_one, scale_two, d_second, d_low, norm_t, ctx_t, x_t, q_t, k, v, prob, prob_q, ds_buf,
                     d_vec, v_in, v_out, stage, r0, acc, r1, r2, r3, ssem, rsem, lsem, psem, vsem, xsem):
     p = Place(inner)
@@ -785,10 +813,11 @@
         for i in range(3):
             d = d + dot_nt(d_inner[rows, part(i)], wa[i])
         d_low[rows] = low(d)
-    mine = pltpu.make_async_copy(d_low, dx_out.at[p.c], xsem.at[0])
-    theirs = remote(d_low, dx_out.at[p.c], xsem.at[1], xsem.at[2], p.sib())
-    mine.start()
-    theirs.start()
+    tokens = [(d_low.at[pl.ds(0, S)], dxp_out), (d_low.at[pl.ds(S, Q)], dxq_out)]
+    mine = [pltpu.make_async_copy(src, out.at[p.c], xsem.at[i]) for i, (src, out) in enumerate(tokens)]
+    theirs = [remote(src, out.at[p.c], xsem.at[2 + i], xsem.at[4 + i], p.sib()) for i, (src, out) in enumerate(tokens)]
+    for copy in mine + theirs:
+        copy.start()
     sc.stage0(11)
     v_out[0] = d_vec[:, sc.own] + vector_recv(0)
     vector(1, v_out.at[0], p.n2()).start()
@@ -813,9 +842,10 @@
     sc.stage2(11)
     for e in range(8, 12):
         sc.stage3(e)
-    mine.wait()
-    theirs.wait_send()
-    remote(dx_out.at[1 - p.c], dx_out.at[1 - p.c], xsem.at[1], xsem.at[2], p.sib()).wait_recv()
+    for i, (src, out) in enumerate(tokens):
+        mine[i].wait()
+        theirs[i].wait_send()
+        remote(out.at[1 - p.c], out.at[1 - p.c], xsem.at[2 + i], xsem.at[4 + i], p.sib()).wait_recv()
     remote(dvec_out.at[:, sc.other], dvec_out.at[:, sc.other], vsem.at[0, 6], vsem.at[1, 6], p.sib()).wait_recv()
     last.wait_send()
     for i in range(6):
@@ -826,7 +856,7 @@
 def backward_call(inner, lens, d_pool, vec, wa, wi, wo, saved, cid=1):
     bf, f32 = jnp.bfloat16, jnp.float32
     sds = jax.ShapeDtypeStruct
-    outs = [sds((2, T, 768), bf), sds((16, 768), f32)] + [sds((48, 768), f32)] * 4 + [sds((48, 3072), f32), sds((192, 768), f32)]
+    outs = [sds((2, Q, 768), bf), sds((2, S, 768), bf), sds((16, 768), f32)] + [sds((48, 768), f32)] * 4 + [sds((48, 3072), f32), sds((192, 768), f32)]
     vmem = pltpu.VMEM
     scratch = [
         vmem((4, 768, 768), bf), vmem((768, 3072), bf), vmem((3072, T), bf), vmem((T, 3072), bf), vmem((T, 3072), bf),
@@ -835,16 +865,63 @@
     scratch += [vmem((2, 2, S, S), bf), vmem((12, Q, Q), bf), vmem((2, S, S), bf), vmem((16, 768), f32), vmem((6, 16, 384), f32), vmem((3, 16, 384), f32)]
     scratch += [vmem((2, 4, 4, 48, 768), bf), vmem((4, 4, 4, 48, 384), bf), vmem((12, 4, 4, 48, 384), bf), vmem((12, 2, 4, 48, 384), bf), vmem((12, 4, 48, 384), bf), vmem((12, 3, 48, 384), bf)]
     dma = pltpu.SemaphoreType.DMA
-    scratch += [dma((12, 8)), dma((12, 8)), dma((19,)), dma((2,)), dma((2, 7)), dma((3,))]
+    scratch += [dma((12, 8)), dma((12, 8)), dma((19,)), dma((2,)), dma((2, 7)), dma((6,))]
     return pl.pallas_call(
         functools.partial(backward_kernel, inner),
         out_shape=outs,
         in_specs=[VM] * 3 + [ANY] * 17,
-        out_specs=[ANY] + [VM] * 7,
+        out_specs=[ANY] * 2 + [VM] * 7,
         scratch_shapes=scratch,
         compiler_params=pltpu.CompilerParams(collective_id=cid, has_side_effects=True, vmem_limit_bytes=63 << 20),
         name="layer_backward",
     )(lens, d_pool, vec, wa, wi, wo, *saved)
+
+
+def outputs_kernel(inner, loss_in, dxq, dxp, d_vec, *refs):
+    grads, (loss, q_out, p_out), g_outs, v_outs = refs[:6], refs[6:9], refs[9:15], refs[15:24]
+    q_low, p_low, q_wide, p_wide, isem, osem, gsem = refs[24:]
+    copies = [pltpu.make_async_copy(src, dst, gsem.at[i]) for i, (src, dst) in enumerate(zip(grads, g_outs))]
+    parts = [(dxp.at[i, pl.ds(r, 256)], p_low.at[i, pl.ds(r, 256)], p_wide.at[i, pl.ds(r, 256)], p_out.at[i, pl.ds(r, 256)]) for i in range(2) for r in (0, 256)]
+    parts.append((dxq, q_low, q_wide, q_out))
+    loads = [pltpu.make_async_copy(part[0], part[1], isem.at[i]) for i, part in enumerate(parts)]
+    for copy in loads + copies:
+        copy.start()
+    loss[...] = loss_in[0:1, 0:1]
+    shard = lax.axis_index("dp") // inner
+    for size, first, outs in ((48, 0, v_outs[:8]), (192, 8, v_outs[8:])):
+        at = lax.broadcasted_iota(jnp.int32, (768, 1), 0) - lax.rem(shard * size, 768)
+        pick = jnp.where(at == lax.broadcasted_iota(jnp.int32, (1, size), 1), 1.0, 0.0)
+        rows = d_vec[0:8] if size == 48 else d_vec[8:16]
+        mine = jnp.dot(rows, pick, precision=lax.Precision.HIGHEST, preferred_element_type=jnp.float32)
+        if size == 48:
+            for i in range(8):
+                outs[i][...] = mine[i : i + 1]
+        else:
+            row = lax.broadcasted_iota(jnp.int32, (8, 1), 0)
+            outs[0][...] = jnp.sum(jnp.where(row == shard // 4, mine, 0.0), axis=0, keepdims=True)
+    stores = []
+    for i, (_, source, wider, out) in enumerate(parts):
+        loads[i].wait()
+        wider[...] = wide(source[...])
+        stores.append(pltpu.make_async_copy(wider, out, osem.at[i]))
+        stores[-1].start()
+    for copy in stores + copies:
+        copy.wait()
+
+
+def outputs_call(inner, loss, dxq, dxp, d_vec, grads):
+    sds, f32, vmem, dma = jax.ShapeDtypeStruct, jnp.float32, pltpu.VMEM, pltpu.SemaphoreType.DMA
+    outs = [sds((1, 1), f32), sds(dxq.shape, f32), sds(dxp.shape, f32)] + [sds(g.shape, f32) for g in grads]
+    outs += [sds((1, 48), f32)] * 8 + [sds((1, 192), f32)]
+    return pl.pallas_call(
+        functools.partial(outputs_kernel, inner),
+        out_shape=outs,
+        in_specs=[VM, ANY, ANY, VM] + [VM] * 6,
+        out_specs=[VM] + [ANY] * 8 + [VM] * 9,
+        scratch_shapes=[vmem(dxq.shape, dxq.dtype), vmem(dxp.shape, dxp.dtype), vmem(dxq.shape, f32), vmem(dxp.shape, f32), dma((5,)), dma((5,)), dma((6,))],
+        compiler_params=pltpu.CompilerParams(vmem_limit_bytes=62 << 20),
+        name="write_outputs",
+    )(loss, dxq, dxp, d_vec, *grads)
 
 
 def per_device(
@@ -855,7 +932,6 @@
 ):
     inner = lax.axis_size("dp") // 16
     groups = None if inner == 1 else [[h * inner + i for i in range(inner)] for h in range(16)]
-    at = lax.axis_index("dp") // inner
     seq = passage_tokens.shape[1]
 
     def fetch(w):
@@ -865,23 +941,22 @@
 
     weights = [fetch(w) for w in (query_weight, key_weight, value_weight, output_weight, inner_weight, outer_weight)]
     vectors = (query_bias, value_bias, output_bias, outer_bias, first_gain, first_shift, second_gain, second_shift, inner_bias)
-    v_shard = jnp.concatenate([fetch(w) for w in vectors] + [jnp.zeros((64,), query_bias.dtype)])
+    vectors = [fetch(w)[None] for w in vectors[:8]] + [fetch(inner_bias)]
     d_pool, loss, lens, vec, wa, wi, wo, *saved = forward_call(
-        inner, float(seq), lengths, v_shard.astype(jnp.float32)[None], positives[:, None], weights, query_tokens, passage_tokens)
+        inner, float(seq), lengths, positives[None], vectors, weights, query_tokens, passage_tokens)
     wa, wi, wo = wa.reshape(4, 768, 768), wi.reshape(768, 3072), wo.reshape(3072, 768)
-    d_x, d_vec, *grads = backward_call(inner, lens, d_pool, vec, wa, wi, wo, saved)
+    dxq, dxp, d_vec, *grads = backward_call(inner, lens, d_pool, vec, wa, wi, wo, saved)
+    loss, dxq, dxp, *grads = outputs_call(inner, loss, dxq, dxp, d_vec, grads)
+    grads = [g.reshape(-1) if g.shape[0] == 1 else g for g in grads]
 
     def finish(x):
         if groups is None:
             return x
         return lax.psum_scatter(x, "dp", scatter_dimension=0, tiled=True, axis_index_groups=groups)
 
-    d_x = d_x.astype(jnp.float32)
-    flat = lax.dynamic_slice_in_dim(d_vec[:8], at * 48, 48, 1)
-    wide_bias = lax.dynamic_slice_in_dim(d_vec[8:12].reshape(3072), at * 192, 192, 0)
-    rows = [finish(flat[i]) for i in range(8)]
-    tail = [rows[0], rows[1], rows[2], finish(wide_bias)] + rows[3:]
-    return (loss[0, 0], d_x[:, seq:], d_x[:, :seq]) + tuple(finish(g) for g in grads) + tuple(tail)
+    grads = [finish(g) for g in grads]
+    flat = grads[6:]
+    return (loss[0, 0], dxq, dxp, *grads[:6], flat[0], flat[1], flat[2], flat[8], *flat[3:8])
 
 
 def solution(mesh):

time: 201 us -> 187 us (0.930)
  local copies, waits for them, and re-layouts: 14.8 us -> 0 us
    slice x5 -> x0, local copies, waits for them, and re-layouts: 6.36 us -> none  [the longest x1 3.43 us: per_device(): d_x[:, :seq]]
    pallas_call x0 -> x1, Pallas kernels: none -> 5.6 us  [outputs_call(): pl.pallas_call(functools.partial(outputs_kernel, inner), out_shape=outs,...]
    unnamed x20 -> x0, local copies, waits for them, and re-layouts: 4.3 us -> none
    pallas_call x1, Pallas kernels: 94.1 us -> 90.2 us  [forward_call(): pl.pallas_call(functools.partial(forward_kernel, inner, seq), out_shape=[...]
where the time goes in v4:
time: 187 us
  Pallas kernels  186 us (99%)
    pallas_call x1, Pallas kernels, forward_call(): pl.pallas_call(functools.partial(forward_kernel, inner, seq), out_shape=[...  90.2 us
    pallas_call x1, Pallas kernels, backward_call(): pl.pallas_call(functools.partial(backward_kernel, inner), out_shape=outs,...  90 us
    pallas_call x1, Pallas kernels, outputs_call(): pl.pallas_call(functools.partial(outputs_kernel, inner), out_shape=outs,...  5.6 us

profile of v4, /device:TPU:0, one launch (start us, length us, event | category | flops | bytes accessed | tf_op | source)
XLA Modules:
  0.0 186.6 jit_solution(9545574685430944838)
XLA Ops:
  0.7 90.2 %layer_forward.1 = (f32[2,768]{1,0:T(2,128)}, f32[8,128]{1,0:T(8,128)}, f32[8,128]{1,0:T(8,128)}, f32[16,3072]{1,0:T(8,128)}, bf16[4,4,4,48,768]{4,3,2,1,0:T(8,1...) custom-call(s32[1,2]{1,0:T(1,128)} %lengths.1, ...), custom_call_target="tpu_custom_call" | custom-call | tf_op jit(solution)/shard_map/layer_forward/pallas_call | solution.py:497
  90.9 90.0 %layer_backward.1 = (bf16[2,64,768]{2,1,0:T(8,128)(2,1)}, bf16[2,512,768]{2,1,0:T(8,128)(2,1)}, f32[16,768]{1,0:T(8,128)}, f32[48,768]{1,0:T(8,128)}, f32[48,768...) custom-call(f32[8,128]{1,0:T(8,128)} %get-tuple-element.67.lens, ...), custom_call_target="tpu_custom_call" | custom-call | tf_op jit(solution)/shard_map/layer_backward/pallas_call | solution.py:869
  180.9 5.6 %write_outputs.1 = (f32[1,1]{1,0:T(1,128)}, f32[2,64,768]{2,1,0:T(8,128)}, f32[2,512,768]{2,1,0:T(8,128)}, f32[48,768]{1,0:T(8,128)}, f32[48,768]{1,0:T(8,128)},...) custom-call(f32[8,128]{1,0:T(8,128)} %get-tuple-element.66.loss_in, ...), custom_call_target="tpu_custom_call" | custom-call | tf_op jit(solution)/shard_map/write_outputs/pallas_call | solution.py:916

commit v5 on v4

--- a/solution.py
+++ b/solution.py
@@ -224,12 +224,93 @@
         vec[8:9, n * 768 : (n + 1) * 768] = jnp.sum(mine, axis=0, keepdims=True)
 
 
-def forward_kernel(inner, seq, lengths, targets, b_query, b_value, b_output, b_outer, gain_one, shift_one, gain_two, shift_two, b_inner, w_query, w_key, w_value, w_output, w_inner, w_outer, query_tokens, passage_tokens,
-                   d_pool, loss, lens, vec, wa_out, wi_out, wo_out,
-                   k_out, v_out, prob_out, prob_q_out, x_t_out, q_t_out, ctx_t_out, norm_t_out, act_t_out, slope_out, y1_out, r1_out, y2_out, r2_out,
-                   wa, wi, wo, x, q, k, v, prob, prob_q, ctx, normed, act, act_t, slope, x_t, q_t, ctx_t, norm_t, y1, r1, y2, r2, pooled, rows, packed, vectors, len_buf,
-                   ssem, rsem, lsem, vsem, osem, psem, xsem):
-    p = Place(inner)
+AHEAD = 2
+LAGS = (1, 3, 4)
+TURNED = ()
+
+
+class Scatter:
+    def __init__(self, p, refs, result):
+        self.p = p
+        self.stage, self.r0, self.acc, self.r1, self.r2, self.r3, self.ssem, self.rsem = refs
+        self.result = result
+        self.own = pl.ds(pl.multiple_of(p.c * 384, 128), 384)
+        self.other = pl.ds(pl.multiple_of((1 - p.c) * 384, 128), 384)
+
+    def copy(self, src, dst, e, k, target):
+        return remote(src, dst, self.ssem.at[e, k], self.rsem.at[e, k], target)
+
+    def recv(self, e, k, ref):
+        self.copy(ref, ref, e, k, self.p.sib()).wait_recv()
+
+    def emit(self, e, left, right, extra=None):
+        if e >= 2:
+            self.shared(e - 2).wait_send()
+
+        @pl.loop(0, 3)
+        def _(n):
+            cols = block(n, 256)
+            values = right(cols)
+            self.stage[e % 2, :, :, :, cols] = low(dot(left(), values)).reshape(4, 4, 48, 256)
+            if extra is not None:
+                extra(cols, values)
+        self.shared(e).start()
+
+    def shared(self, e):
+        return self.copy(self.stage.at[e % 2, :, :, :, self.other], self.r0.at[e % 4], e, 0, self.p.sib())
+
+    def stage0(self, e):
+        p, acc = self.p, self.acc
+        self.recv(e, 0, self.r0.at[e % 4])
+        for j, q in enumerate((p.q2, p.q12, p.q1, p.quad)):
+            acc[e, :, q] = self.stage[e % 2, :, q, :, self.own] + self.r0[e % 4, :, q]
+            if j < 2:
+                self.copy(acc.at[e, :, q], self.r1.at[e, j], e, 1 + j, p.n2()).start()
+
+    def stage1(self, e):
+        p, acc = self.p, self.acc
+        self.recv(e, 2, self.r1.at[e, 1])
+        acc[e, :, p.q1] += self.r1[e, 1]
+        self.copy(acc.at[e, :, p.q1], self.r2.at[e], e, 3, p.n1()).start()
+        self.recv(e, 1, self.r1.at[e, 0])
+        acc[e, :, p.quad] += self.r1[e, 0]
+
+    def stage2(self, e):
+        p, acc = self.p, self.acc
+        self.recv(e, 3, self.r2.at[e])
+        acc[e, :, p.quad] += self.r2[e]
+        for k in range(1, 4):
+            self.copy(acc.at[e, p.ring(k), p.quad], self.r3.at[e, k - 1], e, 3 + k, p.up(k)).start()
+
+    def stage3(self, e):
+        p = self.p
+        total = wide(self.acc[e, p.z, p.quad])
+        for k in range(1, 4):
+            self.recv(e, 3 + k, self.r3.at[e, k - 1])
+            total = total + wide(self.r3[e, k - 1])
+        view = self.result(e, p.c)
+        view[...] = total
+        self.copy(view, view, e, 7, p.sib()).start()
+
+    def finish(self, count):
+        for e in range(count):
+            self.recv(e, 7, self.result(e, 1 - self.p.c))
+            self.copy(self.result(e, self.p.c), self.result(e, self.p.c), e, 7, self.p.sib()).wait_send()
+        for e in range(count - 2, count):
+            self.shared(e).wait_send()
+        four, one = self.r2.at[0], self.r3.at[0, 0]
+
+        @pl.loop(0, count)
+        def _(e):
+            for k in range(1, 7):
+                view = four if k < 4 else one
+                self.copy(view, view, e, k, self.p.sib()).wait_send()
+
+
+def forward_part(p, seq, lengths, targets, vector_shards, weights, query_tokens, passage_tokens, d_pool, loss, prob_out, vec, prob, prob_q,
+                 wa, wi, wo, x, q, k, v, act, act_t, slope, x_t, q_t, ctx_t, norm_t, y1, r1, y2, r2, pooled, rows, packed, vectors, len_buf,
+                 ssem, rsem, lsem, vsem, psem, xsem):
+    normed = q
     pairs = targets.shape[1]
     me = lax.axis_index("dp") * 2 + p.c
 
@@ -247,15 +328,15 @@
     lane = lax.broadcasted_iota(jnp.int32, (8, 128), 1)
     len_buf[p.c] = jnp.where(lane == 0, lengths[0, 0].astype(jnp.float32), lengths[0, 1].astype(jnp.float32))
     packed[...] = jnp.zeros((16, 128), jnp.float32)
-    for i, ref in enumerate((b_query, b_value, b_output, b_outer, gain_one, shift_one, gain_two, shift_two)):
+    for i, ref in enumerate(vector_shards[:8]):
         packed[i : i + 1, :48] = wide(ref[...])
-    last = wide(b_inner[...]).reshape(1, 192)
+    last = wide(vector_shards[8][...]).reshape(1, 192)
     for i in range(4):
         packed[8 + i : 9 + i, :48] = last[:, i * 48 : i * 48 + 48]
     vectors[p.z, p.quad] = low(packed[...])
     pl.semaphore_wait(barrier, pairs - 1)
 
-    gather = Gather(p, (w_query, w_key, w_value, w_output, w_inner, w_outer), wa, wi, wo, ssem, rsem, lsem)
+    gather = Gather(p, weights, wa, wi, wo, ssem, rsem, lsem)
     for t in range(AHEAD):
         gather.stage_own(t)
     len_copy = remote(len_buf.at[p.c], len_buf.at[p.c], xsem.at[2], xsem.at[3], p.sib())
@@ -267,17 +348,6 @@
 
     for i in range(1, 4):
         vector(i, None, p.up(i)).start()
-    saves = []
-
-    def save(src, dst):
-        copy = pltpu.make_async_copy(src, dst, osem.at[len(saves)])
-        copy.start()
-        saves.append(copy)
-
-    for copy in x_loads:
-        copy.wait()
-    x_t[...] = x[...].T
-    save(x_t, x_t_out)
     gather.tick(0)
     for i in range(1, 4):
         view = vectors.at[p.ring(4 - i), p.quad]
@@ -287,6 +357,9 @@
     gather.tick(1)
     vector(4, p.q1, p.sib()).wait_recv()
     vector(6, p.q1, p.n2()).start()
+    for copy in x_loads:
+        copy.wait()
+    x_t[...] = x[...].T
     for i in range(2, LAGS[2]):
         gather.tick(i)
     vector(5, p.q2, p.sib()).wait_recv()
@@ -294,9 +367,6 @@
     expand_vectors(vectors[...], vec)
     remote(len_buf.at[1 - p.c], len_buf.at[1 - p.c], xsem.at[2], xsem.at[3], p.sib()).wait_recv()
     len_q, len_p = [jnp.sum(jnp.where(lane[:1] == p.c, len_buf[i, 0:1], 0.0), axis=1, keepdims=True) for i in range(2)]
-    lens[0:1] = jnp.broadcast_to(len_p, (1, 128))
-    lens[1:2] = jnp.broadcast_to(len_q, (1, 128))
-    lens[2:8] = jnp.zeros((6, 128), jnp.float32)
 
     def project(m, out, row):
         @pl.loop(0, 3)
@@ -306,17 +376,6 @@
             if row is not None:
                 acc = acc + vec[row : row + 1, cols]
             out[:, cols] = low(acc)
-
-    gather.tick(LAGS[2] + 0)
-    project(0, q, 0)
-    gather.tick(LAGS[2] + 1)
-    project(1, k, None)
-    q_t[...] = q[...].T
-    save(q_t, q_t_out)
-    save(k, k_out)
-    gather.tick(LAGS[2] + 2)
-    project(2, v, 1)
-    save(v, v_out)
 
     def store_prob(j):
         return pltpu.make_async_copy(prob.at[lax.rem(j, 2)], prob_out.at[pl.ds(j * 2, 2)], psem.at[lax.rem(j, 2)])
@@ -350,19 +409,25 @@
                             prob_q[2 * j + h] = w
                         piece = dot(w, vp * mask)
                         total = piece if total is None else total + piece
-                    ctx[start + r : start + r + rb, cols] = low(total)
+                    act[start + r : start + r + rb, cols] = low(total)
             store_prob(j).start()
 
+    gather.tick(LAGS[2] + 0)
+    project(0, q, 0)
+    gather.tick(LAGS[2] + 1)
+    project(1, k, None)
+    q_t[...] = q[...].T
+    gather.tick(LAGS[2] + 2)
+    project(2, v, 1)
+    attention(0, 1)
+
     gather.tick(LAGS[2] + 3)
-    save(wa, wa_out)
-    attention(0, 2)
+    attention(1, 3)
     gather.tick(LAGS[2] + 4)
-    attention(2, 4)
+    attention(3, 5)
     gather.tick(LAGS[2] + 5)
-    attention(4, 6)
-    save(prob_q, prob_q_out)
-    ctx_t[...] = ctx[...].T
-    save(ctx_t, ctx_t_out)
+    attention(5, 6)
+    ctx_t[...] = act[:, :768].T
 
     def gain(row):
         return vec[row : row + 1, :768]
@@ -370,17 +435,13 @@
     @pl.loop(0, 3)
     def _(n):
         span = block(n, 192)
-        first = wide(x[span]) + (dot(ctx[span], wa[3].reshape(768, 768)) + gain(2))
+        first = wide(x[span]) + (dot(act[span, :768], wa[3].reshape(768, 768)) + gain(2))
         center = first - jnp.mean(first, axis=1, keepdims=True)
         scale = lax.rsqrt(jnp.mean(center * center, axis=1, keepdims=True) + 1e-12)
         y = center * scale
         y1[span] = y
         r1[span] = scale
         normed[span] = low(y * gain(4) + gain(5))
-    save(y1, y1_out)
-    save(r1, r1_out)
-    norm_t[...] = normed[...].T
-    save(norm_t, norm_t_out)
 
     def hidden(low_n, high_n):
         @pl.loop(low_n, high_n)
@@ -392,20 +453,20 @@
             slope[:, cols] = low(cdf + u * (0.3989422804014327 * jnp.exp(-0.5 * u * u)))
 
     gather.tick(LAGS[2] + 6)
-    hidden(0, 9)
+    norm_t[...] = normed[...].T
+    hidden(0, 6)
     gather.tick(LAGS[2] + 7)
-    save(wi, wi_out)
-    hidden(9, 12)
-    save(slope, slope_out)
-
-    for b in range(4):
-        turned = act[:, b * 768 : (b + 1) * 768].T
-        for s in range(4):
-            for n in range(4):
-                row = n * 768 + (b * 4 + s) * 48
-                act_t[row : row + 48] = turned[s * 192 + n * 48 : s * 192 + n * 48 + 48]
-    save(act_t, act_t_out)
+    hidden(6, 12)
+
     pooled[...] = jnp.zeros_like(pooled)
+
+    def turn_act():
+        for b in range(4):
+            turned = act[:, b * 768 : (b + 1) * 768].T
+            for s in range(4):
+                for n in range(4):
+                    row = n * 768 + (b * 4 + s) * 48
+                    act_t[row : row + 48] = turned[s * 192 + n * 48 : s * 192 + n * 48 + 48]
 
     def outer(i):
         plane = p.ring(4 - i)
@@ -433,19 +494,19 @@
 
     for i in range(4):
         gather.tick(LAGS[2] + 8 + i)
+        if i == 0:
+            turn_act()
         outer(i)
 
     mine = jnp.concatenate([pooled[0:1] / len_q, pooled[1:2] / len_p])
     root = jnp.sqrt(jnp.sum(mine * mine, axis=1, keepdims=True) + 1e-6)
     unit = mine / root
-    rows[me] = unit
+    rows[me, :, :768] = unit[0:1]
+    rows[me, :, 768:] = unit[1:2]
 
     @pl.loop(1, pairs)
     def _(i):
         remote(rows.at[me], rows.at[me], xsem.at[4], xsem.at[5], device(lax.rem(me + i, pairs))).start()
-    save(y2, y2_out)
-    save(r2, r2_out)
-    save(wo, wo_out)
     gather.finish()
     len_copy.wait_send()
     for i in range(1, 7):
@@ -454,169 +515,43 @@
     store_prob(5).wait()
     rest = rows.at[pl.ds(0, pairs - 1)]
     remote(rest, rest, xsem.at[4], xsem.at[5], p.sib()).wait_recv()
-    exact = lax.Precision.HIGHEST
-    qs, ps = rows[:, 0, :], rows[:, 1, :]
-    logits = lax.dot_general(ps, qs, (((1,), (1,)), ((), ())), precision=exact, preferred_element_type=jnp.float32) / 0.01
+    step = 768 if pairs <= 64 else 128
+    logits = None
+    for at in range(0, 768, step):
+        part = lax.dot_general(
+            rows[:, 0, 768 + at : 768 + at + step], rows[:, 0, at : at + step], (((1,), (1,)), ((), ())),
+            precision=lax.Precision.HIGHEST, preferred_element_type=jnp.float32)
+        logits = part if logits is None else logits + part
+    logits = logits / 0.01
     hit = targets[...] == lax.broadcasted_iota(jnp.int32, (pairs, pairs), 0)
     top = jnp.max(logits, axis=0, keepdims=True)
     lse = jnp.log(jnp.sum(jnp.exp(logits - top), axis=0, keepdims=True)) + top
     picked = jnp.sum(jnp.where(hit, logits, 0.0), axis=0, keepdims=True)
     loss[...] = jnp.broadcast_to(jnp.sum(lse - picked, axis=1, keepdims=True) / pairs, loss.shape)
     d_logits = seq * (jnp.exp(logits - lse) - jnp.where(hit, 1.0, 0.0))
-    d_p = jnp.dot(d_logits, qs, precision=exact, preferred_element_type=jnp.float32) / 0.01
-    d_q = lax.dot_general(d_logits, ps, (((0,), (0,)), ((), ())), precision=exact, preferred_element_type=jnp.float32) / 0.01
-    own = lax.broadcasted_iota(jnp.int32, (pairs, 1), 0) == me
-    for row, d in enumerate((d_q, d_p)):
-        d_unit = jnp.sum(jnp.where(own, d, 0.0), axis=0, keepdims=True)
+    across = lax.broadcasted_iota(jnp.int32, (pairs, pairs), 1)
+    down = lax.broadcasted_iota(jnp.int32, (pairs, pairs), 0)
+    for_q = jnp.sum(jnp.where(across == me, d_logits, 0.0), axis=1, keepdims=True)
+    for_p = jnp.sum(jnp.where(down == me, d_logits, 0.0), axis=0, keepdims=True)
+    for_p = jnp.sum(jnp.where(across == down, for_p, 0.0), axis=1, keepdims=True)
+    for row, weight in enumerate((for_q, for_p)):
+        d_unit = jnp.sum(weight * rows[:, 0, (1 - row) * 768 : (2 - row) * 768], axis=0, keepdims=True) / 0.01
         u = unit[row : row + 1]
         d_pool[row : row + 1] = (d_unit - u * jnp.sum(u * d_unit, axis=1, keepdims=True)) / root[row : row + 1]
     remote(rest, rest, xsem.at[4], xsem.at[5], p.sib()).wait_send()
-    for copy in saves:
-        copy.wait()
-
-
-AHEAD = 2
-LAGS = (1, 3, 4)
-TURNED = ()
-
-
-def forward_call(inner, seq, lengths, targets, vectors, weights, query_tokens, passage_tokens, cid=0):
-    bf, f32 = jnp.bfloat16, jnp.float32
-    sds, vmem, dma = jax.ShapeDtypeStruct, pltpu.VMEM, pltpu.SemaphoreType.DMA
-    pairs = targets.shape[1]
-    stored = [((T, 768), bf)] * 2 + [((12, S, S), bf), ((12, Q, Q), bf)] + [((768, T), bf)] * 4 + [
-        ((3072, T), bf), ((T, 3072), bf), ((T, 768), f32), ((T, 1), f32), ((T, 768), f32), ((T, 1), f32)]
-    full = [((4, 4, 4, 48, 768), bf), ((4, 4, 48, 3072), bf), ((4, 4, 192, 768), bf)]
-    outs = [((2, 768), f32), ((8, 128), f32), ((8, 128), f32), ((16, 3072), f32)] + full + stored
-    rows = (T, 768)
-    scratch = [vmem(*w) for w in full] + [vmem(rows, bf)] * 4 + [vmem((2, 2, S, S), bf), vmem((12, Q, Q), bf)] + [vmem(rows, bf)] * 2
-    scratch += [vmem((T, 3072), bf), vmem((3072, T), bf), vmem((T, 3072), bf)] + [vmem((768, T), bf)] * 4
-    scratch += [vmem(rows, f32), vmem((T, 1), f32), vmem(rows, f32), vmem((T, 1), f32), vmem((2, 768), f32)]
-    scratch += [vmem((pairs, 2, 768), f32), vmem((16, 128), f32), vmem((4, 4, 16, 128), bf), vmem((2, 8, 128), f32)]
-    scratch += [dma((12, 16)), dma((12, 16)), dma((9,)), dma((2, 7)), dma((17,)), dma((2,)), dma((6,))]
-    return pl.pallas_call(
-        functools.partial(forward_kernel, inner, seq),
-        out_shape=[sds(*o) for o in outs],
-        in_specs=[pl.BlockSpec(memory_space=pltpu.SMEM)] + [VM] * 10 + [ANY] * 8,
-        out_specs=[VM] * 4 + [ANY] * 17,
-        scratch_shapes=scratch,
-        compiler_params=pltpu.CompilerParams(collective_id=cid, has_side_effects=True, vmem_limit_bytes=62 << 20),
-        name="layer_forward",
-    )(lengths, targets, *vectors, *weights, query_tokens, passage_tokens)
-
-
-class Scatter:
-    def __init__(self, p, refs, result):
-        self.p = p
-        self.stage, self.r0, self.acc, self.r1, self.r2, self.r3, self.ssem, self.rsem = refs
-        self.result = result
-        self.own = pl.ds(pl.multiple_of(p.c * 384, 128), 384)
-        self.other = pl.ds(pl.multiple_of((1 - p.c) * 384, 128), 384)
-
-    def copy(self, src, dst, e, k, target):
-        return remote(src, dst, self.ssem.at[e, k], self.rsem.at[e, k], target)
-
-    def recv(self, e, k, ref):
-        self.copy(ref, ref, e, k, self.p.sib()).wait_recv()
-
-    def emit(self, e, left, right, extra=None):
-        if e >= 2:
-            self.shared(e - 2).wait_send()
-
-        @pl.loop(0, 3)
-        def _(n):
-            cols = block(n, 256)
-            values = right(cols)
-            self.stage[e % 2, :, :, :, cols] = low(dot(left(), values)).reshape(4, 4, 48, 256)
-            if extra is not None:
-                extra(cols, values)
-        self.shared(e).start()
-
-    def shared(self, e):
-        return self.copy(self.stage.at[e % 2, :, :, :, self.other], self.r0.at[e % 4], e, 0, self.p.sib())
-
-    def stage0(self, e):
-        p, acc = self.p, self.acc
-        self.recv(e, 0, self.r0.at[e % 4])
-        for j, q in enumerate((p.q2, p.q12, p.q1, p.quad)):
-            acc[e, :, q] = self.stage[e % 2, :, q, :, self.own] + self.r0[e % 4, :, q]
-            if j < 2:
-                self.copy(acc.at[e, :, q], self.r1.at[e, j], e, 1 + j, p.n2()).start()
-
-    def stage1(self, e):
-        p, acc = self.p, self.acc
-        self.recv(e, 2, self.r1.at[e, 1])
-        acc[e, :, p.q1] += self.r1[e, 1]
-        self.copy(acc.at[e, :, p.q1], self.r2.at[e], e, 3, p.n1()).start()
-        self.recv(e, 1, self.r1.at[e, 0])
-        acc[e, :, p.quad] += self.r1[e, 0]
-
-    def stage2(self, e):
-        p, acc = self.p, self.acc
-        self.recv(e, 3, self.r2.at[e])
-        acc[e, :, p.quad] += self.r2[e]
-        for k in range(1, 4):
-            self.copy(acc.at[e, p.ring(k), p.quad], self.r3.at[e, k - 1], e, 3 + k, p.up(k)).start()
-
-    def stage3(self, e):
-        p = self.p
-        total = wide(self.acc[e, p.z, p.quad])
-        for k in range(1, 4):
-            self.recv(e, 3 + k, self.r3.at[e, k - 1])
-            total = total + wide(self.r3[e, k - 1])
-        view = self.result(e, p.c)
-        view[...] = total
-        self.copy(view, view, e, 7, p.sib()).start()
-
-    def finish(self, count):
-        for e in range(count):
-            self.recv(e, 7, self.result(e, 1 - self.p.c))
-            self.copy(self.result(e, self.p.c), self.result(e, self.p.c), e, 7, self.p.sib()).wait_send()
-        for e in range(count - 2, count):
-            self.shared(e).wait_send()
-        four, one = self.r2.at[0], self.r3.at[0, 0]
-
-        @pl.loop(0, count)
-        def _(e):
-            for k in range(1, 7):
-                view = four if k < 4 else one
-                self.copy(view, view, e, k, self.p.sib()).wait_send()
-
-
-def backward_kernel(inner, lens, d_pool, vec, a_hbm, i_hbm, o_hbm, k_hbm, v_hbm, prob_hbm, prob_q_hbm, x_t_hbm, q_t_hbm, ctx_t_hbm, norm_t_hbm,
-                    act_t_hbm, slope_hbm, y1_hbm, r1_hbm, y2_hbm, r2_hbm,
-                    dxq_out, dxp_out, dvec_out, g_query, g_key, g_value, g_output, g_inner, g_outer,
-                    wa, wi, act_t, slope, d_inner, y, scale_one, scale_two, d_second, d_low, norm_t, ctx_t, x_t, q_t, k, v, prob, prob_q, ds_buf,
-                    d_vec, v_in, v_out, stage, r0, acc, r1, r2, r3, ssem, rsem, lsem, psem, vsem, xsem):
-    p = Place(inner)
-
-    def load(i, src, dst):
-        return pltpu.make_async_copy(src, dst, lsem.at[i])
-
-    loads = {
-        "y2": load(0, y2_hbm, y), "r2": load(1, r2_hbm, scale_two), "act_t": load(2, act_t_hbm, act_t),
-        "slope": load(7, slope_hbm, slope), "norm_t": load(8, norm_t_hbm, norm_t), "wi": load(9, i_hbm, wi),
-        "y1": load(10, y1_hbm, y), "r1": load(11, r1_hbm, scale_one), "ctx_t": load(12, ctx_t_hbm, ctx_t), "wa": load(13, a_hbm, wa),
-        "k": load(14, k_hbm, k), "v": load(15, v_hbm, v), "q_t": load(16, q_t_hbm, q_t), "x_t": load(17, x_t_hbm, x_t), "prob_q": load(18, prob_q_hbm, prob_q),
-    }
-    for n in range(4):
-        loads["wo%d" % n] = load(3 + n, o_hbm.at[pl.ds(n * 768, 768)], wa.at[n])
-
-    def start(*names):
-        for name in names:
-            loads[name].start()
-
-    def need(*names):
-        for name in names:
-            loads[name].wait()
+    return len_p, len_q
+
+
+def backward_part(p, len_p, len_q, d_pool, vec, prob_hbm, prob, prob_q, dxq_out, dxp_out, dvec_out, grads,
+                  wa, wi, wo, d_low, k, v, d_inner, act_t, slope, x_t, q_t, ctx_t, norm_t, y1, r1, d_second, r2, ds_buf,
+                  d_vec, v_in, v_out, chunks, psem, vsem, xsem):
+    g_query, g_key, g_value, g_output, g_inner, g_outer = grads
 
     def load_prob(j):
         return pltpu.make_async_copy(prob_hbm.at[pl.ds(j * 2, 2)], prob.at[lax.rem(j, 2)], psem.at[lax.rem(j, 2)])
 
-    start("y2", "r2", "act_t", "wo0", "wo1", "wo2", "wo3", "slope", "norm_t", "wi", "r1", "ctx_t", "k", "v", "q_t", "x_t", "prob_q")
     load_prob(0).start()
     load_prob(1).start()
-    p.barrier()
 
     def result(e, which):
         cols = pl.ds(pl.multiple_of(which * 384, 128), 384)
@@ -626,7 +561,7 @@
             return g_inner.at[:, pl.ds(pl.multiple_of((e - 4) * 768 + which * 384, 128), 384)]
         return (g_output, g_query, g_key, g_value)[e - 8].at[:, cols]
 
-    sc = Scatter(p, (stage, r0, acc, r1, r2, r3, ssem, rsem), result)
+    sc = Scatter(p, chunks, result)
     d_vec[...] = jnp.zeros_like(d_vec)
 
     def gain(row):
@@ -635,7 +570,6 @@
     def tally(row, value):
         d_vec[row : row + 1] += jnp.sum(value, axis=0, keepdims=True)
 
-    len_p, len_q = lens[0:1, 0:1], lens[1:2, 0:1]
     pool_q = d_pool[0:1] / len_q
     pool_p = d_pool[1:2] / len_p
 
@@ -648,18 +582,15 @@
         d_low[rows] = low(d)
         return d
 
-    need("y2", "r2")
 
     @pl.loop(0, 3)
     def _(n):
         rows = block(n, 192)
         at = wide(lax.broadcasted_iota(jnp.int32, (192, 1), 0) + n * 192)
         d_rows = jnp.where(at < S, jnp.where(at < len_p, pool_p, 0.0), jnp.where(at - S < len_q, pool_q, 0.0))
-        d = norm_back(d_rows, 6, y[rows], scale_two[rows], rows)
+        d = norm_back(d_rows, 6, d_second[rows], r2[rows], rows)
         tally(3, wide(low(d)))
 
-    start("y1")
-    need("act_t")
 
     def emit_outer(n):
         sc.emit(n, lambda: act_t[n * 768 : (n + 1) * 768], lambda cols: d_low[:, cols])
@@ -676,20 +607,17 @@
     sc.stage0(1)
     emit_outer(3)
     sc.stage0(2)
-    need("wo0", "wo1", "wo2", "wo3", "slope")
 
     def inner_back(low_n, high_n):
         @pl.loop(low_n, high_n)
         def _(n):
-            cols = block(n, 256)
-            d_inner[:, cols] = low(dot_nt(d_low[...], wa[n // 3, block(lax.rem(n, 3), 256)]) * wide(slope[:, cols]))
-
-    inner_back(0, 6)
+            cols = block(n, 768)
+            d_inner[:, cols] = low(dot_nt(d_low[...], wo[n].reshape(768, 768)) * wide(slope[:, cols]))
+
+    inner_back(0, 2)
     sc.stage0(3)
-    inner_back(6, 12)
-    start("wa")
     sc.stage1(0)
-    need("norm_t")
+    inner_back(2, 4)
     emit_inner(0)
     sc.stage1(1)
     emit_inner(1)
@@ -697,43 +625,41 @@
     sc.stage2(0)
     emit_inner(2)
     sc.stage0(5)
-    sc.stage1(2)
     emit_inner(3)
     sc.stage0(6)
+    sc.stage1(2)
     sc.stage2(1)
-    need("wi", "y1", "r1")
+
+    def first_back(low_n, high_n):
+        @pl.loop(low_n, high_n)
+        def _(n):
+            rows = block(n, 192)
+            d = norm_back(d_second[rows] + dot_nt(d_inner[rows], wi[...].reshape(768, 3072)), 4, y1[rows], r1[rows], rows)
+            tally(2, wide(low(d)))
+
+    first_back(0, 1)
+    sc.stage0(7)
+    first_back(1, 3)
+    sc.stage1(3)
+    sc.stage2(2)
+    sc.stage3(0)
+    sc.emit(8, lambda: ctx_t[...], lambda cols: d_low[:, cols])
+
+    def part(i):
+        return pl.ds(i * 768, 768)
+
+    def pair_cols(i, j):
+        return pl.ds(pl.multiple_of(i * 768 + j * 128, 128), 128)
+
+    def head_rows(i, head):
+        return pl.ds(pl.multiple_of(i * 768 + head * 64, 64), 64)
 
     @pl.loop(0, 3)
     def _(n):
         rows = block(n, 192)
-        d = norm_back(d_second[rows] + dot_nt(d_inner[rows], wi[...]), 4, y[rows], scale_one[rows], rows)
-        tally(2, wide(low(d)))
-
-    sc.stage0(7)
-    sc.stage1(3)
-    sc.stage2(2)
-    need("ctx_t", "wa")
-    sc.emit(8, lambda: ctx_t[...], lambda cols: d_low[:, cols])
-
-    def part(i):
-        return pl.ds(i * 768, 768)
-
-    def pair_cols(i, j):
-        return pl.ds(pl.multiple_of(i * 768 + j * 128, 128), 128)
-
-    def head_rows(i, head):
-        return pl.ds(pl.multiple_of(i * 768 + head * 64, 64), 64)
-
-    @pl.loop(0, 3)
-    def _(n):
-        rows = block(n, 192)
-        d_inner[rows, part(3)] = low(dot_nt(d_low[rows], wa[3]))
+        d_inner[rows, part(3)] = low(dot_nt(d_low[rows], wa[3].reshape(768, 768)))
     act_t[part(2)] = d_inner[:, part(3)].T
-    need("k", "v", "q_t", "prob_q")
     sc.stage0(8)
-    sc.stage1(4)
-    sc.stage2(3)
-    sc.stage3(0)
 
     def attention(low_j, high_j):
         @pl.loop(low_j, high_j)
@@ -767,20 +693,15 @@
                 load_prob(j + 2).start()
 
     attention(0, 2)
+    sc.stage1(4)
+    sc.stage2(3)
+    sc.stage3(1)
+    attention(2, 6)
     sc.stage1(5)
     sc.stage2(4)
-    sc.stage3(1)
-    attention(2, 4)
-    sc.stage1(6)
-    sc.stage2(5)
     sc.stage3(2)
-    attention(4, 6)
-    sc.stage1(7)
-    sc.stage2(6)
-    sc.stage3(3)
     d_inner[:, part(1)] = act_t[part(0)].T
     d_inner[:, part(2)] = act_t[part(1)].T
-    need("x_t")
 
     def emit_first(n):
         row = (0, None, 1)[n]
@@ -790,10 +711,10 @@
         sc.emit(9 + n, lambda: x_t[...], lambda cols: d_inner[:, pl.ds(pl.multiple_of(n * 768 + cols.start, 256), 256)], None if row is None else bias)
 
     emit_first(0)
-    sc.stage1(8)
     emit_first(1)
     sc.stage0(9)
     emit_first(2)
+    sc.stage0(10)
 
     def vector(i, src, target):
         return remote(src, v_in.at[i], vsem.at[0, i], vsem.at[1, i], target)
@@ -803,44 +724,50 @@
         return v_in[i]
 
     vector(0, d_vec.at[:, sc.other], p.sib()).start()
-    sc.stage0(10)
-    sc.stage2(7)
+    sc.stage1(6)
+    sc.stage2(5)
+    sc.stage3(3)
+    sc.stage0(11)
 
     @pl.loop(0, 3)
     def _(n):
         rows = block(n, 192)
         d = d_second[rows]
         for i in range(3):
-            d = d + dot_nt(d_inner[rows, part(i)], wa[i])
+            d = d + dot_nt(d_inner[rows, part(i)], wa[i].reshape(768, 768))
         d_low[rows] = low(d)
     tokens = [(d_low.at[pl.ds(0, S)], dxp_out), (d_low.at[pl.ds(S, Q)], dxq_out)]
     mine = [pltpu.make_async_copy(src, out.at[p.c], xsem.at[i]) for i, (src, out) in enumerate(tokens)]
     theirs = [remote(src, out.at[p.c], xsem.at[2 + i], xsem.at[4 + i], p.sib()) for i, (src, out) in enumerate(tokens)]
     for copy in mine + theirs:
         copy.start()
-    sc.stage0(11)
     v_out[0] = d_vec[:, sc.own] + vector_recv(0)
     vector(1, v_out.at[0], p.n2()).start()
+    sc.stage1(7)
+    sc.stage2(6)
     sc.stage3(4)
+    sc.stage1(8)
+    sc.stage2(7)
+    sc.stage3(5)
     sc.stage1(9)
+    sc.stage2(8)
+    sc.stage3(6)
     v_out[1] = v_out[0] + vector_recv(1)
     vector(2, v_out.at[1], p.n1()).start()
-    sc.stage2(8)
-    sc.stage3(5)
     sc.stage1(10)
+    sc.stage2(9)
+    sc.stage3(7)
+    sc.stage1(11)
     v_out[2] = v_out[1] + vector_recv(2)
     for i in range(1, 4):
         vector(2 + i, v_out.at[2], p.up(i)).start()
-    sc.stage2(9)
-    sc.stage3(6)
-    sc.stage1(11)
     sc.stage2(10)
-    sc.stage3(7)
+    sc.stage3(8)
+    sc.stage2(11)
     dvec_out[:, sc.own] = v_out[2] + vector_recv(3) + vector_recv(4) + vector_recv(5)
     last = remote(dvec_out.at[:, sc.own], dvec_out.at[:, sc.own], vsem.at[0, 6], vsem.at[1, 6], p.sib())
     last.start()
-    sc.stage2(11)
-    for e in range(8, 12):
+    for e in range(9, 12):
         sc.stage3(e)
     for i, (src, out) in enumerate(tokens):
         mine[i].wait()
@@ -853,28 +780,48 @@
     sc.finish(12)
 
 
-def backward_call(inner, lens, d_pool, vec, wa, wi, wo, saved, cid=1):
+def layer_kernel(inner, seq, lengths, targets, *refs):
+    vector_shards, weights, (query_tokens, passage_tokens) = refs[:9], refs[9:15], refs[15:17]
+    loss, dxq_out, dxp_out, dvec_out = refs[17:21]
+    grads, prob_hbm = refs[21:27], refs[27]
+    (wa, wi, wo, x, q, k, v, act, act_t, slope, x_t, q_t, ctx_t, norm_t, y1, r1, y2, r2, prob, prob_q, ds_buf, vec, d_pool, pooled,
+     rows, packed, vectors, len_buf, d_vec, v_in, v_out) = refs[28:59]
+    chunks, (g_ssem, g_rsem, g_lsem, g_vsem, psem, g_xsem, vsem, xsem) = refs[59:67], refs[67:75]
+    p = Place(inner)
+    len_p, len_q = forward_part(
+        p, seq, lengths, targets, vector_shards, weights, query_tokens, passage_tokens, d_pool, loss, prob_hbm, vec, prob, prob_q,
+        wa, wi, wo, x, q, k, v, act, act_t, slope, x_t, q_t, ctx_t, norm_t, y1, r1, y2, r2, pooled, rows, packed, vectors, len_buf,
+        g_ssem, g_rsem, g_lsem, g_vsem, psem, g_xsem)
+    backward_part(
+        p, len_p, len_q, d_pool, vec, prob_hbm, prob, prob_q, dxq_out, dxp_out, dvec_out, grads,
+        wa, wi, wo, x, k, v, act, act_t, slope, x_t, q_t, ctx_t, norm_t, y1, r1, y2, r2, ds_buf,
+        d_vec, v_in, v_out, chunks, psem, vsem, xsem)
+
+
+def layer_call(inner, seq, lengths, targets, vectors, weights, query_tokens, passage_tokens, cid=0):
     bf, f32 = jnp.bfloat16, jnp.float32
-    sds = jax.ShapeDtypeStruct
-    outs = [sds((2, Q, 768), bf), sds((2, S, 768), bf), sds((16, 768), f32)] + [sds((48, 768), f32)] * 4 + [sds((48, 3072), f32), sds((192, 768), f32)]
-    vmem = pltpu.VMEM
-    scratch = [
-        vmem((4, 768, 768), bf), vmem((768, 3072), bf), vmem((3072, T), bf), vmem((T, 3072), bf), vmem((T, 3072), bf),
-        vmem((T, 768), f32), vmem((T, 1), f32), vmem((T, 1), f32), vmem((T, 768), f32), vmem((T, 768), bf)]
-    scratch += [vmem((768, T), bf)] * 4 + [vmem((T, 768), bf)] * 2
-    scratch += [vmem((2, 2, S, S), bf), vmem((12, Q, Q), bf), vmem((2, S, S), bf), vmem((16, 768), f32), vmem((6, 16, 384), f32), vmem((3, 16, 384), f32)]
-    scratch += [vmem((2, 4, 4, 48, 768), bf), vmem((4, 4, 4, 48, 384), bf), vmem((12, 4, 4, 48, 384), bf), vmem((12, 2, 4, 48, 384), bf), vmem((12, 4, 48, 384), bf), vmem((12, 3, 48, 384), bf)]
-    dma = pltpu.SemaphoreType.DMA
-    scratch += [dma((12, 8)), dma((12, 8)), dma((19,)), dma((2,)), dma((2, 7)), dma((6,))]
+    sds, vmem, dma = jax.ShapeDtypeStruct, pltpu.VMEM, pltpu.SemaphoreType.DMA
+    pairs = targets.shape[1]
+    outs = [sds((8, 128), f32), sds((2, Q, 768), bf), sds((2, S, 768), bf), sds((16, 768), f32)]
+    outs += [sds((48, 768), f32)] * 4 + [sds((48, 3072), f32), sds((192, 768), f32), sds((12, S, S), bf)]
+    wide_rows, rows, turned, column = vmem((T, 768), f32), vmem((T, 768), bf), vmem((768, T), bf), vmem((T, 1), f32)
+    scratch = [vmem((4, 4, 4, 48, 768), bf), vmem((4, 4, 48, 3072), bf), vmem((4, 4, 192, 768), bf)] + [rows] * 4
+    scratch += [vmem((T, 3072), bf), vmem((3072, T), bf), vmem((T, 3072), bf)] + [turned] * 4 + [wide_rows, column] * 2
+    scratch += [vmem((2, 2, S, S), bf), vmem((12, Q, Q), bf), vmem((2, S, S), bf), vmem((16, 3072), f32), vmem((2, 768), f32), vmem((2, 768), f32)]
+    scratch += [vmem((pairs, 1, 1536), f32), vmem((16, 128), f32), vmem((4, 4, 16, 128), bf), vmem((2, 8, 128), f32)]
+    scratch += [vmem((16, 768), f32), vmem((6, 16, 384), f32), vmem((3, 16, 384), f32)]
+    scratch += [vmem((2, 4, 4, 48, 768), bf), vmem((4, 4, 4, 48, 384), bf), vmem((12, 4, 4, 48, 384), bf), vmem((12, 2, 4, 48, 384), bf)]
+    scratch += [vmem((12, 4, 48, 384), bf), vmem((12, 3, 48, 384), bf), dma((12, 8)), dma((12, 8))]
+    scratch += [dma((12, 16)), dma((12, 16)), dma((9,)), dma((2, 7)), dma((2,)), dma((6,)), dma((2, 7)), dma((6,))]
     return pl.pallas_call(
-        functools.partial(backward_kernel, inner),
+        functools.partial(layer_kernel, inner, seq),
         out_shape=outs,
-        in_specs=[VM] * 3 + [ANY] * 17,
-        out_specs=[ANY] * 2 + [VM] * 7,
+        in_specs=[pl.BlockSpec(memory_space=pltpu.SMEM)] + [VM] * 10 + [ANY] * 8,
+        out_specs=[VM, ANY, ANY] + [VM] * 7 + [ANY],
         scratch_shapes=scratch,
         compiler_params=pltpu.CompilerParams(collective_id=cid, has_side_effects=True, vmem_limit_bytes=63 << 20),
-        name="layer_backward",
-    )(lens, d_pool, vec, wa, wi, wo, *saved)
+        name="layer",
+    )(lengths, targets, *vectors, *weights, query_tokens, passage_tokens)
 
 
 def outputs_kernel(inner, loss_in, dxq, dxp, d_vec, *refs):
@@ -942,10 +889,8 @@
     weights = [fetch(w) for w in (query_weight, key_weight, value_weight, output_weight, inner_weight, outer_weight)]
     vectors = (query_bias, value_bias, output_bias, outer_bias, first_gain, first_shift, second_gain, second_shift, inner_bias)
     vectors = [fetch(w)[None] for w in vectors[:8]] + [fetch(inner_bias)]
-    d_pool, loss, lens, vec, wa, wi, wo, *saved = forward_call(
+    loss, dxq, dxp, d_vec, *grads, _ = layer_call(
         inner, float(seq), lengths, positives[None], vectors, weights, query_tokens, passage_tokens)
-    wa, wi, wo = wa.reshape(4, 768, 768), wi.reshape(768, 3072), wo.reshape(3072, 768)
-    dxq, dxp, d_vec, *grads = backward_call(inner, lens, d_pool, vec, wa, wi, wo, saved)
     loss, dxq, dxp, *grads = outputs_call(inner, loss, dxq, dxp, d_vec, grads)
     grads = [g.reshape(-1) if g.shape[0] == 1 else g for g in grads]
 

time: 187 us -> 177 us (0.947)
  Pallas kernels: 186 us -> 176 us
    pallas_call x2 -> x1, Pallas kernels: 180 us -> 171 us  [layer_call(): pl.pallas_call(functools.partial(layer_kernel, inner, seq), out_shape=out...]
where the time goes in v5:
time: 177 us
  Pallas kernels  176 us (99%)
    pallas_call x1, Pallas kernels, layer_call(): pl.pallas_call(functools.partial(layer_kernel, inner, seq), out_shape=out...  171 us
    pallas_call x1, Pallas kernels, outputs_call(): pl.pallas_call(functools.partial(outputs_kernel, inner), out_shape=outs,...  5.6 us

profile of v5, /device:TPU:0, one launch (start us, length us, event | category | flops | bytes accessed | tf_op | source)
XLA Modules:
  0.0 177.0 jit_solution(17929418512844141380)
XLA Ops:
  0.7 170.6 %layer.1 = (f32[8,128]{1,0:T(8,128)}, bf16[2,64,768]{2,1,0:T(8,128)(2,1)}, bf16[2,512,768]{2,1,0:T(8,128)(2,1)}, f32[16,768]{1,0:T(8,128)}, f32[48,768]{1,0:T(8,...) custom-call(s32[1,2]{1,0:T(1,128)} %lengths.1, ...), custom_call_target="tpu_custom_call" | custom-call | tf_op jit(solution)/shard_map/layer/pallas_call | solution.py:816
  171.2 5.6 %write_outputs.1 = (f32[1,1]{1,0:T(1,128)}, f32[2,64,768]{2,1,0:T(8,128)}, f32[2,512,768]{2,1,0:T(8,128)}, f32[48,768]{1,0:T(8,128)}, f32[48,768]{1,0:T(8,128)},...) custom-call(f32[8,128]{1,0:T(8,128)} %get-tuple-element.46.loss_in, ...), custom_call_target="tpu_custom_call" | custom-call | tf_op jit(solution)/shard_map/write_outputs/pallas_call | solution.py:863

commit v6 on v5

--- a/solution.py
+++ b/solution.py
@@ -48,11 +48,15 @@
     def sib(self):
         return {"dp": self.me * self.inner + self.low, "tower": 1 - self.c}
 
-    def barrier(self):
-        sem = pltpu.get_barrier_semaphore()
+    def across(self, k):
+        return {"dp": (self.ring(k) * 4 + self.quad) * self.inner + self.low, "tower": 1 - self.c}
+
+    def greet(self):
         for target in (self.up(1), self.up(2), self.up(3), self.n1(), self.n2(), self.sib()):
-            pl.semaphore_signal(sem, inc=1, device_id=target, device_id_type=MESH)
-        pl.semaphore_wait(sem, 6)
+            pl.semaphore_signal(pltpu.get_barrier_semaphore(), inc=1, device_id=target, device_id_type=MESH)
+
+    def met(self):
+        pl.semaphore_wait(pltpu.get_barrier_semaphore(), 6)
 
 
 def remote(src, dst, send_sem, recv_sem, target):
@@ -94,31 +98,32 @@
 
 
 class Gather:
+    last = 10
+
     def __init__(self, p, shards, wa, wi, wo, ssem, rsem, lsem):
         self.p, self.shards, self.wa, self.wi, self.wo = p, shards, wa, wi, wo
         self.ssem, self.rsem, self.lsem = ssem, rsem, lsem
 
     def cols(self, t, which):
-        start = which * 384 if t < 4 or t > 7 else (t - 4) * 768 + which * 384
-        return pl.ds(pl.multiple_of(start, 128), 384)
+        if t < 8:
+            return pl.ds(pl.multiple_of(which * 384 if t < 4 else (t - 4) * 768 + which * 384, 128), 384)
+        return pl.ds(pl.multiple_of(which * 384 + (t - 8) * 128, 128), 128)
 
     def shard(self, t):
-        ref = self.shards[t] if t < 4 else self.shards[4 if t < 8 else 5]
+        ref = self.shards[(1, 0, 2, 3)[t]] if t < 4 else self.shards[4 if t < 8 else 5]
         return ref.at[:, self.cols(t, self.p.c)]
 
+    def whole(self, t):
+        return self.wa.at[(1, 0, 2, 3)[t]] if t < 4 else self.wi if t < 8 else self.wo
+
     def one(self, t, z, q):
-        cols = self.cols(t, self.p.c)
-        if t < 4:
-            return self.wa.at[t, z, q, :, cols]
-        return (self.wi if t < 8 else self.wo).at[z, q, :, cols]
+        return self.whole(t).at[z, q, :, self.cols(t, self.p.c)]
 
     def four(self, t, q, which):
-        cols = self.cols(t, which)
-        if t < 4:
-            return self.wa.at[t, :, q, :, cols]
-        if t < 8:
-            return self.wi.at[:, q, :, cols]
-        return self.wo.at[self.p.ring(12 - t), q, :, cols]
+        return self.whole(t).at[:, q, :, self.cols(t, which)]
+
+    def plane(self, t, z, which):
+        return self.whole(t).at[z, :, :, self.cols(t, which)]
 
     def copy(self, src, dst, t, k, target):
         return remote(src, dst, self.ssem.at[t, k], self.rsem.at[t, k], target)
@@ -126,89 +131,93 @@
     def recv(self, t, k, ref):
         self.copy(ref, ref, t, k, self.p.sib()).wait_recv()
 
-    def push(self, t, q, k, target):
-        view = self.four(t, q, self.p.c)
+    def push(self, view, t, k, target):
         self.copy(view, view, t, k, target).start()
-
-    def steps(self, t):
-        return range(1, 4) if t < 8 else range(t - 8, t - 7) if t > 8 else ()
 
     def local(self, t):
         return pltpu.make_async_copy(self.shard(t), self.one(t, self.p.z, self.p.quad), self.lsem.at[t])
 
-    def push_one(self, t, z, q, k, target):
-        view = self.one(t, z, q)
-        self.copy(view, view, t, k, target).start()
-
-    def direct(self, t):
-        return t not in TURNED
-
     def stage_own(self, t):
         p = self.p
-        if t <= 8:
-            self.local(t).start()
-        for k in self.steps(t):
-            self.copy(self.shard(t), self.one(t, p.z, p.quad), t, k, p.up(k)).start()
-        if t <= 8:
-            self.copy(self.shard(t), self.one(t, p.z, p.quad), t, 4, p.n1()).start()
-            self.copy(self.shard(t), self.one(t, p.z, p.quad), t, 5, p.n2()).start()
+        self.local(t).start()
+        mine = self.one(t, p.z, p.quad)
+        for k in range(1, 4) if t < self.last else ():
+            self.copy(self.shard(t), mine, t, k, p.up(k)).start()
+        self.copy(self.shard(t), mine, t, 4, p.n1()).start()
+        self.copy(self.shard(t), mine, t, 5, p.n2()).start()
 
     def stage_z(self, t):
         p = self.p
-        if not self.direct(t):
-            self.recv(t, 4, self.one(t, p.z, p.q1))
-            for k in range(1, 4):
-                self.push_one(t, p.z, p.q1, 11 + k, p.up(k))
-            self.push_one(t, p.z, p.q1, 6, p.n2())
-        for k in self.steps(t):
-            z = p.ring(4 - k)
-            self.recv(t, k, self.one(t, z, p.quad))
-            if self.direct(t):
-                self.push_one(t, z, p.quad, 4, p.n1())
-            self.push_one(t, z, p.quad, 5, p.n2())
-        if t <= 8:
-            self.local(t).wait()
-        self.push(t, p.quad, 8, p.sib())
+        for k in range(1, 4):
+            view = self.one(t, p.ring(4 - k), p.quad)
+            self.recv(t, k, view)
+            self.push(view, t, 4, p.n1())
+            self.push(view, t, 5, p.n2())
+        self.local(t).wait()
+        self.push(self.four(t, p.quad, p.c), t, 8, p.sib())
 
     def stage_one(self, t):
         p = self.p
-        if self.direct(t):
-            self.recv(t, 4, self.four(t, p.q1, p.c))
-            self.push(t, p.q1, 6, p.n2())
-        else:
-            for k in range(1, 4):
-                z = p.ring(4 - k)
-                self.recv(t, 11 + k, self.one(t, z, p.q1))
-                self.push_one(t, z, p.q1, 6, p.n2())
-        self.push(t, p.q1, 9, p.sib())
+        view = self.four(t, p.q1, p.c)
+        self.recv(t, 4, view)
+        self.push(view, t, 6, p.n2())
+        self.push(view, t, 9, p.sib())
 
     def stage_two(self, t):
         p = self.p
         for k, q in ((5, p.q2), (6, p.q12)):
-            self.recv(t, k, self.four(t, q, p.c))
-            self.push(t, q, k + 5, p.sib())
+            view = self.four(t, q, p.c)
+            self.recv(t, k, view)
+            self.push(view, t, k + 5, p.sib())
 
     def stage_sib(self, t):
         p = self.p
         for k, q in ((8, p.quad), (9, p.q2), (10, p.q1), (11, p.q12)):
             self.recv(t, k, self.four(t, q, 1 - p.c))
 
+    def last_one(self):
+        p, t = self.p, self.last
+        view = self.one(t, p.z, p.q1)
+        self.recv(t, 4, view)
+        self.push(view, t, 6, p.n2())
+
+    def last_two(self):
+        p, t = self.p, self.last
+        self.recv(t, 5, self.one(t, p.z, p.q2))
+        self.recv(t, 6, self.one(t, p.z, p.q12))
+        self.local(t).wait()
+        view = self.plane(t, p.z, p.c)
+        for k in range(1, 4):
+            self.push(view, t, k, p.up(k))
+        self.push(view, t, 8, p.sib())
+
+    def last_z(self):
+        p, t = self.p, self.last
+        for k in range(1, 4):
+            view = self.plane(t, p.ring(4 - k), p.c)
+            self.recv(t, k, view)
+            self.push(view, t, 8 + k, p.sib())
+
+    def last_sib(self):
+        p, t = self.p, self.last
+        for k in range(4):
+            self.recv(t, 8 + k, self.plane(t, p.ring(4 - k), 1 - p.c))
+
     def tick(self, i):
         for lag, stage in ((0, self.stage_z), (-AHEAD, self.stage_own), (LAGS[0], self.stage_one), (LAGS[1], self.stage_two), (LAGS[2], self.stage_sib)):
-            if 0 <= i - lag < 12:
+            if 0 <= i - lag < self.last:
                 stage(i - lag)
+        for at, stage in zip(LATE, (lambda: self.stage_own(self.last), self.last_one, self.last_two, self.last_z, self.last_sib)):
+            if i == at:
+                stage()
 
     def finish(self):
         p = self.p
-        for t in range(12):
-            single, view = self.one(t, p.z, p.quad), self.four(t, p.quad, p.c)
-            for k in self.steps(t):
-                self.copy(single, single, t, k, p.sib()).wait_send()
-            for k in (4, 5, 6, 8, 9, 10, 11):
-                shape = single if k == 4 and not self.direct(t) else view
-                self.copy(shape, shape, t, k, p.sib()).wait_send()
-            for k in () if self.direct(t) else (12, 13, 14):
-                self.copy(single, single, t, k, p.sib()).wait_send()
+        for t in range(self.last + 1):
+            single, four, plane = self.one(t, p.z, p.quad), self.four(t, p.quad, p.c), self.plane(t, p.z, p.c)
+            for k in (1, 2, 3, 4, 5, 6, 8, 9, 10, 11):
+                view = (single if k < 4 else four) if t < self.last else (single if 4 <= k < 8 else plane)
+                self.copy(view, view, t, k, p.sib()).wait_send()
 
 
 def expand_vectors(shards, vec):
@@ -224,9 +233,12 @@
         vec[8:9, n * 768 : (n + 1) * 768] = jnp.sum(mine, axis=0, keepdims=True)
 
 
-AHEAD = 2
+AHEAD = 4
 LAGS = (1, 3, 4)
-TURNED = ()
+LATE = (0, 1, 5, 9, 13)
+
+
+ALONG_Z = (0,)
 
 
 class Scatter:
@@ -262,13 +274,32 @@
     def stage0(self, e):
         p, acc = self.p, self.acc
         self.recv(e, 0, self.r0.at[e % 4])
+        if e in ALONG_Z:
+            for k in (1, 2, 3, 0):
+                z = p.ring(k)
+                acc[e, z] = self.stage[e % 2, z, :, :, self.own] + self.r0[e % 4, z]
+                if k:
+                    self.copy(acc.at[e, z], self.plane(e, k), e, k, p.up(k)).start()
+            return
         for j, q in enumerate((p.q2, p.q12, p.q1, p.quad)):
             acc[e, :, q] = self.stage[e % 2, :, q, :, self.own] + self.r0[e % 4, :, q]
             if j < 2:
                 self.copy(acc.at[e, :, q], self.r1.at[e, j], e, 1 + j, p.n2()).start()
 
+    def plane(self, e, k):
+        return self.r2.at[e] if k == 3 else self.r1.at[e, k - 1]
+
     def stage1(self, e):
         p, acc = self.p, self.acc
+        if e in ALONG_Z:
+            total = wide(acc[e, p.z])
+            for k in range(1, 4):
+                self.recv(e, k, self.plane(e, k))
+                total = total + wide(self.plane(e, k)[...])
+            acc[e, p.z] = low(total)
+            for j, q in enumerate((p.q2, p.q12)):
+                self.copy(acc.at[e, p.z, q], self.r3.at[e, j], e, 4 + j, p.n2()).start()
+            return
         self.recv(e, 2, self.r1.at[e, 1])
         acc[e, :, p.q1] += self.r1[e, 1]
         self.copy(acc.at[e, :, p.q1], self.r2.at[e], e, 3, p.n1()).start()
@@ -277,6 +308,12 @@
 
     def stage2(self, e):
         p, acc = self.p, self.acc
+        if e in ALONG_Z:
+            self.recv(e, 5, self.r3.at[e, 1])
+            acc[e, p.z, p.q1] += self.r3[e, 1]
+            self.copy(acc.at[e, p.z, p.q1], self.r3.at[e, 2], e, 6, p.n1()).start()
+            self.recv(e, 4, self.r3.at[e, 0])
+            return
         self.recv(e, 3, self.r2.at[e])
         acc[e, :, p.quad] += self.r2[e]
         for k in range(1, 4):
@@ -284,10 +321,14 @@
 
     def stage3(self, e):
         p = self.p
-        total = wide(self.acc[e, p.z, p.quad])
-        for k in range(1, 4):
-            self.recv(e, 3 + k, self.r3.at[e, k - 1])
-            total = total + wide(self.r3[e, k - 1])
+        if e in ALONG_Z:
+            self.recv(e, 6, self.r3.at[e, 2])
+            total = wide(self.acc[e, p.z, p.quad]) + wide(self.r3[e, 0]) + wide(self.r3[e, 2])
+        else:
+            total = wide(self.acc[e, p.z, p.quad])
+            for k in range(1, 4):
+                self.recv(e, 3 + k, self.r3.at[e, k - 1])
+                total = total + wide(self.r3[e, k - 1])
         view = self.result(e, p.c)
         view[...] = total
         self.copy(view, view, e, 7, p.sib()).start()
@@ -308,7 +349,7 @@
 
 
 def forward_part(p, seq, lengths, targets, vector_shards, weights, query_tokens, passage_tokens, d_pool, loss, prob_out, vec, prob, prob_q,
-                 wa, wi, wo, x, q, k, v, act, act_t, slope, x_t, q_t, ctx_t, norm_t, y1, r1, y2, r2, pooled, rows, packed, vectors, len_buf,
+                 wa, wi, wo, x, q, k, v, act, act_t, slope, x_t, q_t, ctx_t, norm_t, y1, r1, y2, r2, y_sum, rows, packed, vectors, len_buf,
                  ssem, rsem, lsem, vsem, psem, xsem):
     normed = q
     pairs = targets.shape[1]
@@ -337,8 +378,6 @@
     pl.semaphore_wait(barrier, pairs - 1)
 
     gather = Gather(p, weights, wa, wi, wo, ssem, rsem, lsem)
-    for t in range(AHEAD):
-        gather.stage_own(t)
     len_copy = remote(len_buf.at[p.c], len_buf.at[p.c], xsem.at[2], xsem.at[3], p.sib())
     len_copy.start()
 
@@ -348,6 +387,8 @@
 
     for i in range(1, 4):
         vector(i, None, p.up(i)).start()
+    for t in range(AHEAD):
+        gather.stage_own(t)
     gather.tick(0)
     for i in range(1, 4):
         view = vectors.at[p.ring(4 - i), p.quad]
@@ -355,16 +396,14 @@
     vector(4, p.quad, p.n1()).start()
     vector(5, p.quad, p.n2()).start()
     gather.tick(1)
-    vector(4, p.q1, p.sib()).wait_recv()
-    vector(6, p.q1, p.n2()).start()
     for copy in x_loads:
         copy.wait()
     x_t[...] = x[...].T
-    for i in range(2, LAGS[2]):
+    gather.tick(2)
+    vector(4, p.q1, p.sib()).wait_recv()
+    vector(6, p.q1, p.n2()).start()
+    for i in range(3, LAGS[2] + 1):
         gather.tick(i)
-    vector(5, p.q2, p.sib()).wait_recv()
-    vector(6, p.q12, p.sib()).wait_recv()
-    expand_vectors(vectors[...], vec)
     remote(len_buf.at[1 - p.c], len_buf.at[1 - p.c], xsem.at[2], xsem.at[3], p.sib()).wait_recv()
     len_q, len_p = [jnp.sum(jnp.where(lane[:1] == p.c, len_buf[i, 0:1], 0.0), axis=1, keepdims=True) for i in range(2)]
 
@@ -412,10 +451,12 @@
                     act[start + r : start + r + rb, cols] = low(total)
             store_prob(j).start()
 
-    gather.tick(LAGS[2] + 0)
+    project(1, k, None)
+    gather.tick(LAGS[2] + 1)
+    vector(5, p.q2, p.sib()).wait_recv()
+    vector(6, p.q12, p.sib()).wait_recv()
+    expand_vectors(vectors[...], vec)
     project(0, q, 0)
-    gather.tick(LAGS[2] + 1)
-    project(1, k, None)
     q_t[...] = q[...].T
     gather.tick(LAGS[2] + 2)
     project(2, v, 1)
@@ -458,7 +499,7 @@
     gather.tick(LAGS[2] + 7)
     hidden(6, 12)
 
-    pooled[...] = jnp.zeros_like(pooled)
+    y_sum[...] = jnp.zeros_like(y_sum)
 
     def turn_act():
         for b in range(4):
@@ -469,36 +510,32 @@
                     act_t[row : row + 48] = turned[s * 192 + n * 48 : s * 192 + n * 48 + 48]
 
     def outer(i):
-        plane = p.ring(4 - i)
-
-        @pl.loop(0, 3)
-        def _(n):
-            span = block(n, 192)
-            add = dot(act[span, pl.ds(pl.multiple_of(plane * 768, 128), 768)], wo[plane].reshape(768, 768))
-            if i == 0:
-                add = add + (y1[span] * gain(4) + gain(5) + gain(3))
-            else:
-                add = add + y2[span]
-            if i < 3:
-                y2[span] = add
-                return
-            center = add - jnp.mean(add, axis=1, keepdims=True)
-            scale = lax.rsqrt(jnp.mean(center * center, axis=1, keepdims=True) + 1e-12)
-            y = center * scale
-            y2[span] = y
-            r2[span] = scale
-            out = y * gain(6) + gain(7)
-            at = wide(lax.broadcasted_iota(jnp.int32, (192, 1), 0) + n * 192)
-            for row, keep in ((0, (at >= S) & (at - S < len_q)), (1, (at < S) & (at < len_p))):
-                pooled[row : row + 1] += jnp.sum(jnp.where(keep, out, 0.0), axis=0, keepdims=True)
-
-    for i in range(4):
+        cols = [slice(which * 384 + i * 128, which * 384 + i * 128 + 128) for which in range(2)]
+        right = jnp.concatenate([wo[:, :, :, c].reshape(3072, 128) for c in cols], axis=1)
+        add = dot(act[...], right)
+        for which, c in enumerate(cols):
+            y2[:, c] = add[:, which * 128 : which * 128 + 128] + (y1[:, c] * vec[4:5, c] + vec[5:6, c] + vec[3:4, c])
+
+    for i in range(3):
         gather.tick(LAGS[2] + 8 + i)
         if i == 0:
             turn_act()
         outer(i)
 
-    mine = jnp.concatenate([pooled[0:1] / len_q, pooled[1:2] / len_p])
+    @pl.loop(0, 3)
+    def _(n):
+        span = block(n, 192)
+        second = y2[span]
+        center = second - jnp.mean(second, axis=1, keepdims=True)
+        scale = lax.rsqrt(jnp.mean(center * center, axis=1, keepdims=True) + 1e-12)
+        y = center * scale
+        y2[span] = y
+        r2[span] = scale
+        at = wide(lax.broadcasted_iota(jnp.int32, (192, 1), 0) + n * 192)
+        for row, keep in ((0, (at >= S) & (at - S < len_q)), (1, (at < S) & (at < len_p))):
+            y_sum[row : row + 1] += jnp.sum(jnp.where(keep, y, 0.0), axis=0, keepdims=True)
+
+    mine = jnp.concatenate([y_sum[0:1] / len_q, y_sum[1:2] / len_p]) * gain(6) + gain(7)
     root = jnp.sqrt(jnp.sum(mine * mine, axis=1, keepdims=True) + 1e-6)
     unit = mine / root
     rows[me, :, :768] = unit[0:1]
@@ -542,7 +579,7 @@
     return len_p, len_q
 
 
-def backward_part(p, len_p, len_q, d_pool, vec, prob_hbm, prob, prob_q, dxq_out, dxp_out, dvec_out, grads,
+def backward_part(p, len_p, len_q, d_pool, y_sum, vec, prob_hbm, prob, prob_q, dxq_out, dxp_out, dvec_out, grads,
                   wa, wi, wo, d_low, k, v, d_inner, act_t, slope, x_t, q_t, ctx_t, norm_t, y1, r1, d_second, r2, ds_buf,
                   d_vec, v_in, v_out, chunks, psem, vsem, xsem):
     g_query, g_key, g_value, g_output, g_inner, g_outer = grads
@@ -574,8 +611,6 @@
     pool_p = d_pool[1:2] / len_p
 
     def norm_back(d, row, yy, scale, rows):
-        tally(row, d * yy)
-        tally(row + 1, d)
         g = d * gain(row)
         d = (g - jnp.mean(g, axis=1, keepdims=True) - yy * jnp.mean(g * yy, axis=1, keepdims=True)) * scale
         d_second[rows] = d
@@ -588,12 +623,13 @@
         rows = block(n, 192)
         at = wide(lax.broadcasted_iota(jnp.int32, (192, 1), 0) + n * 192)
         d_rows = jnp.where(at < S, jnp.where(at < len_p, pool_p, 0.0), jnp.where(at - S < len_q, pool_q, 0.0))
-        d = norm_back(d_rows, 6, d_second[rows], r2[rows], rows)
-        tally(3, wide(low(d)))
+        norm_back(d_rows, 6, d_second[rows], r2[rows], rows)
 
 
     def emit_outer(n):
-        sc.emit(n, lambda: act_t[n * 768 : (n + 1) * 768], lambda cols: d_low[:, cols])
+        def bias(cols, values):
+            d_vec[3:4, cols] = jnp.sum(wide(values), axis=0, keepdims=True)
+        sc.emit(n, lambda: act_t[n * 768 : (n + 1) * 768], lambda cols: d_low[:, cols], bias if n == 3 else None)
 
     def emit_inner(n):
         def bias(cols, values):
@@ -601,6 +637,8 @@
         sc.emit(4 + n, lambda: norm_t[...], lambda cols: d_inner[:, pl.ds(pl.multiple_of(n * 768 + cols.start, 256), 256)], bias)
 
     emit_outer(0)
+    d_vec[6:7] = pool_q * y_sum[0:1] + pool_p * y_sum[1:2]
+    d_vec[7:8] = d_pool[0:1] + d_pool[1:2]
     emit_outer(1)
     sc.stage0(0)
     emit_outer(2)
@@ -616,13 +654,11 @@
 
     inner_back(0, 2)
     sc.stage0(3)
-    sc.stage1(0)
     inner_back(2, 4)
     emit_inner(0)
     sc.stage1(1)
     emit_inner(1)
     sc.stage0(4)
-    sc.stage2(0)
     emit_inner(2)
     sc.stage0(5)
     emit_inner(3)
@@ -634,15 +670,19 @@
         @pl.loop(low_n, high_n)
         def _(n):
             rows = block(n, 192)
-            d = norm_back(d_second[rows] + dot_nt(d_inner[rows], wi[...].reshape(768, 3072)), 4, y1[rows], r1[rows], rows)
+            y = y1[rows]
+            d = d_second[rows] + dot_nt(d_inner[rows], wi[...].reshape(768, 3072))
+            tally(4, d * y)
+            tally(5, d)
+            d = norm_back(d, 4, y, r1[rows], rows)
             tally(2, wide(low(d)))
 
     first_back(0, 1)
     sc.stage0(7)
     first_back(1, 3)
     sc.stage1(3)
+    sc.stage1(0)
     sc.stage2(2)
-    sc.stage3(0)
     sc.emit(8, lambda: ctx_t[...], lambda cols: d_low[:, cols])
 
     def part(i):
@@ -699,6 +739,7 @@
     attention(2, 6)
     sc.stage1(5)
     sc.stage2(4)
+    sc.stage2(0)
     sc.stage3(2)
     d_inner[:, part(1)] = act_t[part(0)].T
     d_inner[:, part(2)] = act_t[part(1)].T
@@ -727,6 +768,7 @@
     sc.stage1(6)
     sc.stage2(5)
     sc.stage3(3)
+    sc.stage3(0)
     sc.stage0(11)
 
     @pl.loop(0, 3)
@@ -784,16 +826,16 @@
     vector_shards, weights, (query_tokens, passage_tokens) = refs[:9], refs[9:15], refs[15:17]
     loss, dxq_out, dxp_out, dvec_out = refs[17:21]
     grads, prob_hbm = refs[21:27], refs[27]
-    (wa, wi, wo, x, q, k, v, act, act_t, slope, x_t, q_t, ctx_t, norm_t, y1, r1, y2, r2, prob, prob_q, ds_buf, vec, d_pool, pooled,
+    (wa, wi, wo, x, q, k, v, act, act_t, slope, x_t, q_t, ctx_t, norm_t, y1, r1, y2, r2, prob, prob_q, ds_buf, vec, d_pool, y_sum,
      rows, packed, vectors, len_buf, d_vec, v_in, v_out) = refs[28:59]
     chunks, (g_ssem, g_rsem, g_lsem, g_vsem, psem, g_xsem, vsem, xsem) = refs[59:67], refs[67:75]
     p = Place(inner)
     len_p, len_q = forward_part(
         p, seq, lengths, targets, vector_shards, weights, query_tokens, passage_tokens, d_pool, loss, prob_hbm, vec, prob, prob_q,
-        wa, wi, wo, x, q, k, v, act, act_t, slope, x_t, q_t, ctx_t, norm_t, y1, r1, y2, r2, pooled, rows, packed, vectors, len_buf,
+        wa, wi, wo, x, q, k, v, act, act_t, slope, x_t, q_t, ctx_t, norm_t, y1, r1, y2, r2, y_sum, rows, packed, vectors, len_buf,
         g_ssem, g_rsem, g_lsem, g_vsem, psem, g_xsem)
     backward_part(
-        p, len_p, len_q, d_pool, vec, prob_hbm, prob, prob_q, dxq_out, dxp_out, dvec_out, grads,
+        p, len_p, len_q, d_pool, y_sum, vec, prob_hbm, prob, prob_q, dxq_out, dxp_out, dvec_out, grads,
         wa, wi, wo, x, k, v, act, act_t, slope, x_t, q_t, ctx_t, norm_t, y1, r1, y2, r2, ds_buf,
         d_vec, v_in, v_out, chunks, psem, vsem, xsem)
 
@@ -812,7 +854,7 @@
     scratch += [vmem((16, 768), f32), vmem((6, 16, 384), f32), vmem((3, 16, 384), f32)]
     scratch += [vmem((2, 4, 4, 48, 768), bf), vmem((4, 4, 4, 48, 384), bf), vmem((12, 4, 4, 48, 384), bf), vmem((12, 2, 4, 48, 384), bf)]
     scratch += [vmem((12, 4, 48, 384), bf), vmem((12, 3, 48, 384), bf), dma((12, 8)), dma((12, 8))]
-    scratch += [dma((12, 16)), dma((12, 16)), dma((9,)), dma((2, 7)), dma((2,)), dma((6,)), dma((2, 7)), dma((6,))]
+    scratch += [dma((11, 12)), dma((11, 12)), dma((11,)), dma((2, 7)), dma((2,)), dma((6,)), dma((2, 7)), dma((6,))]
     return pl.pallas_call(
         functools.partial(layer_kernel, inner, seq),
         out_shape=outs,

time: 177 us -> 172 us (0.972)
  Pallas kernels: 176 us -> 171 us
    pallas_call x1, Pallas kernels: 171 us -> 165 us  [layer_call(): pl.pallas_call(functools.partial(layer_kernel, inner, seq), out_shape=out...]
where the time goes in v6:
time: 172 us
  Pallas kernels  171 us (99%)
    pallas_call x1, Pallas kernels, layer_call(): pl.pallas_call(functools.partial(layer_kernel, inner, seq), out_shape=out...  165 us
    pallas_call x1, Pallas kernels, outputs_call(): pl.pallas_call(functools.partial(outputs_kernel, inner), out_shape=outs,...  5.6 us

profile of v6, /device:TPU:0, one launch (start us, length us, event | category | flops | bytes accessed | tf_op | source)
XLA Modules:
  0.0 171.6 jit_solution(7743132460228712125)
XLA Ops:
  0.7 165.1 %layer.1 = (f32[8,128]{1,0:T(8,128)}, bf16[2,64,768]{2,1,0:T(8,128)(2,1)}, bf16[2,512,768]{2,1,0:T(8,128)(2,1)}, f32[16,768]{1,0:T(8,128)}, f32[48,768]{1,0:T(8,...) custom-call(s32[1,2]{1,0:T(1,128)} %lengths.1, ...), custom_call_target="tpu_custom_call" | custom-call | tf_op jit(solution)/shard_map/layer/pallas_call | solution.py:858
  165.8 5.6 %write_outputs.1 = (f32[1,1]{1,0:T(1,128)}, f32[2,64,768]{2,1,0:T(8,128)}, f32[2,512,768]{2,1,0:T(8,128)}, f32[48,768]{1,0:T(8,128)}, f32[48,768]{1,0:T(8,128)},...) custom-call(f32[8,128]{1,0:T(8,128)} %get-tuple-element.46.loss_in, ...), custom_call_target="tpu_custom_call" | custom-call | tf_op jit(solution)/shard_map/write_outputs/pallas_call | solution.py:905

commit v7 on v6

--- a/solution.py
+++ b/solution.py
@@ -398,7 +398,6 @@
     gather.tick(1)
     for copy in x_loads:
         copy.wait()
-    x_t[...] = x[...].T
     gather.tick(2)
     vector(4, p.q1, p.sib()).wait_recv()
     vector(6, p.q1, p.n2()).start()
@@ -458,23 +457,14 @@
     expand_vectors(vectors[...], vec)
     project(0, q, 0)
     q_t[...] = q[...].T
-    gather.tick(LAGS[2] + 2)
-    project(2, v, 1)
-    attention(0, 1)
-
-    gather.tick(LAGS[2] + 3)
-    attention(1, 3)
-    gather.tick(LAGS[2] + 4)
-    attention(3, 5)
-    gather.tick(LAGS[2] + 5)
-    attention(5, 6)
-    ctx_t[...] = act[:, :768].T
-
     def gain(row):
         return vec[row : row + 1, :768]
 
-    @pl.loop(0, 3)
-    def _(n):
+    def attended():
+        ctx_t[...] = act[:, :768].T
+        pl.loop(0, 3)(first_norm)
+
+    def first_norm(n):
         span = block(n, 192)
         first = wide(x[span]) + (dot(act[span, :768], wa[3].reshape(768, 768)) + gain(2))
         center = first - jnp.mean(first, axis=1, keepdims=True)
@@ -493,21 +483,21 @@
             act[:, cols] = low(u * cdf)
             slope[:, cols] = low(cdf + u * (0.3989422804014327 * jnp.exp(-0.5 * u * u)))
 
+    gather.tick(LAGS[2] + 2)
+    project(2, v, 1)
+    attention(0, 2)
+    gather.tick(LAGS[2] + 3)
+    attention(2, 4)
+    gather.tick(LAGS[2] + 4)
+    attention(4, 6)
+    attended()
+    gather.tick(LAGS[2] + 5)
+    hidden(0, 6)
     gather.tick(LAGS[2] + 6)
-    norm_t[...] = normed[...].T
-    hidden(0, 6)
+    hidden(6, 9)
     gather.tick(LAGS[2] + 7)
-    hidden(6, 12)
-
+    hidden(9, 12)
     y_sum[...] = jnp.zeros_like(y_sum)
-
-    def turn_act():
-        for b in range(4):
-            turned = act[:, b * 768 : (b + 1) * 768].T
-            for s in range(4):
-                for n in range(4):
-                    row = n * 768 + (b * 4 + s) * 48
-                    act_t[row : row + 48] = turned[s * 192 + n * 48 : s * 192 + n * 48 + 48]
 
     def outer(i):
         cols = [slice(which * 384 + i * 128, which * 384 + i * 128 + 128) for which in range(2)]
@@ -518,8 +508,6 @@
 
     for i in range(3):
         gather.tick(LAGS[2] + 8 + i)
-        if i == 0:
-            turn_act()
         outer(i)
 
     @pl.loop(0, 3)
@@ -535,6 +523,14 @@
         for row, keep in ((0, (at >= S) & (at - S < len_q)), (1, (at < S) & (at < len_p))):
             y_sum[row : row + 1] += jnp.sum(jnp.where(keep, y, 0.0), axis=0, keepdims=True)
 
+    def turn_act():
+        for b in range(4):
+            turned = act[:, b * 768 : (b + 1) * 768].T
+            for s in range(4):
+                for n in range(4):
+                    row = n * 768 + (b * 4 + s) * 48
+                    act_t[row : row + 48] = turned[s * 192 + n * 48 : s * 192 + n * 48 + 48]
+
     mine = jnp.concatenate([y_sum[0:1] / len_q, y_sum[1:2] / len_p]) * gain(6) + gain(7)
     root = jnp.sqrt(jnp.sum(mine * mine, axis=1, keepdims=True) + 1e-6)
     unit = mine / root
@@ -544,6 +540,9 @@
     @pl.loop(1, pairs)
     def _(i):
         remote(rows.at[me], rows.at[me], xsem.at[4], xsem.at[5], device(lax.rem(me + i, pairs))).start()
+    turn_act()
+    norm_t[...] = normed[...].T
+    x_t[...] = x[...].T
     gather.finish()
     len_copy.wait_send()
     for i in range(1, 7):
@@ -868,33 +867,39 @@
 
 def outputs_kernel(inner, loss_in, dxq, dxp, d_vec, *refs):
     grads, (loss, q_out, p_out), g_outs, v_outs = refs[:6], refs[6:9], refs[9:15], refs[15:24]
-    q_low, p_low, q_wide, p_wide, isem, osem, gsem = refs[24:]
-    copies = [pltpu.make_async_copy(src, dst, gsem.at[i]) for i, (src, dst) in enumerate(zip(grads, g_outs))]
+    q_low, p_low, q_wide, p_wide, v_buf = refs[24:29]
+    g_bufs, (isem, osem, gsem, vsem) = refs[29:35], refs[35:]
     parts = [(dxp.at[i, pl.ds(r, 256)], p_low.at[i, pl.ds(r, 256)], p_wide.at[i, pl.ds(r, 256)], p_out.at[i, pl.ds(r, 256)]) for i in range(2) for r in (0, 256)]
     parts.append((dxq, q_low, q_wide, q_out))
     loads = [pltpu.make_async_copy(part[0], part[1], isem.at[i]) for i, part in enumerate(parts)]
-    for copy in loads + copies:
+    v_load = pltpu.make_async_copy(d_vec, v_buf, vsem)
+    g_loads = [pltpu.make_async_copy(src, buf, gsem.at[0, i]) for i, (src, buf) in enumerate(zip(grads, g_bufs))]
+    g_stores = [pltpu.make_async_copy(buf, dst, gsem.at[1, i]) for i, (buf, dst) in enumerate(zip(g_bufs, g_outs))]
+    for copy in loads + [v_load] + g_loads:
         copy.start()
     loss[...] = loss_in[0:1, 0:1]
+    stores = []
+    for i, (_, source, wider, out) in enumerate(parts):
+        loads[i].wait()
+        wider[...] = wide(source[...])
+        stores.append(pltpu.make_async_copy(wider, out, osem.at[i]))
+        stores[-1].start()
+    for load, store in zip(g_loads, g_stores):
+        load.wait()
+        store.start()
+    v_load.wait()
     shard = lax.axis_index("dp") // inner
     for size, first, outs in ((48, 0, v_outs[:8]), (192, 8, v_outs[8:])):
         at = lax.broadcasted_iota(jnp.int32, (768, 1), 0) - lax.rem(shard * size, 768)
         pick = jnp.where(at == lax.broadcasted_iota(jnp.int32, (1, size), 1), 1.0, 0.0)
-        rows = d_vec[0:8] if size == 48 else d_vec[8:16]
-        mine = jnp.dot(rows, pick, precision=lax.Precision.HIGHEST, preferred_element_type=jnp.float32)
+        mine = jnp.dot(v_buf[first : first + 8], pick, precision=lax.Precision.HIGHEST, preferred_element_type=jnp.float32)
         if size == 48:
             for i in range(8):
                 outs[i][...] = mine[i : i + 1]
         else:
             row = lax.broadcasted_iota(jnp.int32, (8, 1), 0)
             outs[0][...] = jnp.sum(jnp.where(row == shard // 4, mine, 0.0), axis=0, keepdims=True)
-    stores = []
-    for i, (_, source, wider, out) in enumerate(parts):
-        loads[i].wait()
-        wider[...] = wide(source[...])
-        stores.append(pltpu.make_async_copy(wider, out, osem.at[i]))
-        stores[-1].start()
-    for copy in stores + copies:
+    for copy in stores + g_stores:
         copy.wait()
 
 
@@ -902,12 +907,14 @@
     sds, f32, vmem, dma = jax.ShapeDtypeStruct, jnp.float32, pltpu.VMEM, pltpu.SemaphoreType.DMA
     outs = [sds((1, 1), f32), sds(dxq.shape, f32), sds(dxp.shape, f32)] + [sds(g.shape, f32) for g in grads]
     outs += [sds((1, 48), f32)] * 8 + [sds((1, 192), f32)]
+    scratch = [vmem(dxq.shape, dxq.dtype), vmem(dxp.shape, dxp.dtype), vmem(dxq.shape, f32), vmem(dxp.shape, f32), vmem(d_vec.shape, f32)]
+    scratch += [vmem(g.shape, f32) for g in grads] + [dma((5,)), dma((5,)), dma((2, 6)), dma]
     return pl.pallas_call(
         functools.partial(outputs_kernel, inner),
         out_shape=outs,
-        in_specs=[VM, ANY, ANY, VM] + [VM] * 6,
+        in_specs=[VM] + [ANY] * 9,
         out_specs=[VM] + [ANY] * 8 + [VM] * 9,
-        scratch_shapes=[vmem(dxq.shape, dxq.dtype), vmem(dxp.shape, dxp.dtype), vmem(dxq.shape, f32), vmem(dxp.shape, f32), dma((5,)), dma((5,)), dma((6,))],
+        scratch_shapes=scratch,
         compiler_params=pltpu.CompilerParams(vmem_limit_bytes=62 << 20),
         name="write_outputs",
     )(loss, dxq, dxp, d_vec, *grads)

time: 172 us -> 169 us (0.983)
  Pallas kernels: 171 us -> 168 us
    pallas_call x1, Pallas kernels: 165 us -> 163 us  [layer_call(): pl.pallas_call(functools.partial(layer_kernel, inner, seq), out_shape=out...]
where the time goes in v7:
time: 169 us
  Pallas kernels  168 us (99%)
    pallas_call x1, Pallas kernels, layer_call(): pl.pallas_call(functools.partial(layer_kernel, inner, seq), out_shape=out...  163 us
    pallas_call x1, Pallas kernels, outputs_call(): pl.pallas_call(functools.partial(outputs_kernel, inner), out_shape=outs,...  4.99 us

profile of v7, /device:TPU:0, one launch (start us, length us, event | category | flops | bytes accessed | tf_op | source)
XLA Modules:
  0.0 168.6 jit_solution(5866200528627095940)
XLA Ops:
  0.7 162.7 %layer.1 = (f32[8,128]{1,0:T(8,128)}, bf16[2,64,768]{2,1,0:T(8,128)(2,1)}, bf16[2,512,768]{2,1,0:T(8,128)(2,1)}, f32[16,768]{1,0:T(8,128)}, f32[48,768]{1,0:T(8,...) custom-call(s32[1,2]{1,0:T(1,128)} %lengths.1, ...), custom_call_target="tpu_custom_call" | custom-call | tf_op jit(solution)/shard_map/layer/pallas_call | solution.py:857
  163.4 5.0 %write_outputs.1 = (f32[1,1]{1,0:T(1,128)}, f32[2,64,768]{2,1,0:T(8,128)}, f32[2,512,768]{2,1,0:T(8,128)}, f32[48,768]{1,0:T(8,128)}, f32[48,768]{1,0:T(8,128)},...) custom-call(f32[8,128]{1,0:T(8,128)} %get-tuple-element.46.loss_in, ...), custom_call_target="tpu_custom_call" | custom-call | tf_op jit(solution)/shard_map/write_outputs/pallas_call | solution.py:912

commit v8 on v7

--- a/solution.py
+++ b/solution.py
@@ -537,13 +537,14 @@
     rows[me, :, :768] = unit[0:1]
     rows[me, :, 768:] = unit[1:2]
 
-    @pl.loop(1, pairs)
-    def _(i):
-        remote(rows.at[me], rows.at[me], xsem.at[4], xsem.at[5], device(lax.rem(me + i, pairs))).start()
+    for first, end in ((pairs // 4, pairs), (1, pairs // 4)):
+
+        @pl.loop(first, end)
+        def _(i):
+            remote(rows.at[me], rows.at[me], xsem.at[4], xsem.at[5], device(lax.rem(me + i, pairs))).start()
     turn_act()
     norm_t[...] = normed[...].T
     x_t[...] = x[...].T
-    gather.finish()
     len_copy.wait_send()
     for i in range(1, 7):
         vector(i, p.quad, p.sib()).wait_send()
@@ -575,10 +576,10 @@
         u = unit[row : row + 1]
         d_pool[row : row + 1] = (d_unit - u * jnp.sum(u * d_unit, axis=1, keepdims=True)) / root[row : row + 1]
     remote(rest, rest, xsem.at[4], xsem.at[5], p.sib()).wait_send()
-    return len_p, len_q
-
-
-def backward_part(p, len_p, len_q, d_pool, y_sum, vec, prob_hbm, prob, prob_q, dxq_out, dxp_out, dvec_out, grads,
+    return len_p, len_q, gather.finish
+
+
+def backward_part(p, settle, len_p, len_q, d_pool, y_sum, vec, prob_hbm, prob, prob_q, dxq_out, dxp_out, dvec_out, grads,
                   wa, wi, wo, d_low, k, v, d_inner, act_t, slope, x_t, q_t, ctx_t, norm_t, y1, r1, d_second, r2, ds_buf,
                   d_vec, v_in, v_out, chunks, psem, vsem, xsem):
     g_query, g_key, g_value, g_output, g_inner, g_outer = grads
@@ -784,6 +785,7 @@
         copy.start()
     v_out[0] = d_vec[:, sc.own] + vector_recv(0)
     vector(1, v_out.at[0], p.n2()).start()
+    settle()
     sc.stage1(7)
     sc.stage2(6)
     sc.stage3(4)
@@ -793,16 +795,16 @@
     sc.stage1(9)
     sc.stage2(8)
     sc.stage3(6)
+    sc.stage1(10)
     v_out[1] = v_out[0] + vector_recv(1)
     vector(2, v_out.at[1], p.n1()).start()
-    sc.stage1(10)
     sc.stage2(9)
     sc.stage3(7)
     sc.stage1(11)
+    sc.stage2(10)
     v_out[2] = v_out[1] + vector_recv(2)
     for i in range(1, 4):
         vector(2 + i, v_out.at[2], p.up(i)).start()
-    sc.stage2(10)
     sc.stage3(8)
     sc.stage2(11)
     dvec_out[:, sc.own] = v_out[2] + vector_recv(3) + vector_recv(4) + vector_recv(5)
@@ -829,12 +831,12 @@
      rows, packed, vectors, len_buf, d_vec, v_in, v_out) = refs[28:59]
     chunks, (g_ssem, g_rsem, g_lsem, g_vsem, psem, g_xsem, vsem, xsem) = refs[59:67], refs[67:75]
     p = Place(inner)
-    len_p, len_q = forward_part(
+    len_p, len_q, settle = forward_part(
         p, seq, lengths, targets, vector_shards, weights, query_tokens, passage_tokens, d_pool, loss, prob_hbm, vec, prob, prob_q,
         wa, wi, wo, x, q, k, v, act, act_t, slope, x_t, q_t, ctx_t, norm_t, y1, r1, y2, r2, y_sum, rows, packed, vectors, len_buf,
         g_ssem, g_rsem, g_lsem, g_vsem, psem, g_xsem)
     backward_part(
-        p, len_p, len_q, d_pool, y_sum, vec, prob_hbm, prob, prob_q, dxq_out, dxp_out, dvec_out, grads,
+        p, settle, len_p, len_q, d_pool, y_sum, vec, prob_hbm, prob, prob_q, dxq_out, dxp_out, dvec_out, grads,
         wa, wi, wo, x, k, v, act, act_t, slope, x_t, q_t, ctx_t, norm_t, y1, r1, y2, r2, ds_buf,
         d_vec, v_in, v_out, chunks, psem, vsem, xsem)
 

time: 169 us -> 169 us (level)
  no operation moved by 1% of the time
where the time goes in v8:
time: 169 us
  Pallas kernels  168 us (99%)
    pallas_call x1, Pallas kernels, layer_call(): pl.pallas_call(functools.partial(layer_kernel, inner, seq), out_shape=out...  163 us
    pallas_call x1, Pallas kernels, outputs_call(): pl.pallas_call(functools.partial(outputs_kernel, inner), out_shape=outs,...  4.99 us

profile of v8, /device:TPU:0, one launch (start us, length us, event | category | flops | bytes accessed | tf_op | source)
XLA Modules:
  0.0 168.7 jit_solution(12889872457530001373)
XLA Ops:
  0.7 162.8 %layer.1 = (f32[8,128]{1,0:T(8,128)}, bf16[2,64,768]{2,1,0:T(8,128)(2,1)}, bf16[2,512,768]{2,1,0:T(8,128)(2,1)}, f32[16,768]{1,0:T(8,128)}, f32[48,768]{1,0:T(8,...) custom-call(s32[1,2]{1,0:T(1,128)} %lengths.1, ...), custom_call_target="tpu_custom_call" | custom-call | tf_op jit(solution)/shard_map/layer/pallas_call | solution.py:859
  163.5 5.0 %write_outputs.1 = (f32[1,1]{1,0:T(1,128)}, f32[2,64,768]{2,1,0:T(8,128)}, f32[2,512,768]{2,1,0:T(8,128)}, f32[48,768]{1,0:T(8,128)}, f32[48,768]{1,0:T(8,128)},...) custom-call(f32[8,128]{1,0:T(8,128)} %get-tuple-element.46.loss_in, ...), custom_call_target="tpu_custom_call" | custom-call | tf_op jit(solution)/shard_map/write_outputs/pallas_call | solution.py:914
